TPU v7x, 32 devices: a whole 2x2x4 slice. The times are simulated.
32 devices in a mesh: img: 2 (over y), row: 4 (over x, core), col: 4 (over z).
Axes of the slice: x: 2, y: 2, z: 4, core: 2. Of those that a mesh axis runs over, the one named last changes fastest.
Arguments:
- tokens: bfloat16 [24, 32, 32, 1152], P('img', 'row', 'col'), may hold values from -6 to 6
- conditioning: bfloat16 [24, 4, 1152], P('img'), may hold values from -6 to 6
- images_in_slot: int32 [24], P('img'), may hold values from 1 to 4, as said below
- w_qkv: bfloat16 [1152, 3456], replicated, may hold values from -0.1875 to 0.1875
- b_qv: bfloat16 [2304], replicated, may hold values from -3 to 3
- w_proj: bfloat16 [1152, 1152], replicated, may hold values from -0.375 to 0.375
- b_proj: bfloat16 [1152], replicated, may hold values from -3 to 3
- w_up: bfloat16 [1152, 4608], replicated, may hold values from -0.1875 to 0.1875
- b_up: bfloat16 [4608], replicated, may hold values from -3 to 3
- w_down: bfloat16 [4608, 1152], replicated, may hold values from -0.09375 to 0.09375
- b_down: bfloat16 [1152], replicated, may hold values from -3 to 3
- w_ada: bfloat16 [1152, 6912], replicated, may hold values from -0.1875 to 0.1875
- b_ada: bfloat16 [6912], replicated, may hold values from -2 to 2
- cotangent: bfloat16 [24, 32, 32, 1152], P('img', 'row', 'col'), may hold values from -6 to 6
Outputs:
- output: bfloat16 [24, 32, 32, 1152], P('img', 'row', 'col')
- grad_tokens: float32 [24, 32, 32, 1152], P('img', 'row', 'col')
- grad_conditioning: float32 [24, 4, 1152], P('img')
- grad_w_qkv: float32 [1152, 3456], P(('row', 'col'))
- grad_b_qv: float32 [2304], P(('row', 'col'))
- grad_w_proj: float32 [1152, 1152], P(('row', 'col'))
- grad_b_proj: float32 [1152], P(('row', 'col'))
- grad_w_up: float32 [1152, 4608], P(('row', 'col'))
- grad_b_up: float32 [4608], P(('row', 'col'))
- grad_w_down: float32 [4608, 1152], P(('row', 'col'))
- grad_b_down: float32 [1152], P(('row', 'col'))
- grad_w_ada: float32 [1152, 6912], P(('row', 'col'))
- grad_b_ada: float32 [6912], P(('row', 'col'))
Inputs may be any that keep to these rules, and one draw needn't show every extreme that they name: `images_in_slot`: each value is 1 (one image fills the slot's 32 x 32 grid) or 4 (four images, one in each quadrant of 16 x 16 tokens); among the 12 slots of each index of img at least one holds 1 image.
All inputs are finite; a program needn't handle non-finite values.
Results may differ from a plain program's by a relative error of at most 0.04.
Values may be sent and summed in bfloat16 or wider, within the bound.
A program may use at most 576 MiB of HBM per device.

v0:
```python
import math

import jax
import jax.numpy as jnp
from jax import lax
from jax.sharding import PartitionSpec as P

HEADS = 16


norm_eps = 1e-06
masked_score = -1e30


def layer_norm(values):
    center = values - jnp.mean(values, axis=-1, keepdims=True)
    spread = jnp.mean(center * center, axis=-1, keepdims=True)
    return center * lax.rsqrt(spread + norm_eps)


def modulate(values, shift_term, scale_term):
    return layer_norm(values) * (1.0 + scale_term) + shift_term


def gelu_tanh(values):
    return jax.nn.gelu(values, approximate=True)


def quarter_of(tile_number, col_count, rows_tile, cols_tile, half_grid):
    tile_row = tile_number // col_count
    tile_col = tile_number % col_count
    lower_half = (tile_row * rows_tile >= half_grid).astype(jnp.int32)
    right_half = (tile_col * cols_tile >= half_grid).astype(jnp.int32)
    return lower_half * 2 + right_half


def slot_block(slot_count, tile_tokens):
    for divisor in range(1, slot_count + 1):
        if slot_count % divisor == 0 and divisor * tile_tokens >= 512:
            return divisor
    return slot_count


def over_blocks(function, block_size, arrays):
    block_count = arrays[0].shape[0] // block_size
    shaped = tuple(
        (member.reshape((block_count, block_size) + member.shape[1:]) for member in arrays)
    )

    def apply_block(grouped):
        return function(*grouped)

    outputs = lax.map(apply_block, shaped)
    return jax.tree.map(
        lambda stacked: stacked.reshape((block_count * block_size,) + stacked.shape[2:]), outputs
    )


def to_heads(values, head_count):
    return values.reshape(
        values.shape[0], values.shape[1], head_count, values.shape[2] // head_count
    )


def block_scores(queries, key_block, allowed, head_count, scale_factor):
    raw_scores = (
        jnp.einsum(
            "bqhe,bkhe->bhqk",
            to_heads(queries, head_count),
            to_heads(key_block, head_count),
            preferred_element_type=jnp.float32,
        )
        * scale_factor
    )
    return jnp.where(allowed[:, None, :, :], raw_scores, masked_score)


def attend_block(queries, key_block, value_block, allowed, head_count, scale_factor):
    scores = block_scores(queries, key_block, allowed, head_count, scale_factor)
    row_max = jnp.max(scores, axis=-1, keepdims=True)
    exponent = jnp.exp(scores - row_max)
    row_total = jnp.sum(exponent, axis=-1, keepdims=True)
    summed = jnp.einsum(
        "bhqk,bkhe->bqhe",
        exponent.astype(jnp.bfloat16),
        to_heads(value_block, head_count),
        preferred_element_type=jnp.float32,
    )
    total_rows = jnp.transpose(row_total, (0, 2, 1, 3))
    attended = summed / total_rows
    return (
        attended.reshape(queries.shape),
        total_rows[..., 0],
        jnp.transpose(row_max, (0, 2, 1, 3))[..., 0],
    )


def grad_block(
    queries,
    key_block,
    value_block,
    allowed,
    row_max,
    grad_summed,
    grad_total,
    head_count,
    scale_factor,
):
    scores = block_scores(queries, key_block, allowed, head_count, scale_factor)
    exponent = jnp.exp(scores - jnp.transpose(row_max, (0, 2, 1))[..., None])
    grad_heads = to_heads(grad_summed, head_count)
    grad_prob = jnp.einsum(
        "bqhe,bkhe->bhqk",
        grad_heads,
        to_heads(value_block, head_count),
        preferred_element_type=jnp.float32,
    )
    grad_scores = (exponent * (grad_prob + jnp.transpose(grad_total, (0, 2, 1))[..., None])).astype(
        jnp.bfloat16
    )
    results = []
    grad_query = (
        jnp.einsum(
            "bhqk,bkhe->bqhe",
            grad_scores,
            to_heads(key_block, head_count),
            preferred_element_type=jnp.float32,
        )
        * scale_factor
    )
    results.append(grad_query.reshape(queries.shape))
    grad_key = (
        jnp.einsum(
            "bhqk,bqhe->bkhe",
            grad_scores,
            to_heads(queries, head_count),
            preferred_element_type=jnp.float32,
        )
        * scale_factor
    )
    grad_value = jnp.einsum(
        "bhqk,bqhe->bkhe",
        exponent.astype(jnp.bfloat16),
        grad_heads,
        preferred_element_type=jnp.float32,
    )
    results.append(grad_key.reshape(key_block.shape))
    results.append(grad_value.reshape(value_block.shape))
    return tuple(results)


def shards(
    tokens,
    conditioning,
    images_in_slot,
    w_qkv,
    b_qv,
    w_proj,
    b_proj,
    w_up,
    b_up,
    w_down,
    b_down,
    w_ada,
    b_ada,
    cotangent,
):
    slot_count, rows_tile, cols_tile, model_width = tokens.shape
    row_count = lax.axis_size("row")
    col_count = lax.axis_size("col")
    group_count = row_count * col_count
    rank_index = lax.axis_index("row") * col_count + lax.axis_index("col")
    half_grid = rows_tile * row_count // 2
    tile_tokens = rows_tile * cols_tile
    key_count = tile_tokens * group_count
    token_count = slot_count * tile_tokens
    head_count = HEADS
    scale_factor = 1.0 / math.sqrt(model_width // head_count)
    block_size = slot_block(slot_count, tile_tokens)
    contract_rows = (((0,), (0,)), ((), ()))
    contract_cols = (((1,), (1,)), ((), ()))
    my_quarter = quarter_of(rank_index, col_count, rows_tile, cols_tile, half_grid)
    four_way = images_in_slot == 4
    single = jnp.logical_not(four_way)
    picked = jnp.where(four_way, my_quarter, 0)
    pick_table = picked[:, None] == jnp.arange(4, dtype=jnp.int32)[None, :]
    cond_float = conditioning.astype(jnp.float32)
    silu_cond = jax.nn.silu(cond_float).astype(jnp.bfloat16)
    chosen = jnp.sum(
        jnp.where(pick_table[:, :, None], silu_cond, jnp.zeros_like(silu_cond)), axis=1
    )
    modulation = jnp.dot(chosen, w_ada, preferred_element_type=jnp.float32) + b_ada
    mod_parts = modulation.reshape(slot_count, 6, 1, 1, model_width)
    shift_one = mod_parts[:, 0]
    scale_one = mod_parts[:, 1]
    gate_one = mod_parts[:, 2]
    shift_two = mod_parts[:, 3]
    scale_two = mod_parts[:, 4]
    gate_two = mod_parts[:, 5]
    inputs = tokens.astype(jnp.float32)
    normed_one = (
        modulate(inputs, shift_one, scale_one)
        .astype(jnp.bfloat16)
        .reshape(token_count, model_width)
    )
    projected = jnp.dot(normed_one, w_qkv, preferred_element_type=jnp.float32)
    queries = (
        (projected[:, :model_width] + b_qv[:model_width])
        .astype(jnp.bfloat16)
        .reshape(slot_count, tile_tokens, model_width)
    )
    keys_local = (
        projected[:, model_width : 2 * model_width]
        .astype(jnp.bfloat16)
        .reshape(slot_count, tile_tokens, model_width)
    )
    values_local = (
        (projected[:, 2 * model_width :] + b_qv[model_width:])
        .astype(jnp.bfloat16)
        .reshape(slot_count, tile_tokens, model_width)
    )
    keys_all, values_all = (
        lax.all_gather(keys_local, ("row", "col"), axis=1, tiled=True),
        lax.all_gather(values_local, ("row", "col"), axis=1, tiled=True),
    )
    key_quarter = quarter_of(
        jnp.arange(key_count, dtype=jnp.int32) // tile_tokens,
        col_count,
        rows_tile,
        cols_tile,
        half_grid,
    )
    key_allowed = jnp.logical_or(single[:, None], key_quarter[None, :] == my_quarter)[:, None, :]

    def attend_slots(query_part, key_part, value_part, allowed_part):
        return attend_block(
            query_part, key_part, value_part, allowed_part, head_count, scale_factor
        )

    attended, row_total, row_max = over_blocks(
        attend_slots, block_size, (queries, keys_all, values_all, key_allowed)
    )
    attended_low = attended.astype(jnp.bfloat16).reshape(token_count, model_width)
    branch_one = (
        jnp.dot(attended_low, w_proj, preferred_element_type=jnp.float32) + b_proj
    ).reshape(tokens.shape)
    middle = inputs + gate_one * branch_one
    normed_two = (
        modulate(middle, shift_two, scale_two)
        .astype(jnp.bfloat16)
        .reshape(token_count, model_width)
    )
    hidden_pre = jnp.dot(normed_two, w_up, preferred_element_type=jnp.float32) + b_up
    hidden = gelu_tanh(hidden_pre).astype(jnp.bfloat16)
    branch_two = (jnp.dot(hidden, w_down, preferred_element_type=jnp.float32) + b_down).reshape(
        tokens.shape
    )
    output = (middle + gate_two * branch_two).astype(jnp.bfloat16)
    upstream = cotangent.astype(jnp.float32)
    grad_gate_two = jnp.sum(upstream * branch_two, axis=(1, 2))
    grad_branch_two = (gate_two * upstream).astype(jnp.bfloat16).reshape(token_count, model_width)
    grad_b_down = jnp.sum(grad_branch_two, axis=0, dtype=jnp.float32)
    grad_w_down = lax.dot_general(
        hidden, grad_branch_two, contract_rows, preferred_element_type=jnp.float32
    )
    grad_hidden = lax.dot_general(
        grad_branch_two, w_down, contract_cols, preferred_element_type=jnp.float32
    )
    gelu_back = jax.vjp(gelu_tanh, hidden_pre)[1]
    grad_pre = gelu_back(grad_hidden)[0].astype(jnp.bfloat16)
    grad_b_up = jnp.sum(grad_pre, axis=0, dtype=jnp.float32)
    grad_w_up = lax.dot_general(
        normed_two, grad_pre, contract_rows, preferred_element_type=jnp.float32
    )
    grad_normed_two = lax.dot_general(
        grad_pre, w_up, contract_cols, preferred_element_type=jnp.float32
    ).reshape(tokens.shape)
    norm_back_two = jax.vjp(modulate, middle, shift_two, scale_two)[1]
    grad_middle_norm, grad_shift_two, grad_scale_two = norm_back_two(grad_normed_two)
    grad_middle = upstream + grad_middle_norm
    grad_gate_one = jnp.sum(grad_middle * branch_one, axis=(1, 2))
    grad_branch_one = (
        (gate_one * grad_middle).astype(jnp.bfloat16).reshape(token_count, model_width)
    )
    grad_b_proj = jnp.sum(grad_branch_one, axis=0, dtype=jnp.float32)
    grad_w_proj = lax.dot_general(
        attended_low, grad_branch_one, contract_rows, preferred_element_type=jnp.float32
    )
    grad_attended = lax.dot_general(
        grad_branch_one, w_proj, contract_cols, preferred_element_type=jnp.float32
    )
    grad_heads = to_heads(grad_attended.reshape(slot_count, tile_tokens, model_width), head_count)
    attended_heads = to_heads(attended, head_count)
    grad_summed = (
        (grad_heads / row_total[..., None])
        .astype(jnp.bfloat16)
        .reshape(slot_count, tile_tokens, model_width)
    )
    grad_total = -jnp.sum(grad_heads * attended_heads, axis=-1) / row_total

    def grad_slots(
        query_part, key_part, value_part, allowed_part, max_part, summed_part, total_part
    ):
        return grad_block(
            query_part,
            key_part,
            value_part,
            allowed_part,
            max_part,
            summed_part,
            total_part,
            head_count,
            scale_factor,
        )

    grad_query, key_terms, value_terms = over_blocks(
        grad_slots,
        block_size,
        (queries, keys_all, values_all, key_allowed, row_max, grad_summed, grad_total),
    )
    grad_key, grad_value = (
        lax.psum_scatter(
            key_terms.astype(jnp.bfloat16), ("row", "col"), scatter_dimension=1, tiled=True
        ).astype(jnp.float32),
        lax.psum_scatter(
            value_terms.astype(jnp.bfloat16), ("row", "col"), scatter_dimension=1, tiled=True
        ).astype(jnp.float32),
    )
    grad_q = grad_query.astype(jnp.bfloat16)
    grad_k = grad_key.astype(jnp.bfloat16)
    grad_v = grad_value.astype(jnp.bfloat16)
    grad_qkv = jnp.concatenate([grad_q, grad_k, grad_v], axis=-1).reshape(
        token_count, 3 * model_width
    )
    grad_b_qv = jnp.concatenate(
        [
            jnp.sum(grad_q, axis=(0, 1), dtype=jnp.float32),
            jnp.sum(grad_v, axis=(0, 1), dtype=jnp.float32),
        ]
    )
    grad_w_qkv = lax.dot_general(
        normed_one, grad_qkv, contract_rows, preferred_element_type=jnp.float32
    )
    grad_normed_one = lax.dot_general(
        grad_qkv, w_qkv, contract_cols, preferred_element_type=jnp.float32
    ).reshape(tokens.shape)
    norm_back_one = jax.vjp(modulate, inputs, shift_one, scale_one)[1]
    grad_input_norm, grad_shift_one, grad_scale_one = norm_back_one(grad_normed_one)
    grad_tokens = grad_middle + grad_input_norm
    grad_mod = jnp.concatenate(
        [
            grad_shift_one.reshape(slot_count, model_width),
            grad_scale_one.reshape(slot_count, model_width),
            grad_gate_one,
            grad_shift_two.reshape(slot_count, model_width),
            grad_scale_two.reshape(slot_count, model_width),
            grad_gate_two,
        ],
        axis=-1,
    )
    placed = jnp.where(pick_table[:, :, None], grad_mod[:, None, :], 0.0)
    mod_total = lax.psum(placed.astype(jnp.bfloat16), ("row", "col")).astype(jnp.float32)
    ada_rows = model_width // group_count
    ada_cols = 6 * model_width // group_count
    silu_rows = lax.dynamic_slice_in_dim(silu_cond, rank_index * ada_rows, ada_rows, 2).astype(
        jnp.float32
    )
    grad_w_ada = jnp.einsum("sqd,sqe->de", silu_rows, mod_total, precision=lax.Precision.HIGHEST)
    grad_b_ada = lax.dynamic_slice_in_dim(
        jnp.sum(mod_total, axis=(0, 1)), rank_index * ada_cols, ada_cols, 0
    )
    grad_silu = jnp.einsum(
        "sqe,de->sqd", mod_total, w_ada.astype(jnp.float32), precision=lax.Precision.HIGHEST
    )
    silu_back = jax.vjp(jax.nn.silu, cond_float)[1]
    grad_conditioning = silu_back(grad_silu)[0]
    weight_parts = (
        lax.psum_scatter(
            grad_w_qkv.astype(jnp.bfloat16), ("row", "col"), scatter_dimension=0, tiled=True
        ).astype(jnp.float32),
        lax.psum_scatter(
            grad_b_qv.astype(jnp.bfloat16), ("row", "col"), scatter_dimension=0, tiled=True
        ).astype(jnp.float32),
        lax.psum_scatter(
            grad_w_proj.astype(jnp.bfloat16), ("row", "col"), scatter_dimension=0, tiled=True
        ).astype(jnp.float32),
        lax.psum_scatter(
            grad_b_proj.astype(jnp.bfloat16), ("row", "col"), scatter_dimension=0, tiled=True
        ).astype(jnp.float32),
        lax.psum_scatter(
            grad_w_up.astype(jnp.bfloat16), ("row", "col"), scatter_dimension=0, tiled=True
        ).astype(jnp.float32),
        lax.psum_scatter(
            grad_b_up.astype(jnp.bfloat16), ("row", "col"), scatter_dimension=0, tiled=True
        ).astype(jnp.float32),
        lax.psum_scatter(
            grad_w_down.astype(jnp.bfloat16), ("row", "col"), scatter_dimension=0, tiled=True
        ).astype(jnp.float32),
        lax.psum_scatter(
            grad_b_down.astype(jnp.bfloat16), ("row", "col"), scatter_dimension=0, tiled=True
        ).astype(jnp.float32),
    )
    summed_grads = (
        lax.psum(weight_parts[0].astype(jnp.bfloat16), "img").astype(jnp.float32),
        lax.psum(weight_parts[1].astype(jnp.bfloat16), "img").astype(jnp.float32),
        lax.psum(weight_parts[2].astype(jnp.bfloat16), "img").astype(jnp.float32),
        lax.psum(weight_parts[3].astype(jnp.bfloat16), "img").astype(jnp.float32),
        lax.psum(weight_parts[4].astype(jnp.bfloat16), "img").astype(jnp.float32),
        lax.psum(weight_parts[5].astype(jnp.bfloat16), "img").astype(jnp.float32),
        lax.psum(weight_parts[6].astype(jnp.bfloat16), "img").astype(jnp.float32),
        lax.psum(weight_parts[7].astype(jnp.bfloat16), "img").astype(jnp.float32),
        lax.psum(grad_w_ada.astype(jnp.bfloat16), "img").astype(jnp.float32),
        lax.psum(grad_b_ada.astype(jnp.bfloat16), "img").astype(jnp.float32),
    )
    return (
        output,
        grad_tokens,
        grad_conditioning,
        summed_grads[0],
        summed_grads[1],
        summed_grads[2],
        summed_grads[3],
        summed_grads[4],
        summed_grads[5],
        summed_grads[6],
        summed_grads[7],
        summed_grads[8],
        summed_grads[9],
    )


def solution(mesh):
    placed = (
        P("img", "row", "col", None),
        P("img", None, None),
        P("img"),
        P(),
        P(),
        P(),
        P(),
        P(),
        P(),
        P(),
        P(),
        P(),
        P(),
        P("img", "row", "col", None),
    )
    return jax.shard_map(
        shards,
        mesh=mesh,
        in_specs=placed,
        out_specs=(
            P("img", "row", "col", None),
            P("img", "row", "col", None),
            P("img", None, None),
            P(("row", "col"), None),
            P(("row", "col")),
            P(("row", "col"), None),
            P(("row", "col")),
            P(("row", "col"), None),
            P(("row", "col")),
            P(("row", "col"), None),
            P(("row", "col")),
            P(("row", "col"), None),
            P(("row", "col")),
        ),
        check_vma=False,
    )
```

profile of v0, /device:TPU:0, one launch (start us, length us, event | category | flops | bytes accessed | tf_op | source)
XLA Modules:
  0.0 1795.1 jit_solution(3875297654664587548)
XLA Ops:
  59.2 136.9 %all-gather.5.cloned.1.call-done = bf16[12,1024,1152]{2,1,0:T(8,128)(2,1)} async-done(((bf16[12,64,1152]{2,1,0:T(8,128)(2,1)}), bf16[12,1024,1152]{2,1,0:T(8,128)(2,1)}) %all-gather.5.cloned.1.call-update) | async-done | bytes 28311568 | tf_op jit(solution)/shard_map/all_gather | solution.py:223
  196.2 36.9 %copy.46 = bf16[12,1024,1152]{1,2,0:T(8,128)(2,1)} copy(bf16[12,1024,1152]{2,1,0:T(8,128)(2,1)} %all-gather.5.cloned.1.call-done) | data formatting | bytes 56623104 | tf_op jit(solution)/shard_map/all_gather | solution.py:223
  233.1 30.5 %fusion = (f32[12,16,64]{2,1,0:T(8,128)S(1)}, f32[12,16,64,1024]{3,2,1,0:T(8,128)}) fusion(pred[12,1024]{1,0:T(8,128)(4,1)S(1)} %broadcast_or_fusion, bf16[12,1024,16,72]{1,3,2,0:T(8,128)(2,1)} %bitcast.110, bf16[12,64,16,72]{3,2,1,0:T(8,128)(2,1)} %reshape.318), kind=kOutput, calls=%fused_computation.4 | convolution fusion | flops 1849675776 | bytes 80474112 | tf_op jit(solution)/shard_map/while/body/eval_jaxpr/bqhe,bkhe->bhqk/dot_general | solution.py:67
  263.6 22.0 %fusion.1 = f32[12,16,64]{2,1,0:T(8,128)S(1)} fusion(f32[12,16,64,1024]{3,2,1,0:T(8,128)} %get-tuple-element.158, f32[12,16,64]{2,1,0:T(8,128)S(1)} %get-tuple-element.157, pred[12,1024]{1,0:T(8,128)(4,1)S(1)} %broadcast_or_fusion), kind=kLoop, calls=%fused_computation.5 | loop fusion | flops 50319360 | bytes 50442240 | tf_op jit(solution)/shard_map/while/body/eval_jaxpr/reduce_sum | solution.py:82
  285.6 64.3 %all-gather.3.cloned.1.call-done = bf16[12,1024,1152]{2,1,0:T(8,128)(2,1)} async-done(((bf16[12,64,1152]{2,1,0:T(8,128)(2,1)}), bf16[12,1024,1152]{2,1,0:T(8,128)(2,1)}) %all-gather.3.cloned.1.call-update) | async-done | bytes 28311568 | tf_op jit(solution)/shard_map/all_gather | solution.py:224
  349.9 36.7 %copy.45 = bf16[12,1024,1152]{1,2,0:T(8,128)(2,1)} copy(bf16[12,1024,1152]{2,1,0:T(8,128)(2,1)} %all-gather.3.cloned.1.call-done) | data formatting | bytes 56623104 | tf_op jit(solution)/shard_map/all_gather | solution.py:224
  386.6 31.6 %fusion.76 = (bf16[12,64,16,72]{3,1,2,0:T(8,128)(2,1)}, f32[12,64,16,72]{3,1,2,0:T(8,128)}) fusion(f32[12,64,16]{1,2,0:T(8,128)S(1)} %bitcast.131, bf16[12,1024,16,72]{1,3,2,0:T(8,128)(2,1)} %bitcast.114, f32[12,16,64,1024]{3,2,1,0:T(8,128)} %get-tuple-element.158, f32[12,16,64]{2,1,0:T(8,128)S(1)} %get-tuple-element.157, ...), kind=kOutput, calls=%fused_computation.159 | convolution fusion | flops 1864040448 | bytes 84062208 | tf_op jit(solution)/shard_map/while/body/eval_jaxpr/bhqk,bkhe->bqhe/dot_general | solution.py:83
  424.1 18.2 %convert_element_type.226 = bf16[768,1152]{1,0:T(8,128)(2,1)} reshape(bf16[12,64,16,72]{3,2,1,0:T(8,128)(2,1)} %copy.48) | data formatting | bytes 3538944 | tf_op jit(solution)/shard_map/convert_element_type | solution.py:243
  462.5 24.5 %fusion.68 = (bf16[4608]{0:T(1024)(128)(2,1)}, bf16[768,4608]{1,0:T(8,128)(2,1)}) fusion(f32[768,4608]{1,0:T(8,128)} %fusion.79, f32[4608]{0:T(1024)S(1)} %convert_element_type.229, bf16[768,1152]{1,0:T(8,128)(2,1)} %bitcast.128, bf16[4608,1152]{1,0:T(8,128)(2,1)} %param.23), kind=kOutput, calls=%fused_computation.153 | convolution fusion | flops 8231579136 | bytes 33647616 | tf_op jit(solution)/shard_map/dot_general | solution.py:266
  514.3 44.4 %multiply_convert_fusion.1 = bf16[12,16,64,1024]{3,2,1,0:T(8,128)(2,1)} fusion(f32[12,16,64,1024]{3,2,1,0:T(8,128)} %get-tuple-element.158, f32[12,16,64]{2,1,0:T(8,128)S(1)} %divide_bitcast_fusion, f32[12,16,64]{2,1,0:T(8,128)S(1)} %get-tuple-element.157, pred[12,1024]{1,0:T(8,128)(4,1)S(1)} %broadcast_or_fusion, bf16[12,1024,16,72]{1,3,2,0:T(8,128)(2,1)} %bitcast.115, ...), kind=kOutput, calls=%fused_computation.1 | convolution fusion | flops 1889206272 | bytes 107507712 | tf_op jit(solution)/shard_map/while/body/eval_jaxpr/bqhe,bkhe->bhqk/dot_general | solution.py:112
  558.6 20.6 %multiply_convert_fusion = bf16[12,16,72,1024]{3,2,1,0:T(8,128)(2,1)} fusion(bf16[12,16,64,1024]{3,2,1,0:T(8,128)(2,1)} %multiply_convert_fusion.1, bf16[12,64,16,72]{3,2,1,0:T(8,128)(2,1)} %reshape.318), kind=kOutput, calls=%fused_computation | convolution fusion | flops 1840250880 | bytes 55246848 | tf_op jit(solution)/shard_map/while/body/eval_jaxpr/bhqk,bqhe->bkhe/dot_general | solution.py:133
  579.2 33.2 %copy.51 = bf16[12,1024,1152]{2,1,0:T(8,128)(2,1)} copy(bf16[12,1024,1152]{1,2,0:T(8,128)(2,1)} %bitcast.113) | data formatting | bytes 56623104 | tf_op jit(solution)/shard_map/convert_element_type | solution.py:323
  612.5 39.2 %convolution_convert_fusion.2 = bf16[12,16,72,1024]{3,2,1,0:T(8,128)(2,1)} fusion(f32[12,16,64,1024]{3,2,1,0:T(8,128)} %get-tuple-element.158, f32[12,16,64]{2,1,0:T(8,128)S(1)} %get-tuple-element.157, pred[12,1024]{1,0:T(8,128)(4,1)S(1)} %broadcast_or_fusion, f32[12,64,16,72]{3,1,2,0:T(8,128)} %get-tuple-element.162, f32[12,64,16]{1,2,0:T(8,128)S(1)} %bitcast.133), kind=kOutput, calls=%fused_computation.11 | convolution fusion | flops 1878196224 | bytes 82292736 | tf_op jit(solution)/shard_map/while/body/eval_jaxpr/bhqk,bqhe->bkhe/dot_general | solution.py:141
  651.8 33.8 %copy.52 = bf16[12,1024,1152]{2,1,0:T(8,128)(2,1)} copy(bf16[12,1024,1152]{1,2,0:T(8,128)(2,1)} %bitcast.112) | data formatting | bytes 56623104 | tf_op jit(solution)/shard_map/convert_element_type | solution.py:326
  686.3 22.0 %fusion.77 = (bf16[16,72]{1,0:T(8,128)(2,1)S(1)}, bf16[12,16,72,64]{2,3,1,0:T(8,128)(2,1)}) fusion(bf16[12,1024,16,72]{1,3,2,0:T(8,128)(2,1)} %bitcast.111, bf16[12,16,64,1024]{3,2,1,0:T(8,128)(2,1)} %multiply_convert_fusion.1), kind=kOutput, calls=%fused_computation.160 | convolution fusion | flops 1814592384 | bytes 55249152 | tf_op jit(solution)/shard_map/while/body/eval_jaxpr/bhqk,bkhe->bqhe/dot_general | solution.py:123
  720.8 18.7 %convolution_add_fusion.1 = f32[768,1152]{1,0:T(8,128)} fusion(bf16[4608,1152]{1,0:T(8,128)(2,1)} %param.23, f32[1152]{0:T(1024)S(1)} %convert_element_type.231, f32[768,4608]{1,0:T(8,128)} %fusion.79, f32[4608]{0:T(1024)S(1)} %copy-done.36), kind=kOutput, calls=%fused_computation.48 | convolution fusion | flops 8190001152 | bytes 28334592 | tf_op jit(solution)/shard_map/dot_general | solution.py:255
  739.6 142.3 %reduce-scatter.11.cloned.1.call-done = bf16[12,64,1152]{2,1,0:T(8,128)(2,1)} async-done(((bf16[12,1024,1152]{2,1,0:T(8,128)(2,1)}), bf16[12,64,1152]{2,1,0:T(8,128)(2,1)}) %reduce-scatter.11.cloned.1.call-update) | async-done | bytes 1769488 | tf_op jit(solution)/shard_map/reduce_scatter | solution.py:322
  884.8 269.5 %reduce-scatter.13.cloned.1.call-done = bf16[12,64,1152]{2,1,0:T(8,128)(2,1)} async-done(((bf16[12,1024,1152]{2,1,0:T(8,128)(2,1)}), bf16[12,64,1152]{2,1,0:T(8,128)(2,1)}) %reduce-scatter.13.cloned.1.call-update) | async-done | bytes 1769488 | tf_op jit(solution)/shard_map/reduce_scatter | solution.py:325
  1231.2 40.6 %all-reduce.12.cloned.1.call-done = bf16[12,4,6912]{2,0,1:T(8,128)(2,1)} async-done(((bf16[12,4,6912]{2,0,1:T(8,128)(2,1)}), bf16[12,4,6912]{2,0,1:T(8,128)(2,1)}) %all-reduce.12.cloned.1.call-update) | async-done | bytes 663568 | tf_op jit(solution)/shard_map/psum | solution.py:362
  1274.5 63.9 %reduce-scatter.21.cloned.1.call-done = bf16[72,1152]{1,0:T(8,128)(2,1)} async-done(((bf16[1152,1152]{1,0:T(8,128)(2,1)}), bf16[72,1152]{1,0:T(8,128)(2,1)}) %reduce-scatter.21.cloned.1.call-update) | async-done | bytes 165904
  1338.4 123.8 %reduce-scatter.17.cloned.1.call-done = bf16[288,1152]{1,0:T(8,128)(2,1)} async-done(((bf16[4608,1152]{1,0:T(8,128)(2,1)}), bf16[288,1152]{1,0:T(8,128)(2,1)}) %reduce-scatter.17.cloned.1.call-update) | async-done | bytes 663568 | tf_op jit(solution)/shard_map/reduce_scatter | solution.py:396
  1462.2 124.6 %reduce-scatter.15.cloned.1.call-done = bf16[72,4608]{1,0:T(8,128)(2,1)} async-done(((bf16[1152,4608]{1,0:T(8,128)(2,1)}), bf16[72,4608]{1,0:T(8,128)(2,1)}) %reduce-scatter.15.cloned.1.call-update) | async-done | bytes 663568 | tf_op jit(solution)/shard_map/reduce_scatter | solution.py:390
  1586.9 105.2 %reduce-scatter.19.cloned.1.call-done = bf16[72,3456]{1,0:T(8,128)(2,1)} async-done(((bf16[1152,3456]{1,0:T(8,128)(2,1)}), bf16[72,3456]{1,0:T(8,128)(2,1)}) %reduce-scatter.19.cloned.1.call-update) | async-done | bytes 497680
  1694.8 60.5 %all-reduce.6 = (bf16[2304]{0:T(1024)(128)(2,1)S(1)}, bf16[1152]{0:T(1024)(128)(2,1)S(1)}, bf16[4608]{0:T(1024)(128)(2,1)S(1)}, bf16[1152]{0:T(1024)(128)(2,1)S(1)}) all-reduce(bf16[2304]{0:T(1024)(128)(2,1)S(1)} %pad_maximum_fusion, ...), channel_id=5, replica_groups=mesh['img'=2,'row'=4,'col'=4] {'row','col'}, use_global_device_ids=true, to_apply=%region_25.26.clone | all-reduce | flops 9216 | bytes 36864
  (216 shorter events, 233.7 us)
Async XLA Ops:
  7.2 435.2 %copy-start = (bf16[1152,1152]{1,0:T(8,128)(2,1)S(1)}, bf16[1152,1152]{1,0:T(8,128)(2,1)}, u32[]{:S(2)}) copy-start(bf16[1152,1152]{1,0:T(8,128)(2,1)} %param.19) | copy-start | bytes 7962628
  7.2 189.0 %all-gather.5.cloned.1.call-start = ((), (), s32[]{:S(2)}) async-start(), calls=%async_computation.7 | async-start | bytes 30081024 | tf_op jit(solution)/shard_map/all_gather | solution.py:223
  23.2 32.2 %copy-start.27 = (f32[12,1152]{1,0:T(8,128)}, f32[12,1152]{1,0:T(8,128)S(1)}, u32[]{:S(2)}) copy-start(f32[12,1152]{1,0:T(8,128)S(1)} %get-tuple-element.169) | copy-start | bytes 165892
  41.7 308.2 %all-gather.3.cloned.1.call-start = ((), (), s32[]{:S(2)}) async-start(), calls=%async_computation.6 | async-start | bytes 30081024 | tf_op jit(solution)/shard_map/all_gather | solution.py:224
  47.2 834.6 %reduce-scatter.11.cloned.1.call-start = ((), (), s32[]{:S(2)}) async-start(), calls=%async_computation.8 | async-start | bytes 30081024 | tf_op jit(solution)/shard_map/reduce_scatter | solution.py:322
  47.6 414.9 %copy-start.35 = (f32[4608]{0:T(1024)}, f32[4608]{0:T(1024)S(1)}, u32[]{:S(2)}) copy-start(f32[4608]{0:T(1024)S(1)} %convert_element_type.229) | copy-start | bytes 55300
  612.5 541.8 %reduce-scatter.13.cloned.1.call-start = ((), (), s32[]{:S(2)}) async-start(), calls=%async_computation.9 | async-start | bytes 30081024 | tf_op jit(solution)/shard_map/reduce_scatter | solution.py:325
  685.6 586.2 %all-reduce.12.cloned.1.call-start = ((), (), s32[]{:S(2)}) async-start(), calls=%async_computation.10 | async-start | bytes 1769472 | tf_op jit(solution)/shard_map/psum | solution.py:362
  739.6 417.9 %copy-start.6 = (bf16[12,8,8,1152]{3,2,1,0:T(8,128)(2,1)S(1)}, bf16[12,8,8,1152]{3,2,1,0:T(8,128)(2,1)}, u32[]{:S(2)}) copy-start(bf16[12,8,8,1152]{3,2,1,0:T(8,128)(2,1)} %param.14) | copy-start | bytes 5308420
  739.6 417.9 %copy-start.22 = (f32[12,8,8]{2,1,0:T(8,128)S(1)}, f32[12,8,8]{2,1,0:T(8,128)}, u32[]{:S(2)}) copy-start(f32[12,8,8]{2,1,0:T(8,128)} %copy-done.21) | copy-start | bytes 9220
  739.6 417.9 %copy-start.24 = (f32[12,1152]{1,0:T(8,128)S(1)}, f32[12,1152]{1,0:T(8,128)}, u32[]{:S(2)}) copy-start(f32[12,1152]{1,0:T(8,128)} %copy-done.23) | copy-start | bytes 165892
  1157.5 14.1 copy-start.8
  1157.5 14.1 copy-start.12
  1179.5 158.9 %reduce-scatter.21.cloned.1.call-start = ((), (), s32[]{:S(2)}) async-start(), calls=%async_computation.14 | async-start | bytes 2820096
  1185.8 276.5 %reduce-scatter.17.cloned.1.call-start = ((), (), s32[]{:S(2)}) async-start(), calls=%async_computation.12 | async-start | bytes 11280384 | tf_op jit(solution)/shard_map/reduce_scatter | solution.py:396
  1203.4 383.4 %reduce-scatter.15.cloned.1.call-start = ((), (), s32[]{:S(2)}) async-start(), calls=%async_computation.11 | async-start | bytes 11280384 | tf_op jit(solution)/shard_map/reduce_scatter | solution.py:390
  1218.6 473.5 %reduce-scatter.19.cloned.1.call-start = ((), (), s32[]{:S(2)}) async-start(), calls=%async_computation.13 | async-start | bytes 8460288
  1231.1 461.0 %copy-start.47 = (u32[32]{0:T(128)S(1)}, u32[32]{0:T(128)}, u32[]{:S(2)}) copy-start(u32[32]{0:T(128)} %constant.178) | copy-start | bytes 388
  1231.1 463.7 %copy-start.37 = (bf16[1152]{0:T(1024)(128)(2,1)S(1)}, bf16[1152]{0:T(1024)(128)(2,1)}, u32[]{:S(2)}) copy-start(bf16[1152]{0:T(1024)(128)(2,1)} %get-tuple-element.135) | copy-start | bytes 6916
  1231.1 463.7 %copy-start.38 = (bf16[1152]{0:T(1024)(128)(2,1)S(1)}, bf16[1152]{0:T(1024)(128)(2,1)}, u32[]{:S(2)}) copy-start(bf16[1152]{0:T(1024)(128)(2,1)} %get-tuple-element.131) | copy-start | bytes 6916
  1231.1 463.7 %copy-start.40 = (bf16[4608]{0:T(1024)(128)(2,1)S(1)}, bf16[4608]{0:T(1024)(128)(2,1)}, u32[]{:S(2)}) copy-start(bf16[4608]{0:T(1024)(128)(2,1)} %get-tuple-element.133) | copy-start | bytes 27652
  1231.1 546.9 %all-reduce.14.cloned.1.call-start = ((), (), s32[]{:S(2)}) async-start(), calls=%async_computation.15 | async-start | bytes 5971968 | tf_op jit(solution)/shard_map/psum | solution.py:404
  1271.8 483.8 %copy-start.13 = (bf16[12,4,6912]{2,0,1:T(8,128)(2,1)S(1)}, bf16[12,4,6912]{2,0,1:T(8,128)(2,1)}, u32[]{:S(2)}) copy-start(bf16[12,4,6912]{2,0,1:T(8,128)(2,1)} %all-reduce.12.cloned.1.call-done) | copy-start | bytes 1990660
  1763.9 23.9 %copy-start.1 = (bf16[1152,1152]{1,0:T(8,128)(2,1)S(1)}, bf16[1152,1152]{1,0:T(8,128)(2,1)}, u32[]{:S(2)}) copy-start(bf16[1152,1152]{1,0:T(8,128)(2,1)} %param.19) | copy-start | bytes 7962628
  (39 other events, 216.1 us)
Sparse Core Ops, SparseCore 0:
  41.8 154.2 all-gather.4
  198.3 151.5 all-gather.2
  612.6 269.2 reduce-scatter.10
  885.9 268.3 reduce-scatter.12
  1179.6 92.0 all-reduce.11
  1275.5 62.8 reduce-scatter.20
  1343.0 119.1 reduce-scatter.16
  1466.8 119.9 reduce-scatter.14
  1591.5 100.5 reduce-scatter.18
  1695.2 82.8 all-reduce.13
where the time goes:
time: 1810 us; the launch traced here: 1800 us
  waiting for transfers between devices  1070 us (59%)
  matrix products  360 us (20%)
  local copies, waits for them, and re-layouts  203 us (11%)
  other arithmetic  74.3 us (4%)
  blocking collectives  65.7 us (4%)
    reduce_scatter x1, waiting for transfers between devices, shards(): lax.psum_scatter(value_terms.astype(jnp.bfloat16), ('row', 'col'), scatte...  270 us
    unnamed x12, waiting for transfers between devices  169 us
    reduce_scatter x1, waiting for transfers between devices, shards(): lax.psum_scatter(key_terms.astype(jnp.bfloat16), ('row', 'col'), scatter_...  142 us
    all_gather x1, waiting for transfers between devices, shards(): lax.all_gather(keys_local, ('row', 'col'), axis=1, tiled=True)  137 us
    reduce_scatter x1, waiting for transfers between devices, shards(): lax.psum_scatter(grad_w_up.astype(jnp.bfloat16), ('row', 'col'), scatter_...  125 us
    reduce_scatter x1, waiting for transfers between devices, shards(): lax.psum_scatter(grad_w_down.astype(jnp.bfloat16), ('row', 'col'), scatte...  124 us
    all_gather x1, waiting for transfers between devices, shards(): lax.all_gather(values_local, ('row', 'col'), axis=1, tiled=True)  64.3 us
    unnamed x1, blocking collectives  60.5 us
  transfers between devices with their start and end apart: 10, of which 10 were waited for; matrix products, arithmetic and copies ran while one was open for 17% of the time, Pallas kernels for 0%

commit v1 on v0

v1 whole, which is shorter than its diff:
```python
import functools
import math

import jax
import jax.numpy as jnp
from jax import lax
from jax.experimental import pallas as pl
from jax.experimental.pallas import tpu as pltpu
from jax.sharding import PartitionSpec as P

HEADS = 16
EPS = 1e-06
LOG2E = math.log2(math.e)
GELU_A = math.sqrt(2.0 / math.pi)
GELU_B = 0.044715
VMEM_LIMIT = 60 * 2**20

f32 = jnp.float32
bf16 = jnp.bfloat16
NT = (((1,), (1,)), ((), ()))
NN = (((1,), (0,)), ((), ()))
TN = (((0,), (0,)), ((), ()))

VMEM = pl.BlockSpec(memory_space=pltpu.VMEM)
SMEM = pl.BlockSpec(memory_space=pltpu.SMEM)


def dot(left, right, dims):
    return lax.dot_general(left, right, dims, preferred_element_type=f32)


def shaped(shape, dtype=bf16):
    return jax.ShapeDtypeStruct(shape, dtype)


def norm(values):
    center = values - jnp.mean(values, axis=-1, keepdims=True)
    rstd = lax.rsqrt(jnp.mean(center * center, axis=-1, keepdims=True) + EPS)
    return center * rstd, rstd


def qkv_kernel(blk, core_ref, x_ref, mod_ref, w_ref, b_ref, other_ref, mine_ref, nt_ref, n_s):
    half, step = pl.program_id(0), pl.program_id(1)
    rows = x_ref.shape[0]

    @pl.when(half == 0)
    def _():
        parts = []
        for i in range(rows // blk):
            y, _ = norm(x_ref[i * blk : (i + 1) * blk].astype(f32))
            parts.append((y * (1.0 + mod_ref[i, 1:2]) + mod_ref[i, 0:1]).astype(bf16))
        normed = jnp.concatenate(parts, axis=0)
        n_s[step] = normed
        nt_ref[...] = normed.T

    result = (dot(n_s[step], w_ref[0], NN) + b_ref[0]).astype(bf16)

    @pl.when(half == 0)
    def _():
        other_ref[...] = result

    @pl.when(half == 1)
    def _():
        mine_ref[...] = result


def qkv(core, x, mod, w_half, b_half, blk):
    tokens, width = x.shape
    wide = w_half.shape[2]
    steps = 3
    rows = tokens // steps
    last = steps - 1
    return pl.pallas_call(
        functools.partial(qkv_kernel, blk),
        grid_spec=pltpu.PrefetchScalarGridSpec(
            num_scalar_prefetch=1,
            grid=(2, steps),
            in_specs=[
                pl.BlockSpec((rows, width), lambda h, s, c: (s, 0)),
                pl.BlockSpec((rows // blk, 6, width), lambda h, s, c: (s, 0, 0)),
                pl.BlockSpec((1, width, wide), lambda h, s, c: (1 - c[0] + h * (2 * c[0] - 1), 0, 0)),
                pl.BlockSpec((1, 1, wide), lambda h, s, c: (1 - c[0] + h * (2 * c[0] - 1), 0, 0)),
            ],
            out_specs=[
                pl.BlockSpec((rows, wide), lambda h, s, c: (jnp.where(h == 0, s, last), 0)),
                pl.BlockSpec((rows, wide), lambda h, s, c: (jnp.where(h == 0, 0, s), 0)),
                pl.BlockSpec((width, rows), lambda h, s, c: (0, jnp.where(h == 0, s, last))),
            ],
            scratch_shapes=[pltpu.VMEM((steps, rows, width), bf16)],
        ),
        out_shape=(shaped((tokens, wide)), shaped((tokens, wide)), shaped((width, tokens))),
        compiler_params=pltpu.CompilerParams(vmem_limit_bytes=VMEM_LIMIT),
        cost_estimate=pl.CostEstimate(
            flops=4 * tokens * width * wide, bytes_accessed=20 * 2**20, transcendentals=tokens
        ),
        name="qkv",
    )(core, x, mod, w_half, b_half)


def head_window(head, hd):
    first = head * hd
    start = pl.multiple_of((first // 128) * 128, 128)
    lane = lax.broadcasted_iota(jnp.int32, (1, 256), 1) + start
    inside = jnp.logical_and(lane >= first, lane < first + hd)
    return pl.ds(start, 256), inside


def gather_rows(dst, col, sources, base, count):
    pad = dst.shape[1]
    for i in range(count):
        for j, src in enumerate(sources):
            row = 256 * i + 128 * j
            dst[row : row + 128] = src[base + 128 * i : base + 128 * i + 128, col : col + pad]


def attend_kernel(heads, hd, count, shared, flag_ref, mine_ref, sib_ref, *rest):
    if shared:
        far_ref, *rest = rest
    o_mine, o_sib, stat, q_s, k_s, v_s, o_s = rest
    pad = q_s.shape[1]
    scale = LOG2E / math.sqrt(hd)
    base = mine_ref.shape[0] - 128 * count if shared else 0
    pair = (mine_ref, sib_ref)
    gather_rows(q_s, 0, pair, base, count)
    gather_rows(k_s, pad, pair, base, count)
    gather_rows(v_s, 2 * pad, pair, base, count)
    if shared:
        k_s[256 * count :] = far_ref[:, 0:pad]
        v_s[256 * count :] = far_ref[:, pad : 2 * pad]
    o_s[...] = jnp.zeros_like(o_s)
    stat[...] = jnp.zeros_like(stat)
    lane = lax.broadcasted_iota(jnp.int32, (1, 128), 1)

    def run(single):
        def body(head, carry):
            win, inside = head_window(head, hd)
            for i in range(count):
                rows = slice(256 * i, 256 * i + 256)
                keys = slice(None) if single else rows
                q = jnp.where(inside, q_s[rows, win], jnp.zeros((), bf16))
                s = dot(q, k_s[keys, win], NT)
                top = jnp.max(s, axis=1, keepdims=True)
                p = jnp.exp2((s - top) * scale)
                total = jnp.sum(p, axis=1, keepdims=True)
                o = dot(p.astype(bf16), v_s[keys, win], NN) / total
                o_s[rows, win] = jnp.where(inside, o.astype(bf16), o_s[rows, win])
                stat[rows] = jnp.where(lane == head, top * scale + jnp.log2(total), stat[rows])
            return carry

        lax.fori_loop(0, heads, body, 0)

    one = flag_ref[0] == 1
    pl.when(one)(lambda: run(True))
    pl.when(jnp.logical_not(one))(lambda: run(False))
    for i in range(count):
        o_mine[128 * i : 128 * i + 128] = o_s[256 * i : 256 * i + 128]
        o_sib[128 * i : 128 * i + 128] = o_s[256 * i + 128 : 256 * i + 256]


def attend(flag, mine, sib, far, heads, hd, count):
    pad = mine.shape[1] // 3
    keys = 256 * count + (0 if far is None else far.shape[0])
    tokens = 128 * count
    inputs = [flag, mine, sib] + ([] if far is None else [far])
    return pl.pallas_call(
        functools.partial(attend_kernel, heads, hd, count, far is not None),
        out_shape=(
            shaped((tokens, pad)),
            shaped((tokens, pad)),
            shaped((2 * tokens, 128), f32),
        ),
        in_specs=[SMEM] + [VMEM] * (len(inputs) - 1),
        out_specs=(VMEM,) * 3,
        scratch_shapes=[
            pltpu.VMEM((2 * tokens, pad), bf16),
            pltpu.VMEM((keys, pad), bf16),
            pltpu.VMEM((keys, pad), bf16),
            pltpu.VMEM((2 * tokens, pad), bf16),
        ],
        compiler_params=pltpu.CompilerParams(vmem_limit_bytes=VMEM_LIMIT),
        cost_estimate=pl.CostEstimate(
            flops=1024 * heads * tokens * keys,
            bytes_accessed=8 * 2**20,
            transcendentals=heads * 2 * tokens * keys,
        ),
        name="attend_far" if far is not None else "attend_near",
    )(*inputs)


def attend_back_kernel(heads, hd, count, shared, flag_ref, mine_ref, sib_ref, *rest):
    d_mine, d_sib, o_mine, o_sib, stat, *rest = rest
    if shared:
        far_ref, g_mine, g_sib, g_far, *rest = rest
    else:
        g_mine, g_sib, *rest = rest
    q_s, k_s, v_s, do_s, kt_s, dqt_s, dk_s, dv_s, p_s, ds_s, lse_s, dd_s = rest
    pad = q_s.shape[1]
    inv = 1.0 / math.sqrt(hd)
    scale = LOG2E * inv
    base = mine_ref.shape[0] - 128 * count if shared else 0
    pair = (mine_ref, sib_ref)
    gather_rows(q_s, 0, pair, base, count)
    gather_rows(k_s, pad, pair, base, count)
    gather_rows(v_s, 2 * pad, pair, base, count)
    gather_rows(do_s, 0, (d_mine, d_sib), 0, count)
    if shared:
        k_s[256 * count :] = far_ref[:, 0:pad]
        v_s[256 * count :] = far_ref[:, pad : 2 * pad]
    kt_s[...] = k_s[...].astype(f32).T
    dqt_s[...] = jnp.zeros_like(dqt_s)
    dk_s[...] = jnp.zeros_like(dk_s)
    dv_s[...] = jnp.zeros_like(dv_s)
    row = lax.broadcasted_iota(jnp.int32, (heads, pad), 0)
    col = lax.broadcasted_iota(jnp.int32, (heads, pad), 1)
    member = jnp.where(jnp.logical_and(col >= row * hd, col < row * hd + hd), 1.0, 0.0).astype(bf16)
    for i in range(count):
        rows = slice(256 * i, 256 * i + 256)
        lse_s[i] = stat[rows].T[0:heads]
        o = jnp.concatenate(
            [o_mine[128 * i : 128 * i + 128], o_sib[128 * i : 128 * i + 128]], axis=0
        )
        both = do_s[rows].astype(f32) * o.astype(f32)
        high = both.astype(bf16)
        low = (both - high.astype(f32)).astype(bf16)
        dd_s[i] = dot(member, high, NT) + dot(member, low, NT)

    def run(single):
        def body(head, carry):
            win, inside = head_window(head, hd)
            mine = pl.ds(pl.multiple_of(head * hd, 8), hd)
            zero = jnp.zeros((), bf16)
            for i in range(count):
                rows = slice(256 * i, 256 * i + 256)
                keys = slice(None) if single else rows
                q = jnp.where(inside, q_s[rows, win], zero)
                do = jnp.where(inside, do_s[rows, win], zero)
                lse = lse_s[i, pl.ds(head, 1)]
                dd = dd_s[i, pl.ds(head, 1)]
                s = dot(k_s[keys, win], q, NT)
                p = jnp.exp2(s * scale - lse)
                dp = dot(v_s[keys, win], do, NT)
                ds = (p * (dp - dd)).astype(bf16)
                p = p.astype(bf16)
                if single:
                    p_s[:, rows] = p
                    ds_s[:, rows] = ds
                else:
                    dv_s[rows, win] += dot(p, do, NN)
                    dk_s[rows, win] += dot(ds, q, NN)
                    dqt_s[mine, rows] = dot(kt_s[mine, rows].astype(bf16), ds, NN)
            if single:
                q = jnp.where(inside, q_s[:, win], zero)
                do = jnp.where(inside, do_s[:, win], zero)
                dv_s[:, win] += dot(p_s[...], do, NN)
                dk_s[:, win] += dot(ds_s[...], q, NN)
                dqt_s[mine, :] = dot(kt_s[mine, :].astype(bf16), ds_s[...], NN)
            return carry

        lax.fori_loop(0, heads, body, 0)

    one = flag_ref[0] == 1
    pl.when(one)(lambda: run(True))
    pl.when(jnp.logical_not(one))(lambda: run(False))
    for i in range(count):
        for j, dst in enumerate((g_mine, g_sib)):
            rows = slice(256 * i + 128 * j, 256 * i + 128 * j + 128)
            out = slice(128 * i, 128 * i + 128)
            dst[out, 0:pad] = (dqt_s[:, rows] * inv).T.astype(bf16)
            dst[out, pad : 2 * pad] = (dk_s[rows] * inv).astype(bf16)
            dst[out, 2 * pad : 3 * pad] = dv_s[rows].astype(bf16)
    if shared:
        g_far[:, 0:pad] = (dk_s[256 * count :] * inv).astype(bf16)
        g_far[:, pad : 2 * pad] = dv_s[256 * count :].astype(bf16)


def attend_back(flag, mine, sib, d_mine, d_sib, o_mine, o_sib, stat, far, heads, hd, count):
    pad = mine.shape[1] // 3
    tokens = 128 * count
    keys = 2 * tokens + (0 if far is None else far.shape[0])
    inputs = [flag, mine, sib, d_mine, d_sib, o_mine, o_sib, stat] + ([] if far is None else [far])
    outs = [shaped((tokens, 3 * pad)), shaped((tokens, 3 * pad))]
    if far is not None:
        outs.append(shaped((far.shape[0], 2 * pad)))
    return pl.pallas_call(
        functools.partial(attend_back_kernel, heads, hd, count, far is not None),
        out_shape=tuple(outs),
        in_specs=[SMEM] + [VMEM] * (len(inputs) - 1),
        out_specs=(VMEM,) * len(outs),
        scratch_shapes=[
            pltpu.VMEM((2 * tokens, pad), bf16),
            pltpu.VMEM((keys, pad), bf16),
            pltpu.VMEM((keys, pad), bf16),
            pltpu.VMEM((2 * tokens, pad), bf16),
            pltpu.VMEM((pad, keys), f32),
            pltpu.VMEM((pad, 2 * tokens), f32),
            pltpu.VMEM((keys, pad), f32),
            pltpu.VMEM((keys, pad), f32),
            pltpu.VMEM((keys, 2 * tokens), bf16),
            pltpu.VMEM((keys, 2 * tokens), bf16),
            pltpu.VMEM((count, heads, 256), f32),
            pltpu.VMEM((count, heads, 256), f32),
        ],
        compiler_params=pltpu.CompilerParams(vmem_limit_bytes=VMEM_LIMIT),
        cost_estimate=pl.CostEstimate(
            flops=2560 * heads * tokens * keys,
            bytes_accessed=12 * 2**20,
            transcendentals=heads * 2 * tokens * keys,
        ),
        name="attend_far_back" if far is not None else "attend_near_back",
    )(*inputs)


def middle_kernel(
    blk,
    core_ref,
    x_ref,
    cot_ref,
    am_ref,
    ao_ref,
    mod_ref,
    wpm_ref,
    wpo_ref,
    bp_ref,
    bd_ref,
    wu_ref,
    bu_ref,
    wd_ref,
    out_ref,
    gmid_ref,
    dom_ref,
    doo_ref,
    dwum_ref,
    dwuo_ref,
    dwd_ref,
    dbu_ref,
    dwpm_ref,
    dwpo_ref,
    dmod_ref,
    dbp_ref,
    dbd_ref,
    mid_s,
    br1_s,
    n_s,
    nt_s,
    db2_s,
    br2_s,
    gn_s,
    db1_s,
):
    step = pl.program_id(0)
    tokens, width = x_ref.shape
    blocks = tokens // blk
    part = width // 4

    @pl.when(step == 0)
    def _():
        br1_s[...] = (
            dot(am_ref[...], wpm_ref[...], NN) + dot(ao_ref[...], wpo_ref[...], NN) + bp_ref[...]
        )
        for i in range(blocks):
            rows = slice(i * blk, (i + 1) * blk)
            mid = x_ref[rows].astype(f32) + mod_ref[i, 2:3] * br1_s[rows]
            mid_s[rows] = mid
            y, _ = norm(mid)
            n = (y * (1.0 + mod_ref[i, 4:5]) + mod_ref[i, 3:4]).astype(bf16)
            n_s[rows] = n
            db2_s[rows] = (mod_ref[i, 5:6] * cot_ref[rows].astype(f32)).astype(bf16)
        for g in range(4):
            place = (g % 2 + core_ref[0] - 2 * (g % 2) * core_ref[0]) * (2 * part) + (g // 2) * part
            nt_s[pl.ds(pl.multiple_of(place, 16), part)] = (
                n_s[:, g * part : (g + 1) * part].astype(f32).T.astype(bf16)
            )
        br2_s[...] = jnp.zeros_like(br2_s)
        gn_s[...] = jnp.zeros_like(gn_s)

    pre = dot(n_s[...], wu_ref[...], NN) + bu_ref[...]
    square = pre * pre
    t = jnp.tanh(pre * (GELU_A + (GELU_A * GELU_B) * square))
    hidden = (0.5 * pre * (1.0 + t)).astype(bf16)
    slope = 0.5 * (1.0 + t) + 0.5 * pre * (1.0 - t * t) * (
        GELU_A + (3.0 * GELU_A * GELU_B) * square
    )
    br2_s[...] += dot(hidden, wd_ref[...], NN)
    gpre = dot(db2_s[...], wd_ref[...], NT) * slope
    gp = gpre.astype(bf16)
    gn_s[...] += dot(gp, wu_ref[...], NT)
    dwd_ref[...] = dot(hidden, db2_s[...], TN).astype(bf16)
    dwum_ref[...] = dot(nt_s[0 : 2 * part], gp, NN).astype(bf16)
    dwuo_ref[...] = dot(nt_s[2 * part : 4 * part], gp, NN).astype(bf16)
    dbu_ref[...] = jnp.sum(gpre, axis=0, keepdims=True)

    @pl.when(step == pl.num_programs(0) - 1)
    def _():
        dbp = jnp.zeros((1, width), f32)
        dbd = jnp.zeros((1, width), f32)
        for i in range(blocks):
            rows = slice(i * blk, (i + 1) * blk)
            cot = cot_ref[rows].astype(f32)
            br2 = br2_s[rows] + bd_ref[...]
            mid = mid_s[rows]
            out_ref[rows] = (mid + mod_ref[i, 5:6] * br2).astype(bf16)
            y, rstd = norm(mid)
            gn = gn_s[rows]
            u = gn * (1.0 + mod_ref[i, 4:5])
            gmid = cot + rstd * (
                u
                - jnp.mean(u, axis=-1, keepdims=True)
                - y * jnp.mean(u * y, axis=-1, keepdims=True)
            )
            gmid_ref[rows] = gmid.astype(bf16)
            db1 = mod_ref[i, 2:3] * gmid
            db1_s[rows] = db1.astype(bf16)
            dbp += jnp.sum(db1, axis=0, keepdims=True)
            dbd += jnp.sum(db2_s[rows].astype(f32), axis=0, keepdims=True)
            dmod_ref[i, 0:1] = jnp.sum(gmid * br1_s[rows], axis=0, keepdims=True)
            dmod_ref[i, 1:2] = jnp.sum(gn, axis=0, keepdims=True)
            dmod_ref[i, 2:3] = jnp.sum(gn * y, axis=0, keepdims=True)
            dmod_ref[i, 3:4] = jnp.sum(cot * br2, axis=0, keepdims=True)
        dbp_ref[...] = dbp
        dbd_ref[...] = dbd
        dom_ref[...] = dot(db1_s[...], wpm_ref[...], NT).astype(bf16)
        doo_ref[...] = dot(db1_s[...], wpo_ref[...], NT).astype(bf16)
        dwpm_ref[...] = dot(am_ref[...], db1_s[...], TN).astype(bf16)
        dwpo_ref[...] = dot(ao_ref[...], db1_s[...], TN).astype(bf16)


def middle(core, x, cot, att_m, att_o, mod, wp_m, wp_o, b_proj, b_down, w_up, b_up, w_down, blk):
    tokens, width = x.shape
    pad = att_m.shape[1]
    hidden = w_up.shape[1]
    chunk = 512
    steps = hidden // chunk
    half = width // 2

    def whole(shape):
        return pl.BlockSpec(shape, lambda j, c: (0,) * len(shape))

    return pl.pallas_call(
        functools.partial(middle_kernel, blk),
        grid_spec=pltpu.PrefetchScalarGridSpec(
            num_scalar_prefetch=1,
            grid=(steps,),
            in_specs=[VMEM] * 9
            + [
                pl.BlockSpec((width, chunk), lambda j, c: (0, j)),
                pl.BlockSpec((1, chunk), lambda j, c: (0, j)),
                pl.BlockSpec((chunk, width), lambda j, c: (j, 0)),
            ],
            out_specs=[VMEM] * 4
            + [
                pl.BlockSpec((half, chunk), lambda j, c: (0, j)),
                pl.BlockSpec((half, chunk), lambda j, c: (0, j)),
                pl.BlockSpec((chunk, width), lambda j, c: (j, 0)),
                pl.BlockSpec((1, chunk), lambda j, c: (0, j)),
            ]
            + [VMEM] * 5,
            scratch_shapes=[
                pltpu.VMEM((tokens, width), f32),
                pltpu.VMEM((tokens, width), f32),
                pltpu.VMEM((tokens, width), bf16),
                pltpu.VMEM((width, tokens), bf16),
                pltpu.VMEM((tokens, width), bf16),
                pltpu.VMEM((tokens, width), f32),
                pltpu.VMEM((tokens, width), f32),
                pltpu.VMEM((tokens, width), bf16),
            ],
        ),
        out_shape=(
            shaped((tokens, width)),
            shaped((tokens, width)),
            shaped((tokens, pad)),
            shaped((tokens, pad)),
            shaped((half, hidden)),
            shaped((half, hidden)),
            shaped((hidden, width)),
            shaped((1, hidden), f32),
            shaped((pad, width)),
            shaped((pad, width)),
            shaped((tokens // blk, 4, width), f32),
            shaped((1, width), f32),
            shaped((1, width), f32),
        ),
        compiler_params=pltpu.CompilerParams(vmem_limit_bytes=VMEM_LIMIT),
        cost_estimate=pl.CostEstimate(
            flops=2 * tokens * width * (6 * hidden + 6 * pad),
            bytes_accessed=60 * 2**20,
            transcendentals=tokens * hidden,
        ),
        name="middle",
    )(core, x, cot, att_m, att_o, mod, wp_m, wp_o, b_proj, b_down, w_up, b_up, w_down)


def first_back_kernel(blk, x_ref, ga_ref, gb_ref, gmid_ref, mod_ref, out_ref, dmod_ref):
    for i in range(x_ref.shape[0] // blk):
        rows = slice(i * blk, (i + 1) * blk)
        y, rstd = norm(x_ref[rows].astype(f32))
        gn = ga_ref[rows].astype(f32) + gb_ref[rows].astype(f32)
        u = gn * (1.0 + mod_ref[i, 1:2])
        back = rstd * (
            u - jnp.mean(u, axis=-1, keepdims=True) - y * jnp.mean(u * y, axis=-1, keepdims=True)
        )
        out_ref[rows] = (gmid_ref[rows].astype(f32) + back).astype(bf16)
        dmod_ref[i, 0:1] = jnp.sum(gn, axis=0, keepdims=True)
        dmod_ref[i, 1:2] = jnp.sum(gn * y, axis=0, keepdims=True)


def first_back(x, part_a, part_b, gmid, mod, blk):
    tokens, width = x.shape
    steps = 3
    rows = tokens // steps
    each = pl.BlockSpec((rows, width), lambda s: (s, 0))
    return pl.pallas_call(
        functools.partial(first_back_kernel, blk),
        grid=(steps,),
        in_specs=[each] * 4 + [pl.BlockSpec((rows // blk, 6, width), lambda s: (s, 0, 0))],
        out_specs=[each, pl.BlockSpec((rows // blk, 2, width), lambda s: (s, 0, 0))],
        out_shape=(shaped((tokens, width)), shaped((tokens // blk, 2, width), f32)),
        compiler_params=pltpu.CompilerParams(vmem_limit_bytes=VMEM_LIMIT),
        cost_estimate=pl.CostEstimate(
            flops=20 * tokens * width, bytes_accessed=10 * tokens * width, transcendentals=tokens
        ),
        name="first_back",
    )(x, part_a, part_b, gmid, mod)


def place_kernel(order_ref, in_ref, out_ref):
    out_ref[...] = in_ref[...].astype(out_ref.dtype)


def place(order, tiles, dtype):
    count = tiles.shape[0]
    block = (1,) + tiles.shape[1:]
    return pl.pallas_call(
        place_kernel,
        grid_spec=pltpu.PrefetchScalarGridSpec(
            num_scalar_prefetch=1,
            grid=(count,),
            in_specs=[pl.BlockSpec(block, lambda i, o: (o[i], 0, 0))],
            out_specs=pl.BlockSpec(block, lambda i, o: (i, 0, 0)),
        ),
        out_shape=shaped(tiles.shape, dtype),
        cost_estimate=pl.CostEstimate(
            flops=0, bytes_accessed=6 * math.prod(tiles.shape), transcendentals=0
        ),
        name="place",
    )(order, tiles)


def pick(values, index, axis=0):
    return lax.dynamic_index_in_dim(values, index, axis, keepdims=False)


def over_core(v):
    return lax.ppermute(v, "row", [(r, r ^ 1) for r in range(4)])


def over_x(v):
    return lax.ppermute(v, "row", [(r, r ^ 2) for r in range(4)])


def over_col(v, far):
    return lax.ppermute(v, "col", [(i, i ^ far) for i in range(4)])


def over_plane(v, dx, dz):
    swap = [(i, ((i // 4) ^ (2 * dx)) * 4 + ((i % 4) ^ dz)) for i in range(16)]
    return lax.ppermute(v, ("row", "col"), swap)


def over_img(v):
    if lax.axis_size("img") == 2:
        return v.astype(f32) + lax.ppermute(v, "img", [(0, 1), (1, 0)]).astype(f32)
    return lax.psum(v, "img").astype(f32)


def plus(a, b):
    return (a.astype(f32) + b.astype(f32)).astype(bf16)


def shards(
    tokens,
    conditioning,
    images_in_slot,
    w_qkv,
    b_qv,
    w_proj,
    b_proj,
    w_up,
    b_up,
    w_down,
    b_down,
    w_ada,
    b_ada,
    cotangent,
):
    slots, rows_tile, cols_tile, width = tokens.shape
    tile = rows_tile * cols_tile
    blk = 2 * tile
    count = slots * tile
    main = 8 * tile
    hd = width // HEADS
    heads = HEADS // 2
    half = width // 2
    pad = -(-half // 128) * 128
    hidden = w_up.shape[1]
    r, z = lax.axis_index("row"), lax.axis_index("col")
    x, core = r // 2, r % 2
    core_arr = core.reshape(1).astype(jnp.int32)
    assert lax.axis_size("row") == 4 and lax.axis_size("col") == 4 and slots == 12

    def spread(values):
        grouped = values.reshape(4, 3, tile, width)
        near, far, shared = [], [], []
        for dz in range(4):
            group = pick(grouped, z ^ dz)
            own = jnp.stack([pick(group, x), group[2]])
            other = pick(group, 1 - x)
            if dz:
                own = over_plane(own, 0, dz)
            near.append(own[0])
            shared.append(own[1])
            far.append(over_plane(other, 1, dz))
        return jnp.concatenate(near + far + shared, axis=0)

    def collect(values, dtype):
        tiles = values.reshape(12, tile, width)
        near, far, shared = [], [], []
        for dz in range(4):
            own = jnp.stack([tiles[dz], tiles[8 + dz]])
            if dz:
                own = over_plane(own, 0, dz)
            near.append(own[0])
            shared.append(own[1])
            far.append(over_plane(tiles[4 + dz], 1, dz))
        stacked = jnp.stack(near + far + shared)
        slot = jnp.arange(12, dtype=jnp.int32)
        kind = slot % 3
        dz = (slot // 3) ^ z
        order = jnp.where(kind == 2, 8 + dz, ((kind ^ x) & 1) * 4 + dz)
        return place(order, stacked, dtype).reshape(tokens.shape)

    inputs = spread(tokens)
    upstream = spread(cotangent)

    four_way = images_in_slot == 4
    kinds = pick(four_way.reshape(4, 3), z)
    main_four, shared_four = pick(kinds, x), kinds[2]
    quarter = jnp.stack([2 * (x ^ dx) + ((z // 2) ^ dz) for dx in range(2) for dz in range(2)])
    picks = jnp.concatenate(
        [jnp.where(main_four, quarter, 0), jnp.where(shared_four, quarter[:2], 0)]
    )
    places = jnp.concatenate([jnp.full((4,), x, jnp.int32), jnp.full((2,), 2, jnp.int32)]) * 4 + picks
    flag_main = jnp.where(main_four, 0, 1).reshape(1).astype(jnp.int32)
    flag_shared = jnp.where(shared_four, 0, 1).reshape(1).astype(jnp.int32)
    cond = conditioning.astype(f32)
    silu = jax.nn.silu(cond).astype(bf16)
    silu_groups = silu.reshape(4, 12, width)
    chosen = jnp.take(pick(silu_groups, z), places, axis=0)
    mod = (jnp.dot(chosen, w_ada, preferred_element_type=f32) + b_ada).reshape(6, 6, width)

    def widen(v, axis):
        return jnp.pad(v, [(0, pad - half) if a == axis else (0, 0) for a in range(v.ndim)])

    w_half = widen(w_qkv.reshape(width, 3, 2, half), 3).transpose(2, 0, 1, 3)
    w_half = w_half.reshape(2, width, 3 * pad)
    b_three = jnp.stack([b_qv[:width], jnp.zeros_like(b_qv[:width]), b_qv[width:]])
    b_half = widen(b_three.reshape(3, 2, half).astype(f32), 2).transpose(1, 0, 2)
    b_half = b_half.reshape(2, 1, 3 * pad)
    w_proj_half = widen(w_proj.reshape(2, half, width), 1)
    wp_mine, wp_other = pick(w_proj_half, core), pick(w_proj_half, 1 - core)

    qkv_other, qkv_mine, normed_t = qkv(core_arr, inputs, mod, w_half, b_half, blk)
    qkv_sib = over_core(qkv_other)
    normed_sib = over_core(normed_t)
    far_kv = over_x(jnp.concatenate([qkv_mine[main:, pad:], qkv_sib[main:, pad:]], axis=0))
    om_near, os_near, stat_near = attend(flag_main, qkv_mine, qkv_sib, None, heads, hd, 4)
    back_near = over_core(os_near)
    om_far, os_far, stat_far = attend(flag_shared, qkv_mine, qkv_sib, far_kv, heads, hd, 2)
    back_far = over_core(os_far)
    att_mine = jnp.concatenate([om_near, om_far], axis=0)
    att_other = jnp.concatenate([back_near, back_far], axis=0)

    (
        out,
        gmid,
        do_mine,
        do_other,
        dwu_mine,
        dwu_other,
        dwd,
        dbu,
        dwp_mine,
        dwp_other,
        dmod_mid,
        dbp,
        dbd,
    ) = middle(
        core_arr,
        inputs,
        upstream,
        att_mine,
        att_other,
        mod,
        wp_mine,
        wp_other,
        b_proj.astype(f32).reshape(1, width),
        b_down.astype(f32).reshape(1, width),
        w_up,
        b_up.astype(f32).reshape(1, hidden),
        w_down,
        blk,
    )
    output = collect(out, bf16)
    do_sib = over_core(do_other)

    def reduce_plane(mine):
        got = over_x(pick(mine, 1 - x))
        mine = plus(pick(mine, x), got)
        return reduce_col(mine)

    def reduce_col(mine):
        split = mine.reshape((2, 2) + mine.shape[1:])
        got = over_col(pick(split, 1 - z % 2, 1), 1)
        mine = plus(pick(split, z % 2, 1), got)
        got = over_col(pick(mine, 1 - z // 2), 2)
        mine = plus(pick(mine, z // 2), got)
        return over_img(mine)

    dwd_halves = dwd.reshape(2, 2, hidden // 4, width)
    dwd_sum = plus(pick(dwd_halves, core, 1), over_core(pick(dwd_halves, 1 - core, 1)))
    grad_w_down = reduce_plane(dwd_sum.reshape(2, 4, hidden // 16, width))
    dwu_sum = plus(dwu_mine, over_core(dwu_other))
    grad_w_up = reduce_plane(dwu_sum.reshape(2, 4, width // 16, hidden))
    dwp = jnp.stack([dwp_mine, dwp_other])
    dwp = jnp.stack([pick(dwp, core), pick(dwp, 1 - core)])[:, :half]
    dwp = dwp.reshape(2, 2, half // 2, width)
    dwp_sum = plus(pick(dwp, core, 1), over_core(pick(dwp, 1 - core, 1)))
    grad_w_proj = reduce_plane(dwp_sum.reshape(2, 4, width // 16, width))

    gm_far, gs_far, g_far = attend_back(
        flag_shared,
        qkv_mine,
        qkv_sib,
        do_mine[main:],
        do_sib[main:],
        om_far,
        os_far,
        stat_far,
        far_kv,
        heads,
        hd,
        2,
    )
    far_back = over_x(g_far)
    gm_near, gs_near = attend_back(
        flag_main, qkv_mine, qkv_sib, do_mine, do_sib, om_near, os_near, stat_near, None, heads, hd, 4
    )
    gm_far = jnp.concatenate([gm_far[:, :pad], plus(gm_far[:, pad:], far_back[: count - main])], 1)
    gs_far = jnp.concatenate([gs_far[:, :pad], plus(gs_far[:, pad:], far_back[count - main :])], 1)
    g_mine = jnp.concatenate([gm_near, gm_far], axis=0)
    g_sib = jnp.concatenate([gs_near, gs_far], axis=0)
    w_half_mine = pick(w_half, core)
    gn_other = over_core(dot(g_sib, w_half_mine, NT).astype(bf16))
    gn_mine = dot(g_mine, w_half_mine, NT).astype(bf16)
    dwq = (dot(normed_t, g_mine, NN) + dot(normed_sib, g_sib, NN)).astype(bf16)
    dwq = reduce_plane(
        dwq.reshape(2, 2, 4, width // 16, 3 * pad).transpose(0, 2, 1, 3, 4)
    )
    swap = over_core(pick(dwq, 1 - core).astype(bf16))
    parts = jnp.stack([pick(dwq, core), swap.astype(f32)])
    parts = jnp.stack([pick(parts, core), pick(parts, 1 - core)])
    parts = parts.reshape(2, width // 16, 3, pad)[..., :half]
    grad_w_qkv = parts.transpose(1, 2, 0, 3).reshape(width // 16, 3 * width)

    grad_x, dmod_first = first_back(inputs, gn_mine, gn_other, gmid, mod, blk)
    grad_tokens = collect(grad_x, f32)

    one_hot = (jnp.arange(12, dtype=jnp.int32)[:, None] == places[None, :]).astype(f32)
    silu_rel = jnp.concatenate([pick(silu_groups, z ^ dz) for dz in range(4)], axis=0)
    rank = r * 4 + z
    silu_rows = lax.dynamic_slice_in_dim(silu_rel, rank * (width // 16), width // 16, 1)

    def modulation_grads(dmod, columns):
        values = jnp.sum(one_hot[:, :, None] * dmod.reshape(1, 6, -1), axis=1).astype(bf16)
        values = plus(values, over_core(values))
        values = plus(values, over_x(values))
        every = jnp.concatenate(
            [values] + [over_col(values, dz) for dz in range(1, 4)], axis=0
        )
        d_w = over_img(dot(silu_rows, every, TN).astype(bf16))
        d_b = jnp.sum(every.astype(f32), axis=0)
        d_s = dot(every, w_ada[:, columns], NT)
        return d_w, d_b, d_s

    late = modulation_grads(dmod_first, slice(0, 2 * width))
    early = modulation_grads(dmod_mid, slice(2 * width, 6 * width))
    grad_w_ada = jnp.concatenate([late[0], early[0]], axis=1)
    d_s = (late[2] + early[2]).reshape(4, 12, width)
    d_s = jnp.stack([pick(d_s, z ^ g) for g in range(4)]).reshape(slots, 4, width)
    sig = jax.nn.sigmoid(cond)
    grad_conditioning = d_s * (sig * (1.0 + cond * (1.0 - sig)))

    db_three = jnp.sum(g_mine.astype(f32), axis=0) + jnp.sum(g_sib.astype(f32), axis=0)
    db_three = db_three.reshape(3, pad)[:, :half]
    db_three = jnp.where(
        (jnp.arange(2) == core)[None, :, None], db_three[:, None, :], 0.0
    ).reshape(3, width)
    small = jnp.concatenate([db_three[0], db_three[2], dbp[0], dbu[0], dbd[0]])
    small = lax.psum(small, ("row", "col", "img"))
    d_ada = jnp.concatenate([late[1], early[1]])
    d_ada = lax.dynamic_slice_in_dim(d_ada, rank * (6 * width // 16), 6 * width // 16, 0)
    grad_b_ada = over_img(d_ada)

    def own(start, size):
        return lax.dynamic_slice_in_dim(small, start + rank * (size // 16), size // 16, 0)

    return (
        output,
        grad_tokens,
        grad_conditioning,
        grad_w_qkv,
        own(0, 2 * width),
        grad_w_proj,
        own(2 * width, width),
        grad_w_up,
        own(3 * width, hidden),
        grad_w_down,
        own(3 * width + hidden, width),
        grad_w_ada,
        grad_b_ada,
    )


def solution(mesh):
    grid = P("img", "row", "col", None)
    plane = ("row", "col")
    return jax.shard_map(
        shards,
        mesh=mesh,
        in_specs=(grid, P("img", None, None), P("img")) + (P(),) * 10 + (grid,),
        out_specs=(grid, grid, P("img", None, None))
        + (P(plane, None), P(plane)) * 5,
        check_vma=False,
    )
```

time: 1810 us -> 952 us (0.53)
  waiting for transfers between devices: 1070 us -> 329 us
  matrix products: 360 us -> 59.2 us
  Pallas kernels: 0 us -> 215 us
  starting transfers between devices: 0.67 us -> 94.4 us
  local copies, waits for them, and re-layouts: 203 us -> 139 us
  blocking collectives: 65.7 us -> 40.6 us
    reduce_scatter x4 -> x0, waiting for transfers between devices: 660 us -> none  [the longest x1 270 us: shards(): lax.psum_scatter(value_terms.astype(jnp.bfloat16), ('row', 'col'), scatte...]
    ppermute x0 -> x69, waiting for transfers between devices: none -> 329 us  [the longest x14 108 us: over_col(): return lax.ppermute(v, 'col', [(i, i ^ far) for i in range(4)])]
    dot_general x21 -> x9, matrix products: 360 us -> 59.2 us  [the longest x8 51.4 us: dot(): return lax.dot_general(left, right, dims, preferred_element_type=f32)]
    pallas_call x0 -> x9, Pallas kernels: none -> 215 us  [the longest x1 84.1 us: middle(): pl.pallas_call(functools.partial(middle_kernel, blk), grid_spec=pltpu.Pre...]
    all_gather x2 -> x0, waiting for transfers between devices: 201 us -> none  [the longest x1 137 us: shards(): lax.all_gather(keys_local, ('row', 'col'), axis=1, tiled=True)]
    unnamed x12 -> x0, waiting for transfers between devices: 169 us -> none
    convert_element_type x6 -> x1, local copies, waits for them, and re-layouts: 102 us -> 0.04 us  [shards(): swap = over_core(pick(dwq, 1 - core).astype(bf16))]
    ppermute x0 -> x69, starting transfers between devices: none -> 94.4 us  [the longest x28 47.6 us: over_plane(): return lax.ppermute(v, ('row', 'col'), swap)]
  transfers between devices with their start and end apart: 10 -> 69, of which waited for: 10 -> 24; matrix products, arithmetic and copies ran while one was open for 17% -> 26% of each run, Pallas kernels for 0% -> 21%
where the time goes in v1:
time: 952 us; the launch traced here: 940 us
  waiting for transfers between devices  329 us (35%)
  Pallas kernels  215 us (23%)
  local copies, waits for them, and re-layouts  139 us (15%)
  starting transfers between devices  94.4 us (10%)
  matrix products  59.2 us (6%)
  other arithmetic  59.1 us (6%)
  blocking collectives  40.6 us (4%)
    ppermute x14, waiting for transfers between devices, over_col(): return lax.ppermute(v, 'col', [(i, i ^ far) for i in range(4)])  108 us
    ppermute x28, waiting for transfers between devices, over_plane(): return lax.ppermute(v, ('row', 'col'), swap)  99.2 us
    ppermute x8, waiting for transfers between devices, over_x(): return lax.ppermute(v, 'row', [(r, r ^ 2) for r in range(4)])  97.8 us
    pallas_call x1, Pallas kernels, middle(): pl.pallas_call(functools.partial(middle_kernel, blk), grid_spec=pltpu.Pre...  84.1 us
    unnamed x167, local copies, waits for them, and re-layouts  56.9 us
    dot_general x8, matrix products, dot(): return lax.dot_general(left, right, dims, preferred_element_type=f32)  51.4 us
    pallas_call x2, Pallas kernels, attend(): pl.pallas_call(functools.partial(attend_kernel, heads, hd, count, far is...  48.3 us
    ppermute x28, starting transfers between devices, over_plane(): return lax.ppermute(v, ('row', 'col'), swap)  47.6 us
  transfers between devices with their start and end apart: 69, of which 24 were waited for; matrix products, arithmetic and copies ran while one was open for 26% of the time, Pallas kernels for 21%

profile of v1, /device:TPU:0, one launch (start us, length us, event | category | flops | bytes accessed | tf_op | source)
XLA Modules:
  0.0 939.6 jit_solution(11157629010369511252)
XLA Ops:
  28.5 11.4 %copy.39 = bf16[1152,3456]{0,1:T(8,128)(2,1)} copy(bf16[1152,3456]{1,0:T(8,128)(2,1)} %param.17) | data formatting | bytes 15925248 | tf_op args[3]
  55.2 12.6 %copy.41.w_ref = bf16[2,1152,1920]{2,1,0:T(8,128)(2,1)} copy(bf16[2,1152,1920]{1,2,0:T(8,128)(2,1)} %bitcast.294) | data formatting | bytes 17694720 | tf_op jit(solution)/shard_map/reshape | solution.py:665
  76.7 10.3 %collective-permute-done.7 = bf16[2,64,1152]{2,1,0:T(8,128)(2,1)S(1)} collective-permute-done((bf16[2,64,1152]{2,1,0:T(8,128)(2,1)}, bf16[2,64,1152]{2,1,0:T(8,128)(2,1)S(1)}, u32[]{:S(2)}, u32[]{:S(2)}) %collective-permute-start.7) | collective-permute-done | bytes 294944 | tf_op jit(solution)/shard_map/ppermute | solution.py:567
  88.7 12.7 %collective-permute-done.8 = bf16[2,64,1152]{2,1,0:T(8,128)(2,1)S(1)} collective-permute-done((bf16[2,64,1152]{2,1,0:T(8,128)(2,1)S(1)}, bf16[2,64,1152]{2,1,0:T(8,128)(2,1)S(1)}, u32[]{:S(2)}, u32[]{:S(2)}) %collective-permute-start.8) | collective-permute-done | bytes 294944 | tf_op jit(solution)/shard_map/ppermute | solution.py:567
  138.9 16.5 %qkv.1 = (bf16[768,1920]{1,0:T(8,128)(2,1)}, bf16[768,1920]{1,0:T(8,128)(2,1)}, bf16[1152,768]{1,0:T(8,128)(2,1)}) custom-call(s32[1]{0:T(128)} %bitcast.core_ref, bf16[768,1152]{1,0:T(8,128)(2,1)} %copy-done.10, f32[6,6,1152]{2,1,0:T(8,128)} %reshape.297.mod_ref, bf16[2,1152,1920]{2,1,0:T(8,128)(2,1)} %copy.41.w_ref, f32[2,1,1920]{2,1,0:T(1,128)} %copy.42.b_ref), custom_call_target="tpu_custom_call" | custom-call | flops 6794772480 | bytes 20971520 | tf_op jit(solution)/shard_map/qkv/pallas_call | solution.py:73
  167.5 38.1 %attend_near.1 = (bf16[512,640]{1,0:T(8,128)(2,1)}, bf16[512,640]{1,0:T(8,128)(2,1)}, f32[1024,128]{1,0:T(8,128)}) custom-call(s32[1]{0:T(128)} %bitcast.40.flag_ref, bf16[768,1920]{1,0:T(8,128)(2,1)} %get-tuple-element.42.mine_ref, bf16[768,1920]{1,0:T(8,128)(2,1)} %collective-permute-done.14.sib_ref), custom_call_target="tpu_custom_call" | custom-call | flops 4294967296 | bytes 8388608 | tf_op jit(solution)/shard_map/attend_near/pallas_call | solution.py:165
  205.6 10.2 %attend_far.1 = (bf16[256,640]{1,0:T(8,128)(2,1)}, bf16[256,640]{1,0:T(8,128)(2,1)}, f32[512,128]{1,0:T(8,128)}) custom-call(s32[1]{0:T(128)} %bitcast.52.flag_ref, bf16[768,1920]{1,0:T(8,128)(2,1)} %get-tuple-element.42.mine_ref, bf16[768,1920]{1,0:T(8,128)(2,1)} %collective-permute-done.14.sib_ref, bf16[512,1280]{1,0:T(8,128)(2,1)} %collective-permute-done.15.rest_0_.rest_5_), custom_call_target="tpu_custom_call" | custom-call | flops 2147483648 | bytes 8388608 | tf_op jit(solution)/shard_map/attend_far/pallas_call | solution.py:165
  220.0 84.1 %middle.1 = (bf16[768,1152]{1,0:T(8,128)(2,1)}, bf16[768,1152]{1,0:T(8,128)(2,1)}, bf16[768,640]{1,0:T(8,128)(2,1)}, bf16[768,640]{1,0:T(8,128)(2,1)}, bf16[576,...) custom-call(s32[1]{0:T(128)} %bitcast.core_ref, ...), custom_call_target="tpu_custom_call" | custom-call | flops 55717134336 | bytes 62914560 | tf_op jit(solution)/shard_map/middle/pallas_call | solution.py:438
  394.6 12.6 %attend_far_back.1 = (bf16[256,1920]{1,0:T(8,128)(2,1)}, bf16[256,1920]{1,0:T(8,128)(2,1)}, bf16[512,1280]{1,0:T(8,128)(2,1)}) custom-call(s32[1]{0:T(128)} %bitcast.52.flag_ref, bf16[768,1920]{1,0:T(8,128)(2,1)} %get-tuple-element.42.mine_ref, bf16[768,1920]{1,0:T(8,128)(2,1)} %collective-permute-done.14.sib_ref, bf16[256,640]{1,0:T(8,128)(2,1)} %slice.378.rest_0_, ...), custom_call_target="tpu_custom_call" | custom-call | flops 5368709120 | bytes 12582912 | tf_op jit(solution)/shard_map/attend_far_back/pallas_call | solution.py:284
  409.9 30.0 %attend_near_back.1 = (bf16[512,1920]{1,0:T(8,128)(2,1)}, bf16[512,1920]{1,0:T(8,128)(2,1)}) custom-call(s32[1]{0:T(128)} %bitcast.40.flag_ref, bf16[768,1920]{1,0:T(8,128)(2,1)} %get-tuple-element.42.mine_ref, bf16[768,1920]{1,0:T(8,128)(2,1)} %collective-permute-done.14.sib_ref, bf16[768,640]{1,0:T(8,128)(2,1)} %get-tuple-element.49.rest_0_, ...), custom_call_target="tpu_custom_call" | custom-call | flops 10737418240 | bytes 12582912 | tf_op jit(solution)/shard_map/attend_near_back/pallas_call | solution.py:284
  445.1 40.5 %collective-permute-done.52 = bf16[4,72,1152]{2,1,0:T(8,128)(2,1)S(1)} collective-permute-done((bf16[4,72,1152]{2,1,0:T(8,128)(2,1)S(1)}, bf16[4,72,1152]{2,1,0:T(8,128)(2,1)S(1)}, u32[]{:S(2)}, u32[]{:S(2)}) %collective-permute-start.52) | collective-permute-done | bytes 663584 | tf_op jit(solution)/shard_map/ppermute | solution.py:558
  494.5 10.9 %fusion.18 = bf16[768,1152]{1,0:T(8,128)(2,1)} fusion(bf16[2,1152,1920]{1,2,0:T(8,128)(2,1)} %bitcast.295, s32[]{:T(128)S(6)} %select_n.277, bf16[256,1280]{1,0:T(8,128)(2,1)S(1)} %get-tuple-element.119, bf16[256,640]{1,0:T(8,128)(2,1)S(1)} %copy-done.21, bf16[512,1920]{1,0:T(8,128)(2,1)S(1)} %copy-done.13), kind=kOutput, calls=%fused_computation.30 | convolution fusion | flops 3407118336 | bytes 9142276 | tf_op jit(solution)/shard_map/dot_general | solution.py:29
  521.7 9.6 %fusion.3 = bf16[1152,1920]{1,0:T(8,128)(2,1)S(1)} fusion(f32[1152,1920]{1,0:T(8,128)S(1)} %fusion.76, bf16[1152,768]{1,0:T(8,128)(2,1)} %get-tuple-element.62, bf16[256,1280]{1,0:T(8,128)(2,1)S(1)} %get-tuple-element.120, bf16[256,640]{1,0:T(8,128)(2,1)S(1)} %copy-done.20, bf16[512,1920]{1,0:T(8,128)(2,1)S(1)} %copy-done.12), kind=kOutput, calls=%fused_computation.9 | convolution fusion | flops 3410657280 | bytes 17989632 | tf_op jit(solution)/shard_map/dot_general | solution.py:29
  536.7 9.1 collective-permute-start.54
  555.7 40.6 %psum.7 = f32[9216]{0:T(1024)} all-reduce(f32[9216]{0:T(1024)} %constant_dynamic-update-slice_fusion.9), channel_id=1, replica_groups=mesh['img'=2,'row'=4,'col'=4] {'row','col','img'}, use_global_device_ids=true, to_apply=%region_4.5 | all-reduce | flops 9216 | bytes 73728 | tf_op jit(solution)/shard_map/psum | solution.py:809
  654.0 21.4 %collective-permute-done.29 = bf16[2,64,1152]{2,1,0:T(8,128)(2,1)S(1)} collective-permute-done((bf16[2,64,1152]{2,1,0:T(8,128)(2,1)}, bf16[2,64,1152]{2,1,0:T(8,128)(2,1)S(1)}, u32[]{:S(2)}, u32[]{:S(2)}) %collective-permute-start.29) | collective-permute-done | bytes 294944 | tf_op jit(solution)/shard_map/ppermute | solution.py:567
  703.8 8.6 place.3
  732.4 10.3 %collective-permute-done.47 = bf16[2,2,72,1920]{3,2,1,0:T(8,128)(2,1)} collective-permute-done((bf16[2,2,72,1920]{3,2,1,0:T(8,128)(2,1)}, bf16[2,2,72,1920]{3,2,1,0:T(8,128)(2,1)}, u32[]{:S(2)}, u32[]{:S(2)}) %collective-permute-start.47) | collective-permute-done | bytes 1105952 | tf_op jit(solution)/shard_map/ppermute | solution.py:562
  746.8 24.3 %collective-permute-done.48 = bf16[2,72,1920]{2,1,0:T(8,128)(2,1)S(1)} collective-permute-done((bf16[2,72,1920]{2,1,0:T(8,128)(2,1)S(1)}, bf16[2,72,1920]{2,1,0:T(8,128)(2,1)S(1)}, u32[]{:S(2)}, u32[]{:S(2)}) %collective-permute-start.48) | collective-permute-done | bytes 552992 | tf_op jit(solution)/shard_map/ppermute | solution.py:562
  773.3 11.4 %collective-permute-done.49 = bf16[2,72,1920]{2,1,0:T(8,128)(2,1)S(1)} collective-permute-done((bf16[2,72,1920]{2,1,0:T(8,128)(2,1)S(1)}, bf16[2,72,1920]{2,1,0:T(8,128)(2,1)S(1)}, u32[]{:S(2)}, u32[]{:S(2)}) %collective-permute-start.49) | collective-permute-done | bytes 552992 | tf_op jit(solution)/shard_map/ppermute | solution.py:572
  790.2 52.9 %collective-permute-done.57 = bf16[4,72,4608]{2,1,0:T(8,128)(2,1)S(1)} collective-permute-done((bf16[4,72,4608]{2,1,0:T(8,128)(2,1)S(1)}, bf16[4,72,4608]{2,1,0:T(8,128)(2,1)S(1)}, u32[]{:S(2)}, u32[]{:S(2)}) %collective-permute-start.57) | collective-permute-done | bytes 2654240 | tf_op jit(solution)/shard_map/ppermute | solution.py:558
  847.2 40.9 %collective-permute-done.58 = bf16[2,72,4608]{2,1,0:T(8,128)(2,1)S(1)} collective-permute-done((bf16[2,72,4608]{2,1,0:T(8,128)(2,1)S(1)}, bf16[2,72,4608]{2,1,0:T(8,128)(2,1)S(1)}, u32[]{:S(2)}, u32[]{:S(2)}) %collective-permute-start.58) | collective-permute-done | bytes 1327136 | tf_op jit(solution)/shard_map/ppermute | solution.py:562
  894.7 24.1 %collective-permute-done.59 = bf16[72,4608]{1,0:T(8,128)(2,1)} collective-permute-done((bf16[72,4608]{1,0:T(8,128)(2,1)}, bf16[72,4608]{1,0:T(8,128)(2,1)}, u32[]{:S(2)}, u32[]{:S(2)}) %collective-permute-start.59) | collective-permute-done | bytes 663584 | tf_op jit(solution)/shard_map/ppermute | solution.py:562
  925.0 12.1 %collective-permute-done.60 = bf16[72,4608]{1,0:T(8,128)(2,1)} collective-permute-done((bf16[72,4608]{1,0:T(8,128)(2,1)S(1)}, bf16[72,4608]{1,0:T(8,128)(2,1)}, u32[]{:S(2)}, u32[]{:S(2)}) %collective-permute-start.60) | collective-permute-done | bytes 663584 | tf_op jit(solution)/shard_map/ppermute | solution.py:572
  (442 shorter events, 381.2 us)
Async XLA Ops:
  3.8 65.7 %collective-permute-start = (bf16[2,64,1152]{2,1,0:T(8,128)(2,1)}, bf16[2,64,1152]{2,1,0:T(8,128)(2,1)S(1)}, u32[]{:S(2)}, u32[]{:S(2)}) collective-permute-start(bf16[2,64,1152]{2,1,0:T(8,128)(2,1)} %pad_maximum_fusion.7), channel_id=1, source_target_pairs={{0,1},{1,0},{2,3},{3,2},{4,5},{5,4},{6,7},{7,6},{8,9},{9,8},{10,11... | collective-permute-start | bytes 884744 | tf_op jit(solution)/shard_map/ppermute | solution.py:567
  7.6 66.5 %collective-permute-start.1 = (bf16[2,64,1152]{2,1,0:T(8,128)(2,1)}, bf16[2,64,1152]{2,1,0:T(8,128)(2,1)}, u32[]{:S(2)}, u32[]{:S(2)}) collective-permute-start(bf16[2,64,1152]{2,1,0:T(8,128)(2,1)} %pad_maximum_fusion.8), channel_id=1, source_target_pairs={{0,2},{1,3},{2,0},{3,1},{4,6},{5,7},{6,4},{7,5},{8,10},{9,11},{10,... | collective-permute-start | bytes 884744 | tf_op jit(solution)/shard_map/ppermute | solution.py:567
  10.9 64.2 %collective-permute-start.2 = (bf16[2,64,1152]{2,1,0:T(8,128)(2,1)}, bf16[2,64,1152]{2,1,0:T(8,128)(2,1)}, u32[]{:S(2)}, u32[]{:S(2)}) collective-permute-start(bf16[2,64,1152]{2,1,0:T(8,128)(2,1)} %pad_maximum_fusion.9), channel_id=1, source_target_pairs={{0,3},{1,2},{2,1},{3,0},{4,7},{5,6},{6,5},{7,4},{8,11},{9,10},{10,... | collective-permute-start | bytes 884744 | tf_op jit(solution)/shard_map/ppermute | solution.py:567
  10.9 104.7 %collective-permute-start.3 = (bf16[64,1152]{1,0:T(8,128)(2,1)}, bf16[64,1152]{1,0:T(8,128)(2,1)}, u32[]{:S(2)}, u32[]{:S(2)}) collective-permute-start(bf16[64,1152]{1,0:T(8,128)(2,1)} %get-tuple-element.112), channel_id=1, source_target_pairs={{0,8},{1,9},{2,10},{3,11},{4,12},{5,13},{6,14},{7,15},{8,0},{9,1},... | collective-permute-start | bytes 442376 | tf_op jit(solution)/shard_map/ppermute | solution.py:567
  12.7 106.2 %collective-permute-start.4 = (bf16[64,1152]{1,0:T(8,128)(2,1)}, bf16[64,1152]{1,0:T(8,128)(2,1)S(1)}, u32[]{:S(2)}, u32[]{:S(2)}) collective-permute-start(bf16[64,1152]{1,0:T(8,128)(2,1)} %get-tuple-element.111), channel_id=1, source_target_pairs={{0,9},{1,8},{2,11},{3,10},{4,13},{5,12},{6,15},{7,14},{8,1},{9,0},... | collective-permute-start | bytes 442376 | tf_op jit(solution)/shard_map/ppermute | solution.py:567
  69.6 50.5 %collective-permute-start.5 = (bf16[64,1152]{1,0:T(8,128)(2,1)}, bf16[64,1152]{1,0:T(8,128)(2,1)S(1)}, u32[]{:S(2)}, u32[]{:S(2)}) collective-permute-start(bf16[64,1152]{1,0:T(8,128)(2,1)} %get-tuple-element.110), channel_id=1, source_target_pairs={{0,10},{1,11},{2,8},{3,9},{4,14},{5,15},{6,12},{7,13},{8,2},{9,3},... | collective-permute-start | bytes 442376 | tf_op jit(solution)/shard_map/ppermute | solution.py:567
  74.1 49.1 %collective-permute-start.6 = (bf16[64,1152]{1,0:T(8,128)(2,1)}, bf16[64,1152]{1,0:T(8,128)(2,1)S(1)}, u32[]{:S(2)}, u32[]{:S(2)}) collective-permute-start(bf16[64,1152]{1,0:T(8,128)(2,1)} %get-tuple-element.109), channel_id=1, source_target_pairs={{0,11},{1,10},{2,9},{3,8},{4,15},{5,14},{6,13},{7,12},{8,3},{9,2},... | collective-permute-start | bytes 442376 | tf_op jit(solution)/shard_map/ppermute | solution.py:567
  162.6 353.5 %collective-permute-start.45 = (bf16[1152,768]{1,0:T(8,128)(2,1)}, bf16[1152,768]{1,0:T(8,128)(2,1)}, u32[]{:S(2)}, u32[]{:S(2)}) collective-permute-start(bf16[1152,768]{1,0:T(8,128)(2,1)} %get-tuple-element.62), channel_id=1, source_target_pairs={{0,4},{4,0},{8,12},{12,8},{1,5},{5,1},{9,13},{13,9},{2,6},{6,2},{1... | collective-permute-start | bytes 5308424 | tf_op jit(solution)/shard_map/ppermute | solution.py:554
  308.8 84.1 %collective-permute-start.25 = (bf16[768,640]{1,0:T(8,128)(2,1)}, bf16[768,640]{1,0:T(8,128)(2,1)}, u32[]{:S(2)}, u32[]{:S(2)}) collective-permute-start(bf16[768,640]{1,0:T(8,128)(2,1)} %get-tuple-element.50), channel_id=1, source_target_pairs={{0,4},{4,0},{8,12},{12,8},{1,5},{5,1},{9,13},{13,9},{2,6},{6,2},{1... | collective-permute-start | bytes 2949128 | tf_op jit(solution)/shard_map/ppermute | solution.py:554
  381.5 338.3 %collective-permute-start.61 = (bf16[2,1152,1152]{2,1,0:T(8,128)(2,1)}, bf16[2,1152,1152]{2,1,0:T(8,128)(2,1)}, u32[]{:S(2)}, u32[]{:S(2)}) collective-permute-start(bf16[2,1152,1152]{2,1,0:T(8,128)(2,1)} %dynamic-slice_bitcast_fusion), channel_id=1, source_target_pairs={{0,4},{4,0},{8,12},{12,8},{1,5},{5,1},{9,13},{13,9},{2,6},{6,2},{1... | collective-permute-start | bytes 15925256 | tf_op jit(solution)/shard_map/ppermute | solution.py:554
  381.5 345.3 %collective-permute-start.56 = (bf16[576,4608]{1,0:T(8,128)(2,1)}, bf16[576,4608]{1,0:T(8,128)(2,1)}, u32[]{:S(2)}, u32[]{:S(2)}) collective-permute-start(bf16[576,4608]{1,0:T(8,128)(2,1)} %get-tuple-element.69), channel_id=1, source_target_pairs={{0,4},{4,0},{8,12},{12,8},{1,5},{5,1},{9,13},{13,9},{2,6},{6,2},{1... | collective-permute-start | bytes 15925256 | tf_op jit(solution)/shard_map/ppermute | solution.py:554
  382.0 57.9 %collective-permute-start.51 = (bf16[2,288,1152]{2,1,0:T(8,128)(2,1)}, bf16[2,288,1152]{2,1,0:T(8,128)(2,1)}, u32[]{:S(2)}, u32[]{:S(2)}) collective-permute-start(bf16[2,288,1152]{2,1,0:T(8,128)(2,1)} %dynamic-slice_bitcast_fusion.5), channel_id=1, source_target_pairs={{0,4},{4,0},{8,12},{12,8},{1,5},{5,1},{9,13},{13,9},{2,6},{6,2},{1... | collective-permute-start | bytes 3981320 | tf_op jit(solution)/shard_map/ppermute | solution.py:554
  392.8 48.9 %collective-permute-start.67 = (bf16[72,4608]{1,0:T(8,128)(2,1)S(1)}, bf16[72,4608]{1,0:T(8,128)(2,1)}, u32[]{:S(2)}, u32[]{:S(2)}) collective-permute-start(bf16[72,4608]{1,0:T(8,128)(2,1)S(1)} %convolution_convert_fusion), channel_id=1, source_target_pairs={{0,16},{16,0},{1,17},{17,1},{2,18},{18,2},{3,19},{19,3},{4,20},{20... | collective-permute-start | bytes 1990664 | tf_op jit(solution)/shard_map/ppermute | solution.py:572
  439.9 54.2 %collective-permute-start.26 = (bf16[512,1280]{1,0:T(8,128)(2,1)}, bf16[512,1280]{1,0:T(8,128)(2,1)S(1)}, u32[]{:S(2)}, u32[]{:S(2)}) collective-permute-start(bf16[512,1280]{1,0:T(8,128)(2,1)} %get-tuple-element.55), channel_id=1, source_target_pairs={{0,8},{4,12},{8,0},{12,4},{1,9},{5,13},{9,1},{13,5},{2,10},{6,14},... | collective-permute-start | bytes 3932168 | tf_op jit(solution)/shard_map/ppermute | solution.py:558
  487.3 48.3 %collective-permute-start.53 = (bf16[2,72,1152]{2,1,0:T(8,128)(2,1)}, bf16[2,72,1152]{2,1,0:T(8,128)(2,1)}, u32[]{:S(2)}, u32[]{:S(2)}) collective-permute-start(bf16[2,72,1152]{2,1,0:T(8,128)(2,1)} %dynamic-slice_bitcast_fusion.11), channel_id=1, source_target_pairs={{0,1},{1,0},{2,3},{3,2},{4,5},{5,4},{6,7},{7,6},{8,9},{9,8},{10,11... | collective-permute-start | bytes 995336 | tf_op jit(solution)/shard_map/ppermute | solution.py:562
  505.4 99.8 %collective-permute-start.27 = (bf16[768,1152]{1,0:T(8,128)(2,1)}, bf16[768,1152]{1,0:T(8,128)(2,1)}, u32[]{:S(2)}, u32[]{:S(2)}) collective-permute-start(bf16[768,1152]{1,0:T(8,128)(2,1)} %fusion.18), channel_id=1, source_target_pairs={{0,4},{4,0},{8,12},{12,8},{1,5},{5,1},{9,13},{13,9},{2,6},{6,2},{1... | collective-permute-start | bytes 5308424 | tf_op jit(solution)/shard_map/ppermute | solution.py:554
  554.4 49.1 %collective-permute-start.55 = (bf16[72,1152]{1,0:T(8,128)(2,1)}, bf16[72,1152]{1,0:T(8,128)(2,1)}, u32[]{:S(2)}, u32[]{:S(2)}) collective-permute-start(bf16[72,1152]{1,0:T(8,128)(2,1)} %fusion.39), channel_id=1, source_target_pairs={{0,16},{16,0},{1,17},{17,1},{2,18},{18,2},{3,19},{19,3},{4,20},{20... | collective-permute-start | bytes 497672 | tf_op jit(solution)/shard_map/ppermute | solution.py:572
  627.6 84.8 %collective-permute-start.46 = (bf16[4,2,72,1920]{3,2,1,0:T(8,128)(2,1)}, bf16[4,2,72,1920]{3,2,1,0:T(8,128)(2,1)}, u32[]{:S(2)}, u32[]{:S(2)}) collective-permute-start(bf16[4,2,72,1920]{3,2,1,0:T(8,128)(2,1)} %bitcast.292), channel_id=1, source_target_pairs={{0,8},{4,12},{8,0},{12,4},{1,9},{5,13},{9,1},{13,5},{2,10},{6,14},... | collective-permute-start | bytes 6635528 | tf_op jit(solution)/shard_map/ppermute | solution.py:558
  726.8 60.8 %collective-permute-start.62 = (bf16[4,288,1152]{2,1,0:T(8,128)(2,1)}, bf16[4,288,1152]{2,1,0:T(8,128)(2,1)}, u32[]{:S(2)}, u32[]{:S(2)}) collective-permute-start(bf16[4,288,1152]{2,1,0:T(8,128)(2,1)} %dynamic-slice_bitcast_fusion.1), channel_id=1, source_target_pairs={{0,8},{4,12},{8,0},{12,4},{1,9},{5,13},{9,1},{13,5},{2,10},{6,14},... | collective-permute-start | bytes 7962632 | tf_op jit(solution)/shard_map/ppermute | solution.py:558
  746.7 96.4 %collective-permute-start.57 = (bf16[4,72,4608]{2,1,0:T(8,128)(2,1)S(1)}, bf16[4,72,4608]{2,1,0:T(8,128)(2,1)S(1)}, u32[]{:S(2)}, u32[]{:S(2)}) collective-permute-start(bf16[4,72,4608]{2,1,0:T(8,128)(2,1)S(1)} %dynamic-slice_bitcast_fusion.2), channel_id=1, source_target_pairs={{0,8},{4,12},{8,0},{12,4},{1,9},{5,13},{9,1},{13,5},{2,10},{6,14},... | collective-permute-start | bytes 7962632 | tf_op jit(solution)/shard_map/ppermute | solution.py:558
  784.9 59.3 %collective-permute-start.50 = (bf16[72,1920]{1,0:T(8,128)(2,1)S(1)}, bf16[72,1920]{1,0:T(8,128)(2,1)S(1)}, u32[]{:S(2)}, u32[]{:S(2)}) collective-permute-start(bf16[72,1920]{1,0:T(8,128)(2,1)S(1)} %fusion.40), channel_id=1, source_target_pairs={{0,4},{4,0},{8,12},{12,8},{1,5},{5,1},{9,13},{13,9},{2,6},{6,2},{1... | collective-permute-start | bytes 829448 | tf_op jit(solution)/shard_map/ppermute | solution.py:554
  790.1 54.4 %collective-permute-start.63 = (bf16[2,288,1152]{2,1,0:T(8,128)(2,1)S(1)}, bf16[2,288,1152]{2,1,0:T(8,128)(2,1)S(1)}, u32[]{:S(2)}, u32[]{:S(2)}) collective-permute-start(bf16[2,288,1152]{2,1,0:T(8,128)(2,1)S(1)} %dynamic-slice_bitcast_fusion.3), channel_id=1, source_target_pairs={{0,1},{1,0},{2,3},{3,2},{4,5},{5,4},{6,7},{7,6},{8,9},{9,8},{10,11... | collective-permute-start | bytes 3981320 | tf_op jit(solution)/shard_map/ppermute | solution.py:562
  843.9 44.2 %collective-permute-start.58 = (bf16[2,72,4608]{2,1,0:T(8,128)(2,1)S(1)}, bf16[2,72,4608]{2,1,0:T(8,128)(2,1)S(1)}, u32[]{:S(2)}, u32[]{:S(2)}) collective-permute-start(bf16[2,72,4608]{2,1,0:T(8,128)(2,1)S(1)} %dynamic-slice_bitcast_fusion.4), channel_id=1, source_target_pairs={{0,1},{1,0},{2,3},{3,2},{4,5},{5,4},{6,7},{7,6},{8,9},{9,8},{10,11... | collective-permute-start | bytes 3981320 | tf_op jit(solution)/shard_map/ppermute | solution.py:562
  845.0 47.4 %collective-permute-start.64 = (bf16[288,1152]{1,0:T(8,128)(2,1)S(1)}, bf16[288,1152]{1,0:T(8,128)(2,1)}, u32[]{:S(2)}, u32[]{:S(2)}) collective-permute-start(bf16[288,1152]{1,0:T(8,128)(2,1)S(1)} %dynamic-slice_bitcast_fusion.7), channel_id=1, source_target_pairs={{0,2},{1,3},{2,0},{3,1},{4,6},{5,7},{6,4},{7,5},{8,10},{9,11},{10,... | collective-permute-start | bytes 1990664 | tf_op jit(solution)/shard_map/ppermute | solution.py:562
  (103 other events, 2256.2 us)

commit v2 on v1

--- a/solution.py
+++ b/solution.py
@@ -37,6 +37,10 @@
     center = values - jnp.mean(values, axis=-1, keepdims=True)
     rstd = lax.rsqrt(jnp.mean(center * center, axis=-1, keepdims=True) + EPS)
     return center * rstd, rstd
+
+
+def plus(a, b):
+    return (a.astype(f32) + b.astype(f32)).astype(bf16)
 
 
 def qkv_kernel(blk, core_ref, x_ref, mod_ref, w_ref, b_ref, other_ref, mine_ref, nt_ref, n_s):
@@ -310,9 +314,38 @@
     )(*inputs)
 
 
+def flip(index):
+    return index + 1 - 2 * (index % 2)
+
+
+def partners():
+    img, r, z = lax.axis_index("img"), lax.axis_index("row"), lax.axis_index("col")
+    return (img, flip(r), z), (img, (r + 2) % 4, z), (flip(img), r, z)
+
+
+def greet(devices):
+    barrier = pltpu.get_barrier_semaphore()
+    for device in devices:
+        pl.semaphore_signal(
+            barrier, inc=1, device_id=device, device_id_type=pl.DeviceIdType.MESH
+        )
+    pl.semaphore_wait(barrier, len(devices))
+
+
+def send(src, dst, send_sem, recv_sem, device):
+    return pltpu.make_async_remote_copy(
+        src_ref=src,
+        dst_ref=dst,
+        send_sem=send_sem,
+        recv_sem=recv_sem,
+        device_id=device,
+        device_id_type=pl.DeviceIdType.MESH,
+    )
+
+
 def middle_kernel(
     blk,
-    core_ref,
+    chunks,
     x_ref,
     cot_ref,
     am_ref,
@@ -329,9 +362,7 @@
     gmid_ref,
     dom_ref,
     doo_ref,
-    dwum_ref,
-    dwuo_ref,
-    dwd_ref,
+    sum_ref,
     dbu_ref,
     dwpm_ref,
     dwpo_ref,
@@ -343,53 +374,133 @@
     n_s,
     nt_s,
     db2_s,
+    db2t_s,
     br2_s,
     gn_s,
     db1_s,
+    mine_s,
+    other_s,
+    in1_s,
+    out2_s,
+    keep2_s,
+    in2_s,
+    out3_s,
+    keep3_s,
+    in3_s,
+    send1,
+    recv1,
+    send2,
+    recv2,
+    send3,
+    recv3,
+    done,
 ):
     step = pl.program_id(0)
     tokens, width = x_ref.shape
     blocks = tokens // blk
     part = width // 4
+    row = lax.axis_index("row")
+    x, core, y = row // 2, row % 2, lax.axis_index("img") % 2
+    to_core, to_x, to_img = partners()
 
     @pl.when(step == 0)
     def _():
+        greet((to_core, to_x, to_img))
         br1_s[...] = (
             dot(am_ref[...], wpm_ref[...], NN) + dot(ao_ref[...], wpo_ref[...], NN) + bp_ref[...]
-        )
+        ).astype(bf16)
         for i in range(blocks):
             rows = slice(i * blk, (i + 1) * blk)
-            mid = x_ref[rows].astype(f32) + mod_ref[i, 2:3] * br1_s[rows]
+            mid = x_ref[rows].astype(f32) + mod_ref[i, 2:3] * br1_s[rows].astype(f32)
             mid_s[rows] = mid
-            y, _ = norm(mid)
-            n = (y * (1.0 + mod_ref[i, 4:5]) + mod_ref[i, 3:4]).astype(bf16)
-            n_s[rows] = n
+            normed, _ = norm(mid)
+            n_s[rows] = (normed * (1.0 + mod_ref[i, 4:5]) + mod_ref[i, 3:4]).astype(bf16)
             db2_s[rows] = (mod_ref[i, 5:6] * cot_ref[rows].astype(f32)).astype(bf16)
         for g in range(4):
-            place = (g % 2 + core_ref[0] - 2 * (g % 2) * core_ref[0]) * (2 * part) + (g // 2) * part
-            nt_s[pl.ds(pl.multiple_of(place, 16), part)] = (
-                n_s[:, g * part : (g + 1) * part].astype(f32).T.astype(bf16)
-            )
+            place_row = ((g + core) % 2) * (2 * part) + (g // 2) * part
+            place_row = pl.ds(pl.multiple_of(place_row, 16), part)
+            cols = slice(g * part, (g + 1) * part)
+            nt_s[place_row] = n_s[:, cols].astype(f32).T.astype(bf16)
+            db2t_s[place_row] = db2_s[:, cols].astype(f32).T.astype(bf16)
         br2_s[...] = jnp.zeros_like(br2_s)
         gn_s[...] = jnp.zeros_like(gn_s)
 
-    pre = dot(n_s[...], wu_ref[...], NN) + bu_ref[...]
-    square = pre * pre
-    t = jnp.tanh(pre * (GELU_A + (GELU_A * GELU_B) * square))
-    hidden = (0.5 * pre * (1.0 + t)).astype(bf16)
-    slope = 0.5 * (1.0 + t) + 0.5 * pre * (1.0 - t * t) * (
-        GELU_A + (3.0 * GELU_A * GELU_B) * square
-    )
-    br2_s[...] += dot(hidden, wd_ref[...], NN)
-    gpre = dot(db2_s[...], wd_ref[...], NT) * slope
-    gp = gpre.astype(bf16)
-    gn_s[...] += dot(gp, wu_ref[...], NT)
-    dwd_ref[...] = dot(hidden, db2_s[...], TN).astype(bf16)
-    dwum_ref[...] = dot(nt_s[0 : 2 * part], gp, NN).astype(bf16)
-    dwuo_ref[...] = dot(nt_s[2 * part : 4 * part], gp, NN).astype(bf16)
-    dbu_ref[...] = jnp.sum(gpre, axis=0, keepdims=True)
-
-    @pl.when(step == pl.num_programs(0) - 1)
+    @pl.when(step < chunks)
+    def _():
+        slot = step % 2
+        pre = dot(n_s[...], wu_ref[...], NN) + bu_ref[...]
+        square = pre * pre
+        t = jnp.tanh(pre * (GELU_A + (GELU_A * GELU_B) * square))
+        hidden = (0.5 * pre * (1.0 + t)).astype(bf16)
+        slope = 0.5 * (1.0 + t) + 0.5 * pre * (1.0 - t * t) * (
+            GELU_A + (3.0 * GELU_A * GELU_B) * square
+        )
+        br2_s[...] += dot(hidden, wd_ref[...], NN)
+        gpre = dot(db2_s[...], wd_ref[...], NT) * slope
+        gp = gpre.astype(bf16)
+        gn_s[...] += dot(gp, wu_ref[...], NT)
+        dbu_ref[...] = jnp.sum(gpre, axis=0, keepdims=True)
+        for k, (left, right) in enumerate(((nt_s, gp), (db2t_s, hidden))):
+            for half, dst in enumerate((mine_s, other_s)):
+                term = dot(left[2 * part * half : 2 * part * (half + 1)], right, NN)
+                dst[slot, k] = term.reshape(dst.shape[2:]).astype(bf16)
+
+    def copy1(a):
+        return send(other_s.at[a % 2], in1_s.at[a % 2], send1.at[a % 2], recv1.at[a % 2], to_core)
+
+    def turn(a, even, odd):
+        return tuple(e + (o - e) * (a % 2) for e, o in zip(even, odd))
+
+    def copy2(a):
+        return send(
+            out2_s.at[a % 2], in2_s.at[a % 4], send2.at[a % 4], recv2.at[a % 4], turn(a, to_x, to_img)
+        )
+
+    def copy3(a):
+        return send(
+            out3_s.at[a % 2], in3_s.at[a % 4], send3.at[a % 4], recv3.at[a % 4], turn(a, to_img, to_x)
+        )
+
+    @pl.when(step >= 5)
+    def _():
+        a = step - 5
+        copy3(a).wait()
+        sum_ref[...] = plus(keep3_s[a % 2], in3_s[a % 4])
+
+    @pl.when(jnp.logical_and(step >= 3, step < chunks + 3))
+    def _():
+        a = step - 3
+        copy2(a).wait()
+        side = y + (x - y) * (a % 2)
+        out3_s[a % 2] = plus(keep2_s[a % 2, 1 - side], in2_s[a % 4, 1 - side])
+        keep3_s[a % 2] = plus(keep2_s[a % 2, side], in2_s[a % 4, side])
+        copy3(a).start()
+
+    @pl.when(jnp.logical_and(step >= 1, step < chunks + 1))
+    def _():
+        a = step - 1
+        s = a % 2
+        copy1(a).wait()
+
+        @pl.when(s == 0)
+        def _():
+            for k in range(2):
+                out2_s[s, k] = plus(mine_s[s, k, 1 - x], in1_s[s, k, 1 - x])
+                keep2_s[s, k] = plus(mine_s[s, k, x], in1_s[s, k, x])
+
+        @pl.when(s == 1)
+        def _():
+            for k in range(2):
+                out2_s[s, k] = plus(mine_s[s, 1 - y, k], in1_s[s, 1 - y, k])
+                keep2_s[s, k] = plus(mine_s[s, y, k], in1_s[s, y, k])
+
+        copy2(a).start()
+
+    @pl.when(step < chunks)
+    def _():
+        copy1(step).start()
+
+    @pl.when(step == chunks)
     def _():
         dbp = jnp.zeros((1, width), f32)
         dbd = jnp.zeros((1, width), f32)
@@ -398,81 +509,92 @@
             cot = cot_ref[rows].astype(f32)
             br2 = br2_s[rows] + bd_ref[...]
             mid = mid_s[rows]
-            out_ref[rows] = (mid + mod_ref[i, 5:6] * br2).astype(bf16)
-            y, rstd = norm(mid)
+            n_s[rows] = (mid + mod_ref[i, 5:6] * br2).astype(bf16)
+            normed, rstd = norm(mid)
             gn = gn_s[rows]
             u = gn * (1.0 + mod_ref[i, 4:5])
             gmid = cot + rstd * (
                 u
                 - jnp.mean(u, axis=-1, keepdims=True)
-                - y * jnp.mean(u * y, axis=-1, keepdims=True)
+                - normed * jnp.mean(u * normed, axis=-1, keepdims=True)
             )
-            gmid_ref[rows] = gmid.astype(bf16)
             db1 = mod_ref[i, 2:3] * gmid
             db1_s[rows] = db1.astype(bf16)
             dbp += jnp.sum(db1, axis=0, keepdims=True)
             dbd += jnp.sum(db2_s[rows].astype(f32), axis=0, keepdims=True)
-            dmod_ref[i, 0:1] = jnp.sum(gmid * br1_s[rows], axis=0, keepdims=True)
+            db2_s[rows] = gmid.astype(bf16)
+            dmod_ref[i, 0:1] = jnp.sum(gmid * br1_s[rows].astype(f32), axis=0, keepdims=True)
             dmod_ref[i, 1:2] = jnp.sum(gn, axis=0, keepdims=True)
-            dmod_ref[i, 2:3] = jnp.sum(gn * y, axis=0, keepdims=True)
+            dmod_ref[i, 2:3] = jnp.sum(gn * normed, axis=0, keepdims=True)
             dmod_ref[i, 3:4] = jnp.sum(cot * br2, axis=0, keepdims=True)
         dbp_ref[...] = dbp
         dbd_ref[...] = dbd
+        first = pltpu.make_async_copy(n_s, out_ref, done.at[0])
+        second = pltpu.make_async_copy(db2_s, gmid_ref, done.at[1])
+        first.start()
+        second.start()
         dom_ref[...] = dot(db1_s[...], wpm_ref[...], NT).astype(bf16)
         doo_ref[...] = dot(db1_s[...], wpo_ref[...], NT).astype(bf16)
         dwpm_ref[...] = dot(am_ref[...], db1_s[...], TN).astype(bf16)
         dwpo_ref[...] = dot(ao_ref[...], db1_s[...], TN).astype(bf16)
-
-
-def middle(core, x, cot, att_m, att_o, mod, wp_m, wp_o, b_proj, b_down, w_up, b_up, w_down, blk):
+        first.wait()
+        second.wait()
+
+
+def middle(x, cot, att_m, att_o, mod, wp_m, wp_o, b_proj, b_down, w_up, b_up, w_down, blk):
     tokens, width = x.shape
     pad = att_m.shape[1]
     hidden = w_up.shape[1]
     chunk = 512
-    steps = hidden // chunk
-    half = width // 2
-
-    def whole(shape):
-        return pl.BlockSpec(shape, lambda j, c: (0,) * len(shape))
+    chunks = hidden // chunk
+    n = width // 16
+    any_ref = pl.BlockSpec(memory_space=pl.ANY)
+
+    def at(j):
+        return jnp.minimum(j, chunks - 1)
 
     return pl.pallas_call(
-        functools.partial(middle_kernel, blk),
-        grid_spec=pltpu.PrefetchScalarGridSpec(
-            num_scalar_prefetch=1,
-            grid=(steps,),
-            in_specs=[VMEM] * 9
-            + [
-                pl.BlockSpec((width, chunk), lambda j, c: (0, j)),
-                pl.BlockSpec((1, chunk), lambda j, c: (0, j)),
-                pl.BlockSpec((chunk, width), lambda j, c: (j, 0)),
-            ],
-            out_specs=[VMEM] * 4
-            + [
-                pl.BlockSpec((half, chunk), lambda j, c: (0, j)),
-                pl.BlockSpec((half, chunk), lambda j, c: (0, j)),
-                pl.BlockSpec((chunk, width), lambda j, c: (j, 0)),
-                pl.BlockSpec((1, chunk), lambda j, c: (0, j)),
-            ]
-            + [VMEM] * 5,
-            scratch_shapes=[
-                pltpu.VMEM((tokens, width), f32),
-                pltpu.VMEM((tokens, width), f32),
-                pltpu.VMEM((tokens, width), bf16),
-                pltpu.VMEM((width, tokens), bf16),
-                pltpu.VMEM((tokens, width), bf16),
-                pltpu.VMEM((tokens, width), f32),
-                pltpu.VMEM((tokens, width), f32),
-                pltpu.VMEM((tokens, width), bf16),
-            ],
-        ),
+        functools.partial(middle_kernel, blk, chunks),
+        grid=(chunks + 5,),
+        in_specs=[VMEM] * 9
+        + [
+            pl.BlockSpec((width, chunk), lambda j: (0, at(j))),
+            pl.BlockSpec((1, chunk), lambda j: (0, at(j))),
+            pl.BlockSpec((chunk, width), lambda j: (at(j), 0)),
+        ],
+        out_specs=[any_ref, any_ref, VMEM, VMEM]
+        + [
+            pl.BlockSpec((4, n, chunk), lambda j: (0, 0, jnp.maximum(j - 5, 0))),
+            pl.BlockSpec((1, chunk), lambda j: (0, at(j))),
+        ]
+        + [VMEM] * 5,
+        scratch_shapes=[
+            pltpu.VMEM((tokens, width), f32),
+            pltpu.VMEM((tokens, width), bf16),
+            pltpu.VMEM((tokens, width), bf16),
+            pltpu.VMEM((width, tokens), bf16),
+            pltpu.VMEM((tokens, width), bf16),
+            pltpu.VMEM((width, tokens), bf16),
+            pltpu.VMEM((tokens, width), f32),
+            pltpu.VMEM((tokens, width), f32),
+            pltpu.VMEM((tokens, width), bf16),
+            pltpu.VMEM((2, 2, 2, 4, n, chunk), bf16),
+            pltpu.VMEM((2, 2, 2, 4, n, chunk), bf16),
+            pltpu.VMEM((2, 2, 2, 4, n, chunk), bf16),
+            pltpu.VMEM((2, 2, 4, n, chunk), bf16),
+            pltpu.VMEM((2, 2, 4, n, chunk), bf16),
+            pltpu.VMEM((4, 2, 4, n, chunk), bf16),
+            pltpu.VMEM((2, 4, n, chunk), bf16),
+            pltpu.VMEM((2, 4, n, chunk), bf16),
+            pltpu.VMEM((4, 4, n, chunk), bf16),
+        ]
+        + [pltpu.SemaphoreType.DMA((k,)) for k in (2, 2, 4, 4, 4, 4, 2)],
         out_shape=(
             shaped((tokens, width)),
             shaped((tokens, width)),
             shaped((tokens, pad)),
             shaped((tokens, pad)),
-            shaped((half, hidden)),
-            shaped((half, hidden)),
-            shaped((hidden, width)),
+            shaped((4, n, hidden)),
             shaped((1, hidden), f32),
             shaped((pad, width)),
             shaped((pad, width)),
@@ -480,14 +602,16 @@
             shaped((1, width), f32),
             shaped((1, width), f32),
         ),
-        compiler_params=pltpu.CompilerParams(vmem_limit_bytes=VMEM_LIMIT),
+        compiler_params=pltpu.CompilerParams(
+            vmem_limit_bytes=62 * 2**20, collective_id=1, has_side_effects=True
+        ),
         cost_estimate=pl.CostEstimate(
             flops=2 * tokens * width * (6 * hidden + 6 * pad),
             bytes_accessed=60 * 2**20,
             transcendentals=tokens * hidden,
         ),
         name="middle",
-    )(core, x, cot, att_m, att_o, mod, wp_m, wp_o, b_proj, b_down, w_up, b_up, w_down)
+    )(x, cot, att_m, att_o, mod, wp_m, wp_o, b_proj, b_down, w_up, b_up, w_down)
 
 
 def first_back_kernel(blk, x_ref, ga_ref, gb_ref, gmid_ref, mod_ref, out_ref, dmod_ref):
@@ -571,10 +695,6 @@
     if lax.axis_size("img") == 2:
         return v.astype(f32) + lax.ppermute(v, "img", [(0, 1), (1, 0)]).astype(f32)
     return lax.psum(v, "img").astype(f32)
-
-
-def plus(a, b):
-    return (a.astype(f32) + b.astype(f32)).astype(bf16)
 
 
 def shards(
@@ -685,9 +805,7 @@
         gmid,
         do_mine,
         do_other,
-        dwu_mine,
-        dwu_other,
-        dwd,
+        dw_sum,
         dbu,
         dwp_mine,
         dwp_other,
@@ -695,7 +813,6 @@
         dbp,
         dbd,
     ) = middle(
-        core_arr,
         inputs,
         upstream,
         att_mine,
@@ -716,21 +833,27 @@
     def reduce_plane(mine):
         got = over_x(pick(mine, 1 - x))
         mine = plus(pick(mine, x), got)
-        return reduce_col(mine)
+        return over_img(reduce_col(mine))
 
     def reduce_col(mine):
         split = mine.reshape((2, 2) + mine.shape[1:])
         got = over_col(pick(split, 1 - z % 2, 1), 1)
         mine = plus(pick(split, z % 2, 1), got)
         got = over_col(pick(mine, 1 - z // 2), 2)
-        mine = plus(pick(mine, z // 2), got)
-        return over_img(mine)
-
-    dwd_halves = dwd.reshape(2, 2, hidden // 4, width)
-    dwd_sum = plus(pick(dwd_halves, core, 1), over_core(pick(dwd_halves, 1 - core, 1)))
-    grad_w_down = reduce_plane(dwd_sum.reshape(2, 4, hidden // 16, width))
-    dwu_sum = plus(dwu_mine, over_core(dwu_other))
-    grad_w_up = reduce_plane(dwu_sum.reshape(2, 4, width // 16, hidden))
+        return plus(pick(mine, z // 2), got)
+
+    size = lax.axis_size("img")
+    side = lax.axis_index("img") % 2
+    dw = reduce_col(dw_sum)
+    step = 2
+    while step < size:
+        dw = plus(dw, lax.ppermute(dw, "img", [(i, i ^ step) for i in range(size)]))
+        step *= 2
+    dw_there = lax.ppermute(dw, "img", [(i, i ^ 1) for i in range(size)])
+    grad_w_up = jnp.where(side == 0, dw, dw_there).astype(f32)
+    dwd = jnp.where(side == 0, dw_there, dw).reshape(width // 16, 16, hidden // 16)
+    dwd = lax.all_to_all(dwd.transpose(1, 0, 2), ("row", "col"), 0, 0, tiled=True)
+    grad_w_down = dwd.reshape(width, hidden // 16).T.astype(f32)
     dwp = jnp.stack([dwp_mine, dwp_other])
     dwp = jnp.stack([pick(dwp, core), pick(dwp, 1 - core)])[:, :half]
     dwp = dwp.reshape(2, 2, half // 2, width)

time: 952 us -> 792 us (0.83)
  waiting for transfers between devices: 329 us -> 159 us
  Pallas kernels: 215 us -> 244 us
  other arithmetic: 59.1 us -> 45.2 us
    ppermute x8 -> x6, waiting for transfers between devices: 97.8 us -> 36.4 us  [over_x(): return lax.ppermute(v, 'row', [(r, r ^ 2) for r in range(4)])]
    ppermute x14 -> x12, waiting for transfers between devices: 108 us -> 51.1 us  [over_col(): return lax.ppermute(v, 'col', [(i, i ^ far) for i in range(4)])]
    pallas_call x1, Pallas kernels: 84.1 us -> 130 us  [middle(): pl.pallas_call(functools.partial(middle_kernel, blk, chunks), grid=(chunk...]
    ppermute x28, waiting for transfers between devices: 99.2 us -> 64.4 us  [over_plane(): return lax.ppermute(v, ('row', 'col'), swap)]
    pallas_call x2, Pallas kernels: 48.3 us -> 32 us  [attend(): pl.pallas_call(functools.partial(attend_kernel, heads, hd, count, far is...]
    ppermute x7 -> x5, waiting for transfers between devices: 23.5 us -> 7.4 us  [over_img(): return v.astype(f32) + lax.ppermute(v, 'img', [(0, 1), (1, 0)]).astype(f32)]
    convert_element_type x20 -> x14, other arithmetic: 26 us -> 11.9 us  [plus(): return (a.astype(f32) + b.astype(f32)).astype(bf16)]
    ppermute x14 -> x12, starting transfers between devices: 28.5 us -> 21.5 us  [over_col(): return lax.ppermute(v, 'col', [(i, i ^ far) for i in range(4)])]
  transfers between devices with their start and end apart: 69 -> 63, of which waited for: 24 -> 17; matrix products, arithmetic and copies ran while one was open for 26% -> 28% of each run, Pallas kernels for 21% -> 29%
where the time goes in v2:
time: 792 us; the launch traced here: 777 us
  Pallas kernels  244 us (31%)
  waiting for transfers between devices  159 us (20%)
  local copies, waits for them, and re-layouts  134 us (17%)
  starting transfers between devices  96.5 us (12%)
  matrix products  53.4 us (7%)
  other arithmetic  45.2 us (6%)
  blocking collectives  41.2 us (5%)
    pallas_call x1, Pallas kernels, middle(): pl.pallas_call(functools.partial(middle_kernel, blk, chunks), grid=(chunk...  130 us
    ppermute x28, waiting for transfers between devices, over_plane(): return lax.ppermute(v, ('row', 'col'), swap)  64.4 us
    unnamed x172, local copies, waits for them, and re-layouts  62.4 us
    ppermute x12, waiting for transfers between devices, over_col(): return lax.ppermute(v, 'col', [(i, i ^ far) for i in range(4)])  51.1 us
    ppermute x28, starting transfers between devices, over_plane(): return lax.ppermute(v, ('row', 'col'), swap)  50.6 us
    dot_general x8, matrix products, dot(): return lax.dot_general(left, right, dims, preferred_element_type=f32)  45.7 us
    pallas_call x2, Pallas kernels, attend_back(): pl.pallas_call(functools.partial(attend_back_kernel, heads, hd, count, fa...  42.6 us
    psum x1, blocking collectives, shards(): small = lax.psum(small, ('row', 'col', 'img'))  41.2 us
  transfers between devices with their start and end apart: 63, of which 17 were waited for; matrix products, arithmetic and copies ran while one was open for 28% of the time, Pallas kernels for 29%

profile of v2, /device:TPU:0, one launch (start us, length us, event | category | flops | bytes accessed | tf_op | source)
XLA Modules:
  0.0 777.1 jit_solution(2456927994585663937)
XLA Ops:
  28.5 11.4 %copy.47 = bf16[1152,3456]{0,1:T(8,128)(2,1)} copy(bf16[1152,3456]{1,0:T(8,128)(2,1)} %param.17) | data formatting | bytes 15925248 | tf_op args[3]
  55.2 12.6 %copy.49.w_ref = bf16[2,1152,1920]{2,1,0:T(8,128)(2,1)} copy(bf16[2,1152,1920]{1,2,0:T(8,128)(2,1)} %bitcast.275) | data formatting | bytes 17694720 | tf_op jit(solution)/shard_map/reshape | solution.py:785
  76.6 10.3 %collective-permute-done.7 = bf16[2,64,1152]{2,1,0:T(8,128)(2,1)S(1)} collective-permute-done((bf16[2,64,1152]{2,1,0:T(8,128)(2,1)}, bf16[2,64,1152]{2,1,0:T(8,128)(2,1)S(1)}, u32[]{:S(2)}, u32[]{:S(2)}) %collective-permute-start.7) | collective-permute-done | bytes 294944 | tf_op jit(solution)/shard_map/ppermute | solution.py:691
  88.7 12.7 %collective-permute-done.8 = bf16[2,64,1152]{2,1,0:T(8,128)(2,1)S(1)} collective-permute-done((bf16[2,64,1152]{2,1,0:T(8,128)(2,1)S(1)}, bf16[2,64,1152]{2,1,0:T(8,128)(2,1)S(1)}, u32[]{:S(2)}, u32[]{:S(2)}) %collective-permute-start.8) | collective-permute-done | bytes 294944 | tf_op jit(solution)/shard_map/ppermute | solution.py:691
  103.8 8.4 %collective-permute-done.9 = bf16[2,64,1152]{2,1,0:T(8,128)(2,1)S(1)} collective-permute-done((bf16[2,64,1152]{2,1,0:T(8,128)(2,1)S(1)}, bf16[2,64,1152]{2,1,0:T(8,128)(2,1)S(1)}, u32[]{:S(2)}, u32[]{:S(2)}) %collective-permute-start.9) | collective-permute-done | bytes 294944 | tf_op jit(solution)/shard_map/ppermute | solution.py:691
  124.5 8.2 %collective-permute-done.12 = bf16[64,1152]{1,0:T(8,128)(2,1)S(1)} collective-permute-done((bf16[64,1152]{1,0:T(8,128)(2,1)}, bf16[64,1152]{1,0:T(8,128)(2,1)S(1)}, u32[]{:S(2)}, u32[]{:S(2)}) %collective-permute-start.12) | collective-permute-done | bytes 147488 | tf_op jit(solution)/shard_map/ppermute | solution.py:691
  138.9 16.5 %qkv.1 = (bf16[768,1920]{1,0:T(8,128)(2,1)}, bf16[768,1920]{1,0:T(8,128)(2,1)}, bf16[1152,768]{1,0:T(8,128)(2,1)}) custom-call(s32[1]{0:T(128)} %bitcast.40.core_ref, bf16[768,1152]{1,0:T(8,128)(2,1)} %copy-done.3, f32[6,6,1152]{2,1,0:T(8,128)} %reshape.281.mod_ref, bf16[2,1152,1920]{2,1,0:T(8,128)(2,1)} %copy.49.w_ref, f32[2,1,1920]{2,1,0:T(1,128)} %copy.50.b_ref), custom_call_target="tpu_custom_call" | custom-call | flops 6794772480 | bytes 20971520 | tf_op jit(solution)/shard_map/qkv/pallas_call | solution.py:77
  167.5 21.8 %attend_near.1 = (bf16[512,640]{1,0:T(8,128)(2,1)}, bf16[512,640]{1,0:T(8,128)(2,1)}, f32[1024,128]{1,0:T(8,128)}) custom-call(s32[1]{0:T(128)} %bitcast.39.flag_ref, bf16[768,1920]{1,0:T(8,128)(2,1)} %get-tuple-element.40.mine_ref, bf16[768,1920]{1,0:T(8,128)(2,1)} %collective-permute-done.14.sib_ref), custom_call_target="tpu_custom_call" | custom-call | flops 4294967296 | bytes 8388608 | tf_op jit(solution)/shard_map/attend_near/pallas_call | solution.py:169
  195.3 10.2 %attend_far.1 = (bf16[256,640]{1,0:T(8,128)(2,1)}, bf16[256,640]{1,0:T(8,128)(2,1)}, f32[512,128]{1,0:T(8,128)}) custom-call(s32[1]{0:T(128)} %bitcast.52.flag_ref, bf16[768,1920]{1,0:T(8,128)(2,1)} %get-tuple-element.40.mine_ref, bf16[768,1920]{1,0:T(8,128)(2,1)} %collective-permute-done.14.sib_ref, bf16[512,1280]{1,0:T(8,128)(2,1)} %collective-permute-done.15.rest_0_.rest_5_), custom_call_target="tpu_custom_call" | custom-call | flops 2147483648 | bytes 8388608 | tf_op jit(solution)/shard_map/attend_far/pallas_call | solution.py:169
  209.3 130.4 %middle.1 = (bf16[768,1152]{1,0:T(8,128)(2,1)}, bf16[768,1152]{1,0:T(8,128)(2,1)}, bf16[768,640]{1,0:T(8,128)(2,1)}, bf16[768,640]{1,0:T(8,128)(2,1)}, bf16[4,72...) custom-call(bf16[768,1152]{1,0:T(8,128)(2,1)} %copy-done.3, ...), custom_call_target="tpu_custom_call" | custom-call | flops 55717134336 | bytes 62914560 | tf_op jit(solution)/shard_map/middle/pallas_call | solution.py:556
  368.8 10.0 %collective-permute-done.18 = bf16[2,64,1152]{2,1,0:T(8,128)(2,1)S(1)} collective-permute-done((bf16[2,64,1152]{2,1,0:T(8,128)(2,1)}, bf16[2,64,1152]{2,1,0:T(8,128)(2,1)S(1)}, u32[]{:S(2)}, u32[]{:S(2)}) %collective-permute-start.18) | collective-permute-done | bytes 294944 | tf_op jit(solution)/shard_map/ppermute | solution.py:691
  416.3 8.5 %collective-permute-start.56 = (bf16[2,72,4608]{2,1,0:T(8,128)(2,1)}, bf16[2,72,4608]{2,1,0:T(8,128)(2,1)}, u32[]{:S(2)}, u32[]{:S(2)}) collective-permute-start(bf16[2,72,4608]{2,1,0:T(8,128)(2,1)} %dynamic-slice_bitcast_fusion), channel_id=1, source_target_pairs={{0,1},{1,0},{2,3},{3,2},{4,5},{5,4},{6,7},{7,6},{8,9},{9,8},{10,11... | collective-permute-start | bytes 3981320 | tf_op jit(solution)/shard_map/ppermute | solution.py:686
  438.4 12.5 %attend_far_back.1 = (bf16[256,1920]{1,0:T(8,128)(2,1)}, bf16[256,1920]{1,0:T(8,128)(2,1)}, bf16[512,1280]{1,0:T(8,128)(2,1)}) custom-call(s32[1]{0:T(128)} %bitcast.52.flag_ref, bf16[768,1920]{1,0:T(8,128)(2,1)} %get-tuple-element.40.mine_ref, bf16[768,1920]{1,0:T(8,128)(2,1)} %collective-permute-done.14.sib_ref, bf16[256,640]{1,0:T(8,128)(2,1)} %slice.378.rest_0_, ...), custom_call_target="tpu_custom_call" | custom-call | flops 5368709120 | bytes 12582912 | tf_op jit(solution)/shard_map/attend_far_back/pallas_call | solution.py:288
  451.8 30.1 %attend_near_back.1 = (bf16[512,1920]{1,0:T(8,128)(2,1)}, bf16[512,1920]{1,0:T(8,128)(2,1)}) custom-call(s32[1]{0:T(128)} %bitcast.39.flag_ref, bf16[768,1920]{1,0:T(8,128)(2,1)} %get-tuple-element.40.mine_ref, bf16[768,1920]{1,0:T(8,128)(2,1)} %collective-permute-done.14.sib_ref, bf16[768,640]{1,0:T(8,128)(2,1)} %get-tuple-element.47.rest_0_, ...), custom_call_target="tpu_custom_call" | custom-call | flops 10737418240 | bytes 12582912 | tf_op jit(solution)/shard_map/attend_near_back/pallas_call | solution.py:288
  492.4 21.7 %collective-permute-done.57 = bf16[72,4608]{1,0:T(8,128)(2,1)S(1)} collective-permute-done((bf16[72,4608]{1,0:T(8,128)(2,1)S(1)}, bf16[72,4608]{1,0:T(8,128)(2,1)S(1)}, u32[]{:S(2)}, u32[]{:S(2)}) %collective-permute-start.57) | collective-permute-done | bytes 663584 | tf_op jit(solution)/shard_map/ppermute | solution.py:686
  518.0 8.5 %fusion.15 = bf16[768,1152]{1,0:T(8,128)(2,1)} fusion(bf16[2,1152,1920]{1,2,0:T(8,128)(2,1)S(1)} %bitcast.279, s32[]{:T(128)S(6)} %select_n.273, bf16[256,1280]{1,0:T(8,128)(2,1)S(1)} %get-tuple-element.156, bf16[256,640]{1,0:T(8,128)(2,1)S(1)} %slice.383, bf16[512,1920]{1,0:T(8,128)(2,1)S(1)} %copy-done.6), kind=kOutput, calls=%fused_computation.22 | convolution fusion | flops 3407118336 | bytes 9142276 | tf_op jit(solution)/shard_map/dot_general | solution.py:29
  528.8 8.5 %fusion.12.ga_ref = bf16[768,1152]{1,0:T(8,128)(2,1)} fusion(bf16[2,1152,1920]{1,2,0:T(8,128)(2,1)} %bitcast.276, s32[]{:T(128)S(6)} %select_n.273, bf16[256,1280]{1,0:T(8,128)(2,1)S(1)} %get-tuple-element.157, bf16[256,640]{1,0:T(8,128)(2,1)} %copy-done.15, bf16[512,1920]{1,0:T(8,128)(2,1)} %get-tuple-element.50), kind=kOutput, calls=%fused_computation.21 | convolution fusion | flops 3407118336 | bytes 9142276 | tf_op jit(solution)/shard_map/dot_general | solution.py:29
  542.9 9.6 %fusion.2 = bf16[1152,1920]{1,0:T(8,128)(2,1)S(1)} fusion(f32[1152,1920]{1,0:T(8,128)S(1)} %fusion.71, bf16[1152,768]{1,0:T(8,128)(2,1)} %get-tuple-element.60, bf16[256,1280]{1,0:T(8,128)(2,1)S(1)} %get-tuple-element.157, bf16[256,640]{1,0:T(8,128)(2,1)S(1)} %copy-done.16, bf16[512,1920]{1,0:T(8,128)(2,1)S(1)} %copy-done.5), kind=kOutput, calls=%fused_computation.6 | convolution fusion | flops 3410657280 | bytes 17989632 | tf_op jit(solution)/shard_map/dot_general | solution.py:29
  569.6 8.4 %all-to-all-start = ((bf16[16,72,288]{2,1,0:T(8,128)(2,1)}), bf16[16,72,288]{2,1,0:T(8,128)(2,1)S(1)}, u32[]{:S(2)}, u32[]{:S(2)}) async-start(bf16[16,72,288]{2,1,0:T(8,128)(2,1)} %bitcast.273), calls=%async_computation | async-start | bytes 1769472 | tf_op jit(solution)/shard_map/all_to_all | solution.py:855
  581.8 41.2 %psum.7 = f32[9216]{0:T(1024)S(1)} all-reduce(f32[9216]{0:T(1024)S(1)} %constant_dynamic-update-slice_fusion.9), channel_id=1, replica_groups=mesh['img'=2,'row'=4,'col'=4] {'row','col','img'}, use_global_device_ids=true, to_apply=%region_4.5 | all-reduce | flops 9216 | bytes 73728 | tf_op jit(solution)/shard_map/psum | solution.py:932
  650.3 27.9 %collective-permute-done.36 = bf16[12,2304]{1,0:T(8,128)(2,1)S(1)} collective-permute-done((bf16[12,2304]{1,0:T(8,128)(2,1)S(1)}, bf16[12,2304]{1,0:T(8,128)(2,1)S(1)}, u32[]{:S(2)}, u32[]{:S(2)}) %collective-permute-start.36) | collective-permute-done | bytes 55328 | tf_op jit(solution)/shard_map/ppermute | solution.py:682
  684.9 8.1 %collective-permute-done.38 = bf16[12,2304]{1,0:T(8,128)(2,1)S(1)} collective-permute-done((bf16[12,2304]{1,0:T(8,128)(2,1)S(1)}, bf16[12,2304]{1,0:T(8,128)(2,1)S(1)}, u32[]{:S(2)}, u32[]{:S(2)}) %collective-permute-start.38) | collective-permute-done | bytes 55328 | tf_op jit(solution)/shard_map/ppermute | solution.py:686
  727.4 17.5 %collective-permute-done.47 = bf16[2,2,72,1920]{3,2,1,0:T(8,128)(2,1)S(1)} collective-permute-done((bf16[2,2,72,1920]{3,2,1,0:T(8,128)(2,1)S(1)}, bf16[2,2,72,1920]{3,2,1,0:T(8,128)(2,1)S(1)}, u32[]{:S(2)}, u32[]{:S(2)}) %collective-permute-start.47) | collective-permute-done | bytes 1105952 | tf_op jit(solution)/shard_map/ppermute | solution.py:686
  749.5 8.4 %place.3 = f32[12,64,1152]{2,1,0:T(8,128)} custom-call(s32[12]{0:T(128)} %compare_select_fusion.1.order_ref, bf16[12,64,1152]{2,1,0:T(8,128)(2,1)} %slice_dynamic-update-slice_fusion.in_ref), custom_call_target="tpu_custom_call" | custom-call | bytes 5308416 | tf_op jit(solution)/shard_map/place/pallas_call | solution.py:657
  (427 shorter events, 310.2 us)
Async XLA Ops:
  3.8 65.7 %collective-permute-start = (bf16[2,64,1152]{2,1,0:T(8,128)(2,1)}, bf16[2,64,1152]{2,1,0:T(8,128)(2,1)S(1)}, u32[]{:S(2)}, u32[]{:S(2)}) collective-permute-start(bf16[2,64,1152]{2,1,0:T(8,128)(2,1)} %pad_maximum_fusion.7), channel_id=1, source_target_pairs={{0,1},{1,0},{2,3},{3,2},{4,5},{5,4},{6,7},{7,6},{8,9},{9,8},{10,11... | collective-permute-start | bytes 884744 | tf_op jit(solution)/shard_map/ppermute | solution.py:691
  7.6 66.5 %collective-permute-start.1 = (bf16[2,64,1152]{2,1,0:T(8,128)(2,1)}, bf16[2,64,1152]{2,1,0:T(8,128)(2,1)}, u32[]{:S(2)}, u32[]{:S(2)}) collective-permute-start(bf16[2,64,1152]{2,1,0:T(8,128)(2,1)} %pad_maximum_fusion.8), channel_id=1, source_target_pairs={{0,2},{1,3},{2,0},{3,1},{4,6},{5,7},{6,4},{7,5},{8,10},{9,11},{10,... | collective-permute-start | bytes 884744 | tf_op jit(solution)/shard_map/ppermute | solution.py:691
  10.9 64.2 %collective-permute-start.2 = (bf16[2,64,1152]{2,1,0:T(8,128)(2,1)}, bf16[2,64,1152]{2,1,0:T(8,128)(2,1)}, u32[]{:S(2)}, u32[]{:S(2)}) collective-permute-start(bf16[2,64,1152]{2,1,0:T(8,128)(2,1)} %pad_maximum_fusion.9), channel_id=1, source_target_pairs={{0,3},{1,2},{2,1},{3,0},{4,7},{5,6},{6,5},{7,4},{8,11},{9,10},{10,... | collective-permute-start | bytes 884744 | tf_op jit(solution)/shard_map/ppermute | solution.py:691
  10.9 104.7 %collective-permute-start.3 = (bf16[64,1152]{1,0:T(8,128)(2,1)}, bf16[64,1152]{1,0:T(8,128)(2,1)}, u32[]{:S(2)}, u32[]{:S(2)}) collective-permute-start(bf16[64,1152]{1,0:T(8,128)(2,1)} %get-tuple-element.147), channel_id=1, source_target_pairs={{0,8},{1,9},{2,10},{3,11},{4,12},{5,13},{6,14},{7,15},{8,0},{9,1},... | collective-permute-start | bytes 442376 | tf_op jit(solution)/shard_map/ppermute | solution.py:691
  12.6 106.2 %collective-permute-start.4 = (bf16[64,1152]{1,0:T(8,128)(2,1)}, bf16[64,1152]{1,0:T(8,128)(2,1)S(1)}, u32[]{:S(2)}, u32[]{:S(2)}) collective-permute-start(bf16[64,1152]{1,0:T(8,128)(2,1)} %get-tuple-element.146), channel_id=1, source_target_pairs={{0,9},{1,8},{2,11},{3,10},{4,13},{5,12},{6,15},{7,14},{8,1},{9,0},... | collective-permute-start | bytes 442376 | tf_op jit(solution)/shard_map/ppermute | solution.py:691
  69.5 50.6 %collective-permute-start.5 = (bf16[64,1152]{1,0:T(8,128)(2,1)}, bf16[64,1152]{1,0:T(8,128)(2,1)S(1)}, u32[]{:S(2)}, u32[]{:S(2)}) collective-permute-start(bf16[64,1152]{1,0:T(8,128)(2,1)} %get-tuple-element.145), channel_id=1, source_target_pairs={{0,10},{1,11},{2,8},{3,9},{4,14},{5,15},{6,12},{7,13},{8,2},{9,3},... | collective-permute-start | bytes 442376 | tf_op jit(solution)/shard_map/ppermute | solution.py:691
  74.0 49.1 %collective-permute-start.6 = (bf16[64,1152]{1,0:T(8,128)(2,1)}, bf16[64,1152]{1,0:T(8,128)(2,1)S(1)}, u32[]{:S(2)}, u32[]{:S(2)}) collective-permute-start(bf16[64,1152]{1,0:T(8,128)(2,1)} %get-tuple-element.144), channel_id=1, source_target_pairs={{0,11},{1,10},{2,9},{3,8},{4,15},{5,14},{6,13},{7,12},{8,3},{9,2},... | collective-permute-start | bytes 442376 | tf_op jit(solution)/shard_map/ppermute | solution.py:691
  162.6 374.7 %collective-permute-start.45 = (bf16[1152,768]{1,0:T(8,128)(2,1)}, bf16[1152,768]{1,0:T(8,128)(2,1)}, u32[]{:S(2)}, u32[]{:S(2)}) collective-permute-start(bf16[1152,768]{1,0:T(8,128)(2,1)} %get-tuple-element.60), channel_id=1, source_target_pairs={{0,4},{4,0},{8,12},{12,8},{1,5},{5,1},{9,13},{13,9},{2,6},{6,2},{1... | collective-permute-start | bytes 5308424 | tf_op jit(solution)/shard_map/ppermute | solution.py:678
  164.4 30.9 %collective-permute-start.15 = (bf16[512,1280]{1,0:T(8,128)(2,1)S(1)}, bf16[512,1280]{1,0:T(8,128)(2,1)}, u32[]{:S(2)}, u32[]{:S(2)}) collective-permute-start(bf16[512,1280]{1,0:T(8,128)(2,1)S(1)} %pad_maximum_fusion.2), channel_id=1, source_target_pairs={{0,8},{4,12},{8,0},{12,4},{1,9},{5,13},{9,1},{13,5},{2,10},{6,14},... | collective-permute-start | bytes 3932168 | tf_op jit(solution)/shard_map/ppermute | solution.py:682
  345.1 91.6 %collective-permute-start.25 = (bf16[768,640]{1,0:T(8,128)(2,1)}, bf16[768,640]{1,0:T(8,128)(2,1)}, u32[]{:S(2)}, u32[]{:S(2)}) collective-permute-start(bf16[768,640]{1,0:T(8,128)(2,1)} %get-tuple-element.48), channel_id=1, source_target_pairs={{0,4},{4,0},{8,12},{12,8},{1,5},{5,1},{9,13},{13,9},{2,6},{6,2},{1... | collective-permute-start | bytes 2949128 | tf_op jit(solution)/shard_map/ppermute | solution.py:678
  352.3 33.6 %collective-permute-start.20 = (bf16[2,64,1152]{2,1,0:T(8,128)(2,1)}, bf16[2,64,1152]{2,1,0:T(8,128)(2,1)}, u32[]{:S(2)}, u32[]{:S(2)}) collective-permute-start(bf16[2,64,1152]{2,1,0:T(8,128)(2,1)} %pad_maximum_fusion.15), channel_id=1, source_target_pairs={{0,3},{1,2},{2,1},{3,0},{4,7},{5,6},{6,5},{7,4},{8,11},{9,10},{10,... | collective-permute-start | bytes 884744 | tf_op jit(solution)/shard_map/ppermute | solution.py:691
  416.3 70.2 %collective-permute-start.56 = (bf16[2,72,4608]{2,1,0:T(8,128)(2,1)}, bf16[2,72,4608]{2,1,0:T(8,128)(2,1)}, u32[]{:S(2)}, u32[]{:S(2)}) collective-permute-start(bf16[2,72,4608]{2,1,0:T(8,128)(2,1)} %dynamic-slice_bitcast_fusion), channel_id=1, source_target_pairs={{0,1},{1,0},{2,3},{3,2},{4,5},{5,4},{6,7},{7,6},{8,9},{9,8},{10,11... | collective-permute-start | bytes 3981320 | tf_op jit(solution)/shard_map/ppermute | solution.py:686
  424.8 64.6 %collective-permute-start.51 = (bf16[2,288,1152]{2,1,0:T(8,128)(2,1)}, bf16[2,288,1152]{2,1,0:T(8,128)(2,1)}, u32[]{:S(2)}, u32[]{:S(2)}) collective-permute-start(bf16[2,288,1152]{2,1,0:T(8,128)(2,1)} %dynamic-slice_bitcast_fusion.1), channel_id=1, source_target_pairs={{0,4},{4,0},{8,12},{12,8},{1,5},{5,1},{9,13},{13,9},{2,6},{6,2},{1... | collective-permute-start | bytes 3981320 | tf_op jit(solution)/shard_map/ppermute | solution.py:678
  427.1 57.0 %collective-permute-start.60 = (bf16[72,4608]{1,0:T(8,128)(2,1)S(1)}, bf16[72,4608]{1,0:T(8,128)(2,1)}, u32[]{:S(2)}, u32[]{:S(2)}) collective-permute-start(bf16[72,4608]{1,0:T(8,128)(2,1)S(1)} %convolution_convert_fusion), channel_id=1, source_target_pairs={{0,16},{16,0},{1,17},{17,1},{2,18},{18,2},{3,19},{19,3},{4,20},{20... | collective-permute-start | bytes 1990664 | tf_op jit(solution)/shard_map/ppermute | solution.py:696
  450.9 65.2 %collective-permute-start.26 = (bf16[512,1280]{1,0:T(8,128)(2,1)}, bf16[512,1280]{1,0:T(8,128)(2,1)}, u32[]{:S(2)}, u32[]{:S(2)}) collective-permute-start(bf16[512,1280]{1,0:T(8,128)(2,1)} %get-tuple-element.53), channel_id=1, source_target_pairs={{0,8},{4,12},{8,0},{12,4},{1,9},{5,13},{9,1},{13,5},{2,10},{6,14},... | collective-permute-start | bytes 3932168 | tf_op jit(solution)/shard_map/ppermute | solution.py:682
  514.2 49.4 %collective-permute-start.58 = (bf16[72,4608]{1,0:T(8,128)(2,1)S(1)}, bf16[72,4608]{1,0:T(8,128)(2,1)}, u32[]{:S(2)}, u32[]{:S(2)}) collective-permute-start(bf16[72,4608]{1,0:T(8,128)(2,1)S(1)} %fusion.28), channel_id=1, source_target_pairs={{0,16},{16,0},{1,17},{17,1},{2,18},{18,2},{3,19},{19,3},{4,20},{20... | collective-permute-start | bytes 1990664 | tf_op jit(solution)/shard_map/ppermute | solution.py:852
  516.1 42.0 %collective-permute-start.53 = (bf16[2,72,1152]{2,1,0:T(8,128)(2,1)}, bf16[2,72,1152]{2,1,0:T(8,128)(2,1)}, u32[]{:S(2)}, u32[]{:S(2)}) collective-permute-start(bf16[2,72,1152]{2,1,0:T(8,128)(2,1)} %dynamic-slice_bitcast_fusion.6), channel_id=1, source_target_pairs={{0,1},{1,0},{2,3},{3,2},{4,5},{5,4},{6,7},{7,6},{8,9},{9,8},{10,11... | collective-permute-start | bytes 995336 | tf_op jit(solution)/shard_map/ppermute | solution.py:686
  526.5 109.8 %collective-permute-start.27 = (bf16[768,1152]{1,0:T(8,128)(2,1)}, bf16[768,1152]{1,0:T(8,128)(2,1)}, u32[]{:S(2)}, u32[]{:S(2)}) collective-permute-start(bf16[768,1152]{1,0:T(8,128)(2,1)} %fusion.15), channel_id=1, source_target_pairs={{0,4},{4,0},{8,12},{12,8},{1,5},{5,1},{9,13},{13,9},{2,6},{6,2},{1... | collective-permute-start | bytes 5308424 | tf_op jit(solution)/shard_map/ppermute | solution.py:678
  569.6 62.2 %all-to-all-start = ((bf16[16,72,288]{2,1,0:T(8,128)(2,1)}), bf16[16,72,288]{2,1,0:T(8,128)(2,1)S(1)}, u32[]{:S(2)}, u32[]{:S(2)}) async-start(bf16[16,72,288]{2,1,0:T(8,128)(2,1)} %bitcast.273), calls=%async_computation | async-start | bytes 1769472 | tf_op jit(solution)/shard_map/all_to_all | solution.py:855
  579.8 50.4 %collective-permute-start.55 = (bf16[72,1152]{1,0:T(8,128)(2,1)}, bf16[72,1152]{1,0:T(8,128)(2,1)S(1)}, u32[]{:S(2)}, u32[]{:S(2)}) collective-permute-start(bf16[72,1152]{1,0:T(8,128)(2,1)} %fusion.34), channel_id=1, source_target_pairs={{0,16},{16,0},{1,17},{17,1},{2,18},{18,2},{3,19},{19,3},{4,20},{20... | collective-permute-start | bytes 497672 | tf_op jit(solution)/shard_map/ppermute | solution.py:696
  627.4 91.9 %collective-permute-start.46 = (bf16[4,2,72,1920]{3,2,1,0:T(8,128)(2,1)}, bf16[4,2,72,1920]{3,2,1,0:T(8,128)(2,1)}, u32[]{:S(2)}, u32[]{:S(2)}) collective-permute-start(bf16[4,2,72,1920]{3,2,1,0:T(8,128)(2,1)} %bitcast.272), channel_id=1, source_target_pairs={{0,8},{4,12},{8,0},{12,4},{1,9},{5,13},{9,1},{13,5},{2,10},{6,14},... | collective-permute-start | bytes 6635528 | tf_op jit(solution)/shard_map/ppermute | solution.py:682
  647.9 64.6 %collective-permute-start.30 = (bf16[2,64,1152]{2,1,0:T(8,128)(2,1)}, bf16[2,64,1152]{2,1,0:T(8,128)(2,1)S(1)}, u32[]{:S(2)}, u32[]{:S(2)}) collective-permute-start(bf16[2,64,1152]{2,1,0:T(8,128)(2,1)} %pad_maximum_fusion.18), channel_id=1, source_target_pairs={{0,3},{1,2},{2,1},{3,0},{4,7},{5,6},{6,5},{7,4},{8,11},{9,10},{10,... | collective-permute-start | bytes 884744 | tf_op jit(solution)/shard_map/ppermute | solution.py:691
  649.5 28.8 %collective-permute-start.36 = (bf16[12,2304]{1,0:T(8,128)(2,1)S(1)}, bf16[12,2304]{1,0:T(8,128)(2,1)S(1)}, u32[]{:S(2)}, u32[]{:S(2)}) collective-permute-start(bf16[12,2304]{1,0:T(8,128)(2,1)S(1)} %add_convert_fusion.5), channel_id=1, source_target_pairs={{0,8},{4,12},{8,0},{12,4},{1,9},{5,13},{9,1},{13,5},{2,10},{6,14},... | collective-permute-start | bytes 165896 | tf_op jit(solution)/shard_map/ppermute | solution.py:682
  717.4 46.6 %collective-permute-start.59 = (bf16[72,2304]{1,0:T(8,128)(2,1)S(1)}, bf16[72,2304]{1,0:T(8,128)(2,1)S(1)}, u32[]{:S(2)}, u32[]{:S(2)}) collective-permute-start(bf16[72,2304]{1,0:T(8,128)(2,1)S(1)} %convolution_convert_fusion.1), channel_id=1, source_target_pairs={{0,16},{16,0},{1,17},{17,1},{2,18},{18,2},{3,19},{19,3},{4,20},{20... | collective-permute-start | bytes 995336 | tf_op jit(solution)/shard_map/ppermute | solution.py:696
  (99 other events, 2000.7 us)

commit v3 on v2

--- a/solution.py
+++ b/solution.py
@@ -43,62 +43,65 @@
     return (a.astype(f32) + b.astype(f32)).astype(bf16)
 
 
-def qkv_kernel(blk, core_ref, x_ref, mod_ref, w_ref, b_ref, other_ref, mine_ref, nt_ref, n_s):
-    half, step = pl.program_id(0), pl.program_id(1)
-    rows = x_ref.shape[0]
-
-    @pl.when(half == 0)
-    def _():
-        parts = []
-        for i in range(rows // blk):
-            y, _ = norm(x_ref[i * blk : (i + 1) * blk].astype(f32))
-            parts.append((y * (1.0 + mod_ref[i, 1:2]) + mod_ref[i, 0:1]).astype(bf16))
-        normed = jnp.concatenate(parts, axis=0)
-        n_s[step] = normed
-        nt_ref[...] = normed.T
-
-    result = (dot(n_s[step], w_ref[0], NN) + b_ref[0]).astype(bf16)
-
-    @pl.when(half == 0)
-    def _():
-        other_ref[...] = result
-
-    @pl.when(half == 1)
-    def _():
-        mine_ref[...] = result
-
-
-def qkv(core, x, mod, w_half, b_half, blk):
-    tokens, width = x.shape
-    wide = w_half.shape[2]
-    steps = 3
-    rows = tokens // steps
-    last = steps - 1
-    return pl.pallas_call(
-        functools.partial(qkv_kernel, blk),
-        grid_spec=pltpu.PrefetchScalarGridSpec(
-            num_scalar_prefetch=1,
-            grid=(2, steps),
-            in_specs=[
-                pl.BlockSpec((rows, width), lambda h, s, c: (s, 0)),
-                pl.BlockSpec((rows // blk, 6, width), lambda h, s, c: (s, 0, 0)),
-                pl.BlockSpec((1, width, wide), lambda h, s, c: (1 - c[0] + h * (2 * c[0] - 1), 0, 0)),
-                pl.BlockSpec((1, 1, wide), lambda h, s, c: (1 - c[0] + h * (2 * c[0] - 1), 0, 0)),
-            ],
-            out_specs=[
-                pl.BlockSpec((rows, wide), lambda h, s, c: (jnp.where(h == 0, s, last), 0)),
-                pl.BlockSpec((rows, wide), lambda h, s, c: (jnp.where(h == 0, 0, s), 0)),
-                pl.BlockSpec((width, rows), lambda h, s, c: (0, jnp.where(h == 0, s, last))),
-            ],
-            scratch_shapes=[pltpu.VMEM((steps, rows, width), bf16)],
-        ),
-        out_shape=(shaped((tokens, wide)), shaped((tokens, wide)), shaped((width, tokens))),
-        compiler_params=pltpu.CompilerParams(vmem_limit_bytes=VMEM_LIMIT),
-        cost_estimate=pl.CostEstimate(
-            flops=4 * tokens * width * wide, bytes_accessed=20 * 2**20, transcendentals=tokens
-        ),
-        name="qkv",
-    )(core, x, mod, w_half, b_half)
+def flip(index):
+    return index + 1 - 2 * (index % 2)
+
+
+def partners():
+    img, r, z = lax.axis_index("img"), lax.axis_index("row"), lax.axis_index("col")
+    return (img, flip(r), z), (img, (r + 2) % 4, z), (flip(img), r, z)
+
+
+def plane_device(dx, dz):
+    img, r, z = lax.axis_index("img"), lax.axis_index("row"), lax.axis_index("col")
+    return img, (r + 2 * dx) % 4, hop(z, dz)
+
+
+def hop(z, dz):
+    return (z, flip(z), (z + 2) % 4, 3 - z)[dz]
+
+
+def greet(devices):
+    barrier = pltpu.get_barrier_semaphore()
+    for device in devices:
+        pl.semaphore_signal(
+            barrier, inc=1, device_id=device, device_id_type=pl.DeviceIdType.MESH
+        )
+    pl.semaphore_wait(barrier, len(devices))
+
+
+def send(src, dst, send_sem, recv_sem, device):
+    return pltpu.make_async_remote_copy(
+        src_ref=src,
+        dst_ref=dst,
+        send_sem=send_sem,
+        recv_sem=recv_sem,
+        device_id=device,
+        device_id_type=pl.DeviceIdType.MESH,
+    )
+
+
+def tile_moves(src, dst, send_sem, recv_sem, local_sem):
+    r, z = lax.axis_index("row"), lax.axis_index("col")
+    x = r // 2
+    shared, near, far, local = [], [], [], []
+    for dz in range(4):
+        first = 3 * hop(z, dz)
+        moves = (
+            (shared, 0, first + 2, 8 + dz),
+            (near, 0, first + x, dz),
+            (far, 1, first + 1 - x, 4 + dz),
+        )
+        for group, dx, slot, place_at in moves:
+            if dx == 0 and dz == 0:
+                sem = local_sem.at[0 if place_at else 1]
+                local.append(pltpu.make_async_copy(src.at[slot], dst.at[place_at], sem))
+            else:
+                sems = send_sem.at[place_at], recv_sem.at[place_at]
+                group.append(
+                    send(src.at[slot], dst.at[place_at], *sems, plane_device(dx, dz))
+                )
+    return local, shared, near, far
 
 
 def head_window(head, hd):
@@ -117,78 +120,292 @@
             dst[row : row + 128] = src[base + 128 * i : base + 128 * i + 128, col : col + pad]
 
 
-def attend_kernel(heads, hd, count, shared, flag_ref, mine_ref, sib_ref, *rest):
-    if shared:
-        far_ref, *rest = rest
-    o_mine, o_sib, stat, q_s, k_s, v_s, o_s = rest
+def attend(heads, hd, count, base, bias, mine, sib, far, o_mine, o_sib, stat, q_s, k_s, v_s, o_s):
     pad = q_s.shape[1]
     scale = LOG2E / math.sqrt(hd)
-    base = mine_ref.shape[0] - 128 * count if shared else 0
-    pair = (mine_ref, sib_ref)
-    gather_rows(q_s, 0, pair, base, count)
-    gather_rows(k_s, pad, pair, base, count)
-    gather_rows(v_s, 2 * pad, pair, base, count)
-    if shared:
-        k_s[256 * count :] = far_ref[:, 0:pad]
-        v_s[256 * count :] = far_ref[:, pad : 2 * pad]
+    gather_rows(q_s, 0, (mine, sib), base, count)
+    gather_rows(k_s, pad, (mine, sib), base, count)
+    gather_rows(v_s, 2 * pad, (mine, sib), base, count)
+    if far is not None:
+        k_s[256 * count :] = far[:, 0:pad]
+        v_s[256 * count :] = far[:, pad : 2 * pad]
+    blocks = k_s.shape[0] // 256
+    lane = lax.broadcasted_iota(jnp.int32, (1, 128), 1)
+
+    def body(head, carry):
+        win, inside = head_window(head, hd)
+        for i in range(count):
+            rows = slice(256 * i, 256 * i + 256)
+            q = jnp.where(inside, q_s[rows, win], jnp.zeros((), bf16))
+            s = dot(q, k_s[:, win], NT)
+            cols = [s[:, 256 * j : 256 * j + 256] for j in range(blocks)]
+            best = [jnp.max(col, axis=1, keepdims=True) for col in cols]
+            own = best[i]
+            rest = best[:i] + best[i + 1 :]
+            top = jnp.maximum(own, functools.reduce(jnp.maximum, rest) + bias)
+            near = -scale * top
+            away = near + bias
+            cols = [
+                jnp.exp2(col * scale + (near if j == i else away)) for j, col in enumerate(cols)
+            ]
+            total = functools.reduce(
+                jnp.add, [jnp.sum(col, axis=1, keepdims=True) for col in cols]
+            )
+            p = jnp.concatenate([col.astype(bf16) for col in cols], axis=1)
+            o = dot(p, v_s[:, win], NN) / total
+            o_s[rows, win] = jnp.where(inside, o.astype(bf16), o_s[rows, win])
+            at = slice(2 * base + 256 * i, 2 * base + 256 * i + 256)
+            stat[at] = jnp.where(lane == head, top * scale + jnp.log2(total), stat[at])
+        return carry
+
+    lax.fori_loop(0, heads, body, 0)
+    for i in range(count):
+        at = slice(base + 128 * i, base + 128 * i + 128)
+        o_mine[at] = o_s[256 * i : 256 * i + 128]
+        o_sib[at] = o_s[256 * i + 128 : 256 * i + 256]
+
+
+def forward_kernel(
+    heads,
+    hd,
+    tok_ref,
+    cot_ref,
+    wq_ref,
+    wa_ref,
+    chosen_ref,
+    bh_ref,
+    ba_ref,
+    bias_ref,
+    x_out,
+    cot_out,
+    mine_out,
+    sib_out,
+    nt_out,
+    ntsib_out,
+    far_out,
+    om_out,
+    os_out,
+    ao_out,
+    stat_out,
+    mod_out,
+    wh_out,
+    x_s,
+    raw_s,
+    w_s,
+    wa_s,
+    mod_s,
+    nt_s,
+    ntsib_s,
+    other_s,
+    mine_s,
+    sib_s,
+    far_s,
+    q_s,
+    k_s,
+    v_s,
+    o_s,
+    om_s,
+    os_s,
+    ao_s,
+    stat_s,
+    tok_send,
+    tok_recv,
+    cot_send,
+    cot_recv,
+    local_sem,
+    raw_sem,
+    wa_sem,
+    side_send,
+    side_recv,
+    out_sem,
+):
+    tile, width = x_s.shape[1:]
+    tokens = 12 * tile
+    main = 8 * tile
+    half = width // 2
+    pad = w_s.shape[2] // 3
+    rows_step = raw_s.shape[1]
+    core = lax.axis_index("row") % 2
+    to_core, to_x, _ = partners()
+
+    raw = [
+        pltpu.make_async_copy(
+            wq_ref.at[pl.ds(i * rows_step, rows_step)], raw_s.at[i % 2], raw_sem.at[i % 2]
+        )
+        for i in range(width // rows_step)
+    ]
+    ada = [
+        pltpu.make_async_copy(
+            wa_ref.at[:, pl.ds(i * width, width)], wa_s.at[i % 2], wa_sem.at[i % 2]
+        )
+        for i in range(6)
+    ]
+    for copy in raw[:2] + ada[:2]:
+        copy.start()
+    greet([to_core] + [plane_device(dx, dz) for dx in range(2) for dz in range(4) if dx or dz])
+    local, shared, near, far = tile_moves(tok_ref, x_s, tok_send, tok_recv, local_sem)
+    for copy in local + shared + near + far:
+        copy.start()
+
+    w_s[...] = jnp.zeros_like(w_s)
+    for i, copy in enumerate(raw):
+        copy.wait()
+        rows = slice(i * rows_step, (i + 1) * rows_step)
+        for h in range(2):
+            for p in range(3):
+                start = half * (2 * p + h)
+                w_s[h, rows, p * pad : p * pad + half] = raw_s[i % 2, :, start : start + half]
+        if i + 2 < len(raw):
+            raw[i + 2].start()
+    for i, copy in enumerate(ada):
+        copy.wait()
+        mod_s[i] = dot(chosen_ref[...], wa_s[i % 2], NN) + ba_ref[i]
+        if i + 2 < len(ada):
+            ada[i + 2].start()
+    outs = []
+
+    def put(src, dst):
+        copy = pltpu.make_async_copy(src, dst, out_sem.at[len(outs)])
+        copy.start()
+        outs.append(copy)
+
+    put(w_s, wh_out)
+    put(mod_s, mod_out)
+
+    sides = []
+
+    def side(src, dst, device):
+        k = len(sides)
+        copy = send(src, dst, side_send.at[k], side_recv.at[k], device)
+        copy.start()
+        sides.append(copy)
+        return copy
+
+    moves = None
+    from_core = []
+    for first, waits in ((8, local[:1] + shared), (0, local[1:] + near), (4, far)):
+        for copy in waits:
+            copy.wait()
+        if first == 4:
+            moves = tile_moves(cot_ref, cot_out, cot_send, cot_recv, local_sem)
+            for group in moves:
+                for copy in group:
+                    copy.start()
+        parts = []
+        for i in range(2):
+            at = first // 2 + i
+            values = x_s[first + 2 * i : first + 2 * i + 2].reshape(2 * tile, width)
+            normed, _ = norm(values.astype(f32))
+            parts.append((normed * (1.0 + mod_s[1, at : at + 1]) + mod_s[0, at : at + 1]).astype(bf16))
+        normed = jnp.concatenate(parts, axis=0)
+        rows = slice(first * tile, (first + 4) * tile)
+        other_s[rows] = (dot(normed, w_s[1 - core], NN) + bh_ref[1 - core]).astype(bf16)
+        at = pl.ds(first * tile, 4 * tile)
+        from_core.append(side(other_s.at[at], sib_s.at[at], to_core))
+        mine_s[rows] = (dot(normed, w_s[core], NN) + bh_ref[core]).astype(bf16)
+        nt_s[:, rows] = normed.T
+        if first == 0:
+            from_core[0].wait_recv()
+            at, cols = pl.ds(main, tokens - main), pl.ds(pad, 2 * pad)
+            size = tokens - main
+            from_x = [
+                side(src.at[at, cols], far_s.at[pl.ds(size * k, size)], to_x)
+                for k, src in enumerate((mine_s, sib_s))
+            ]
+    put(x_s, x_out)
+    put(mine_s, mine_out)
+    put(nt_s, nt_out)
+    nt_copy = side(nt_s, ntsib_s, to_core)
+
     o_s[...] = jnp.zeros_like(o_s)
-    stat[...] = jnp.zeros_like(stat)
-    lane = lax.broadcasted_iota(jnp.int32, (1, 128), 1)
-
-    def run(single):
-        def body(head, carry):
-            win, inside = head_window(head, hd)
-            for i in range(count):
-                rows = slice(256 * i, 256 * i + 256)
-                keys = slice(None) if single else rows
-                q = jnp.where(inside, q_s[rows, win], jnp.zeros((), bf16))
-                s = dot(q, k_s[keys, win], NT)
-                top = jnp.max(s, axis=1, keepdims=True)
-                p = jnp.exp2((s - top) * scale)
-                total = jnp.sum(p, axis=1, keepdims=True)
-                o = dot(p.astype(bf16), v_s[keys, win], NN) / total
-                o_s[rows, win] = jnp.where(inside, o.astype(bf16), o_s[rows, win])
-                stat[rows] = jnp.where(lane == head, top * scale + jnp.log2(total), stat[rows])
-            return carry
-
-        lax.fori_loop(0, heads, body, 0)
-
-    one = flag_ref[0] == 1
-    pl.when(one)(lambda: run(True))
-    pl.when(jnp.logical_not(one))(lambda: run(False))
-    for i in range(count):
-        o_mine[128 * i : 128 * i + 128] = o_s[256 * i : 256 * i + 128]
-        o_sib[128 * i : 128 * i + 128] = o_s[256 * i + 128 : 256 * i + 256]
-
-
-def attend(flag, mine, sib, far, heads, hd, count):
-    pad = mine.shape[1] // 3
-    keys = 256 * count + (0 if far is None else far.shape[0])
-    tokens = 128 * count
-    inputs = [flag, mine, sib] + ([] if far is None else [far])
+    stat_s[...] = jnp.zeros_like(stat_s)
+    for copy in from_core[1:]:
+        copy.wait_recv()
+    put(sib_s, sib_out)
+    scratch = (om_s, os_s, stat_s, q_s, k_s, v_s, o_s)
+    attend(heads, hd, 4, 0, bias_ref[0], mine_s, sib_s, None, *scratch)
+    back = [side(os_s.at[pl.ds(0, main)], ao_s.at[pl.ds(0, main)], to_core)]
+    for copy in from_x:
+        copy.wait_recv()
+    put(far_s, far_out)
+    attend(heads, hd, 2, main, bias_ref[1], mine_s, sib_s, far_s, *scratch)
+    at = pl.ds(main, tokens - main)
+    back.append(side(os_s.at[at], ao_s.at[at], to_core))
+    put(om_s, om_out)
+    put(os_s, os_out)
+    put(stat_s, stat_out)
+    nt_copy.wait_recv()
+    put(ntsib_s, ntsib_out)
+    for copy in back:
+        copy.wait_recv()
+    put(ao_s, ao_out)
+    for copy in sides:
+        copy.wait_send()
+    for group in moves:
+        for copy in group:
+            copy.wait()
+    for copy in outs:
+        copy.wait()
+
+
+def forward(tok, cot, w_qkv, w_ada, chosen, b_half, b_ada, bias, heads, hd):
+    _, tile, width = tok.shape
+    tokens = 12 * tile
+    pad = b_half.shape[2] // 3
+    any_ref = pl.BlockSpec(memory_space=pl.ANY)
+    outs = (
+        shaped((12, tile, width)),
+        shaped((12, tile, width)),
+        shaped((tokens, 3 * pad)),
+        shaped((tokens, 3 * pad)),
+        shaped((width, tokens)),
+        shaped((width, tokens)),
+        shaped((8 * tile, 2 * pad)),
+        shaped((tokens, pad)),
+        shaped((tokens, pad)),
+        shaped((tokens, pad)),
+        shaped((2 * tokens, 128), f32),
+        shaped((6, 8, width), f32),
+        shaped((2, width, 3 * pad)),
+    )
+    scratch = [
+        outs[0],
+        shaped((2, width // 4, 3 * width)),
+        outs[12],
+        shaped((2, width, width)),
+        outs[11],
+        outs[4],
+        outs[4],
+        outs[2],
+        outs[2],
+        outs[2],
+        outs[6],
+        shaped((16 * tile, pad)),
+        shaped((16 * tile, pad)),
+        shaped((16 * tile, pad)),
+        shaped((16 * tile, pad)),
+        outs[7],
+        outs[7],
+        outs[7],
+        outs[10],
+    ]
     return pl.pallas_call(
-        functools.partial(attend_kernel, heads, hd, count, far is not None),
-        out_shape=(
-            shaped((tokens, pad)),
-            shaped((tokens, pad)),
-            shaped((2 * tokens, 128), f32),
+        functools.partial(forward_kernel, heads, hd),
+        in_specs=[any_ref] * 4 + [VMEM] * 3 + [SMEM],
+        out_specs=(any_ref,) * len(outs),
+        scratch_shapes=[pltpu.VMEM(s.shape, s.dtype) for s in scratch]
+        + [pltpu.SemaphoreType.DMA((k,)) for k in (12, 12, 12, 12, 2, 2, 2, 10, 10, 12)],
+        out_shape=outs,
+        compiler_params=pltpu.CompilerParams(
+            vmem_limit_bytes=62 * 2**20, collective_id=2, has_side_effects=True
         ),
-        in_specs=[SMEM] + [VMEM] * (len(inputs) - 1),
-        out_specs=(VMEM,) * 3,
-        scratch_shapes=[
-            pltpu.VMEM((2 * tokens, pad), bf16),
-            pltpu.VMEM((keys, pad), bf16),
-            pltpu.VMEM((keys, pad), bf16),
-            pltpu.VMEM((2 * tokens, pad), bf16),
-        ],
-        compiler_params=pltpu.CompilerParams(vmem_limit_bytes=VMEM_LIMIT),
         cost_estimate=pl.CostEstimate(
-            flops=1024 * heads * tokens * keys,
-            bytes_accessed=8 * 2**20,
-            transcendentals=heads * 2 * tokens * keys,
+            flops=4 * tokens * width * 3 * pad + 4096 * heads * tokens * 16 * tile,
+            bytes_accessed=70 * 2**20,
+            transcendentals=heads * 2 * tokens * 16 * tile,
         ),
-        name="attend_far" if far is not None else "attend_near",
-    )(*inputs)
+        name="forward",
+    )(tok, cot, w_qkv, w_ada, chosen, b_half, b_ada, bias)
 
 
 def attend_back_kernel(heads, hd, count, shared, flag_ref, mine_ref, sib_ref, *rest):
@@ -206,7 +423,7 @@
     gather_rows(q_s, 0, pair, base, count)
     gather_rows(k_s, pad, pair, base, count)
     gather_rows(v_s, 2 * pad, pair, base, count)
-    gather_rows(do_s, 0, (d_mine, d_sib), 0, count)
+    gather_rows(do_s, 0, (d_mine, d_sib), base, count)
     if shared:
         k_s[256 * count :] = far_ref[:, 0:pad]
         v_s[256 * count :] = far_ref[:, pad : 2 * pad]
@@ -219,9 +436,9 @@
     member = jnp.where(jnp.logical_and(col >= row * hd, col < row * hd + hd), 1.0, 0.0).astype(bf16)
     for i in range(count):
         rows = slice(256 * i, 256 * i + 256)
-        lse_s[i] = stat[rows].T[0:heads]
+        lse_s[i] = stat[2 * base + 256 * i : 2 * base + 256 * i + 256].T[0:heads]
         o = jnp.concatenate(
-            [o_mine[128 * i : 128 * i + 128], o_sib[128 * i : 128 * i + 128]], axis=0
+            [ref[base + 128 * i : base + 128 * i + 128] for ref in (o_mine, o_sib)], axis=0
         )
         both = do_s[rows].astype(f32) * o.astype(f32)
         high = both.astype(bf16)
@@ -312,35 +529,6 @@
         ),
         name="attend_far_back" if far is not None else "attend_near_back",
     )(*inputs)
-
-
-def flip(index):
-    return index + 1 - 2 * (index % 2)
-
-
-def partners():
-    img, r, z = lax.axis_index("img"), lax.axis_index("row"), lax.axis_index("col")
-    return (img, flip(r), z), (img, (r + 2) % 4, z), (flip(img), r, z)
-
-
-def greet(devices):
-    barrier = pltpu.get_barrier_semaphore()
-    for device in devices:
-        pl.semaphore_signal(
-            barrier, inc=1, device_id=device, device_id_type=pl.DeviceIdType.MESH
-        )
-    pl.semaphore_wait(barrier, len(devices))
-
-
-def send(src, dst, send_sem, recv_sem, device):
-    return pltpu.make_async_remote_copy(
-        src_ref=src,
-        dst_ref=dst,
-        send_sem=send_sem,
-        recv_sem=recv_sem,
-        device_id=device,
-        device_id_type=pl.DeviceIdType.MESH,
-    )
 
 
 def middle_kernel(
@@ -411,11 +599,11 @@
         ).astype(bf16)
         for i in range(blocks):
             rows = slice(i * blk, (i + 1) * blk)
-            mid = x_ref[rows].astype(f32) + mod_ref[i, 2:3] * br1_s[rows].astype(f32)
+            mid = x_ref[rows].astype(f32) + mod_ref[2, i : i + 1] * br1_s[rows].astype(f32)
             mid_s[rows] = mid
             normed, _ = norm(mid)
-            n_s[rows] = (normed * (1.0 + mod_ref[i, 4:5]) + mod_ref[i, 3:4]).astype(bf16)
-            db2_s[rows] = (mod_ref[i, 5:6] * cot_ref[rows].astype(f32)).astype(bf16)
+            n_s[rows] = (normed * (1.0 + mod_ref[4, i : i + 1]) + mod_ref[3, i : i + 1]).astype(bf16)
+            db2_s[rows] = (mod_ref[5, i : i + 1] * cot_ref[rows].astype(f32)).astype(bf16)
         for g in range(4):
             place_row = ((g + core) % 2) * (2 * part) + (g // 2) * part
             place_row = pl.ds(pl.multiple_of(place_row, 16), part)
@@ -509,16 +697,16 @@
             cot = cot_ref[rows].astype(f32)
             br2 = br2_s[rows] + bd_ref[...]
             mid = mid_s[rows]
-            n_s[rows] = (mid + mod_ref[i, 5:6] * br2).astype(bf16)
+            n_s[rows] = (mid + mod_ref[5, i : i + 1] * br2).astype(bf16)
             normed, rstd = norm(mid)
             gn = gn_s[rows]
-            u = gn * (1.0 + mod_ref[i, 4:5])
+            u = gn * (1.0 + mod_ref[4, i : i + 1])
             gmid = cot + rstd * (
                 u
                 - jnp.mean(u, axis=-1, keepdims=True)
                 - normed * jnp.mean(u * normed, axis=-1, keepdims=True)
             )
-            db1 = mod_ref[i, 2:3] * gmid
+            db1 = mod_ref[2, i : i + 1] * gmid
             db1_s[rows] = db1.astype(bf16)
             dbp += jnp.sum(db1, axis=0, keepdims=True)
             dbd += jnp.sum(db2_s[rows].astype(f32), axis=0, keepdims=True)
@@ -619,7 +807,7 @@
         rows = slice(i * blk, (i + 1) * blk)
         y, rstd = norm(x_ref[rows].astype(f32))
         gn = ga_ref[rows].astype(f32) + gb_ref[rows].astype(f32)
-        u = gn * (1.0 + mod_ref[i, 1:2])
+        u = gn * (1.0 + mod_ref[1, pl.ds(2 * pl.program_id(0) + i, 1)])
         back = rstd * (
             u - jnp.mean(u, axis=-1, keepdims=True) - y * jnp.mean(u * y, axis=-1, keepdims=True)
         )
@@ -636,7 +824,7 @@
     return pl.pallas_call(
         functools.partial(first_back_kernel, blk),
         grid=(steps,),
-        in_specs=[each] * 4 + [pl.BlockSpec((rows // blk, 6, width), lambda s: (s, 0, 0))],
+        in_specs=[each] * 4 + [VMEM],
         out_specs=[each, pl.BlockSpec((rows // blk, 2, width), lambda s: (s, 0, 0))],
         out_shape=(shaped((tokens, width)), shaped((tokens // blk, 2, width), f32)),
         compiler_params=pltpu.CompilerParams(vmem_limit_bytes=VMEM_LIMIT),
@@ -725,22 +913,7 @@
     hidden = w_up.shape[1]
     r, z = lax.axis_index("row"), lax.axis_index("col")
     x, core = r // 2, r % 2
-    core_arr = core.reshape(1).astype(jnp.int32)
     assert lax.axis_size("row") == 4 and lax.axis_size("col") == 4 and slots == 12
-
-    def spread(values):
-        grouped = values.reshape(4, 3, tile, width)
-        near, far, shared = [], [], []
-        for dz in range(4):
-            group = pick(grouped, z ^ dz)
-            own = jnp.stack([pick(group, x), group[2]])
-            other = pick(group, 1 - x)
-            if dz:
-                own = over_plane(own, 0, dz)
-            near.append(own[0])
-            shared.append(own[1])
-            far.append(over_plane(other, 1, dz))
-        return jnp.concatenate(near + far + shared, axis=0)
 
     def collect(values, dtype):
         tiles = values.reshape(12, tile, width)
@@ -759,9 +932,6 @@
         order = jnp.where(kind == 2, 8 + dz, ((kind ^ x) & 1) * 4 + dz)
         return place(order, stacked, dtype).reshape(tokens.shape)
 
-    inputs = spread(tokens)
-    upstream = spread(cotangent)
-
     four_way = images_in_slot == 4
     kinds = pick(four_way.reshape(4, 3), z)
     main_four, shared_four = pick(kinds, x), kinds[2]
@@ -772,33 +942,50 @@
     places = jnp.concatenate([jnp.full((4,), x, jnp.int32), jnp.full((2,), 2, jnp.int32)]) * 4 + picks
     flag_main = jnp.where(main_four, 0, 1).reshape(1).astype(jnp.int32)
     flag_shared = jnp.where(shared_four, 0, 1).reshape(1).astype(jnp.int32)
+    bias = jnp.where(jnp.stack([main_four, shared_four]), -1e30, 0.0).astype(f32)
     cond = conditioning.astype(f32)
     silu = jax.nn.silu(cond).astype(bf16)
     silu_groups = silu.reshape(4, 12, width)
     chosen = jnp.take(pick(silu_groups, z), places, axis=0)
-    mod = (jnp.dot(chosen, w_ada, preferred_element_type=f32) + b_ada).reshape(6, 6, width)
+    chosen = jnp.pad(chosen, ((0, 2), (0, 0)))
 
     def widen(v, axis):
         return jnp.pad(v, [(0, pad - half) if a == axis else (0, 0) for a in range(v.ndim)])
 
-    w_half = widen(w_qkv.reshape(width, 3, 2, half), 3).transpose(2, 0, 1, 3)
-    w_half = w_half.reshape(2, width, 3 * pad)
     b_three = jnp.stack([b_qv[:width], jnp.zeros_like(b_qv[:width]), b_qv[width:]])
     b_half = widen(b_three.reshape(3, 2, half).astype(f32), 2).transpose(1, 0, 2)
     b_half = b_half.reshape(2, 1, 3 * pad)
     w_proj_half = widen(w_proj.reshape(2, half, width), 1)
     wp_mine, wp_other = pick(w_proj_half, core), pick(w_proj_half, 1 - core)
 
-    qkv_other, qkv_mine, normed_t = qkv(core_arr, inputs, mod, w_half, b_half, blk)
-    qkv_sib = over_core(qkv_other)
-    normed_sib = over_core(normed_t)
-    far_kv = over_x(jnp.concatenate([qkv_mine[main:, pad:], qkv_sib[main:, pad:]], axis=0))
-    om_near, os_near, stat_near = attend(flag_main, qkv_mine, qkv_sib, None, heads, hd, 4)
-    back_near = over_core(os_near)
-    om_far, os_far, stat_far = attend(flag_shared, qkv_mine, qkv_sib, far_kv, heads, hd, 2)
-    back_far = over_core(os_far)
-    att_mine = jnp.concatenate([om_near, om_far], axis=0)
-    att_other = jnp.concatenate([back_near, back_far], axis=0)
+    (
+        inputs,
+        upstream,
+        qkv_mine,
+        qkv_sib,
+        normed_t,
+        normed_sib,
+        far_kv,
+        om,
+        os,
+        att_other,
+        stat,
+        mod,
+        w_half,
+    ) = forward(
+        tokens.reshape(slots, tile, width),
+        cotangent.reshape(slots, tile, width),
+        w_qkv,
+        w_ada,
+        chosen,
+        b_half,
+        b_ada.astype(f32).reshape(6, 1, width),
+        bias,
+        heads,
+        hd,
+    )
+    inputs = inputs.reshape(count, width)
+    upstream = upstream.reshape(count, width)
 
     (
         out,
@@ -815,7 +1002,7 @@
     ) = middle(
         inputs,
         upstream,
-        att_mine,
+        om,
         att_other,
         mod,
         wp_mine,
@@ -864,11 +1051,11 @@
         flag_shared,
         qkv_mine,
         qkv_sib,
-        do_mine[main:],
-        do_sib[main:],
-        om_far,
-        os_far,
-        stat_far,
+        do_mine,
+        do_sib,
+        om,
+        os,
+        stat,
         far_kv,
         heads,
         hd,
@@ -876,7 +1063,7 @@
     )
     far_back = over_x(g_far)
     gm_near, gs_near = attend_back(
-        flag_main, qkv_mine, qkv_sib, do_mine, do_sib, om_near, os_near, stat_near, None, heads, hd, 4
+        flag_main, qkv_mine, qkv_sib, do_mine, do_sib, om, os, stat, None, heads, hd, 4
     )
     gm_far = jnp.concatenate([gm_far[:, :pad], plus(gm_far[:, pad:], far_back[: count - main])], 1)
     gs_far = jnp.concatenate([gs_far[:, :pad], plus(gs_far[:, pad:], far_back[count - main :])], 1)

time: 792 us -> 683 us (0.86)
  waiting for transfers between devices: 159 us -> 71.3 us
  local copies, waits for them, and re-layouts: 134 us -> 79.5 us
  Pallas kernels: 244 us -> 279 us
  blocking collectives: 41.2 us -> 67.9 us
  starting transfers between devices: 96.5 us -> 80.7 us
  matrix products: 53.4 us -> 44.6 us
    ppermute x28 -> x14, waiting for transfers between devices: 64.4 us -> 0.38 us  [over_plane(): return lax.ppermute(v, ('row', 'col'), swap)]
    pallas_call x3 -> x1, Pallas kernels: 48.5 us -> 90 us  [forward(): pl.pallas_call(functools.partial(forward_kernel, heads, hd), in_specs=[an...]
    psum x1, blocking collectives: 41.2 us -> 67.9 us  [shards(): small = lax.psum(small, ('row', 'col', 'img'))]
    ppermute x6 -> x5, waiting for transfers between devices: 36.4 us -> 11.4 us  [over_x(): return lax.ppermute(v, 'row', [(r, r ^ 2) for r in range(4)])]
    unnamed x172 -> x116, local copies, waits for them, and re-layouts: 62.4 us -> 38.2 us
    ppermute x28 -> x14, starting transfers between devices: 50.6 us -> 27.2 us  [over_plane(): return lax.ppermute(v, ('row', 'col'), swap)]
    transpose x2 -> x0, local copies, waits for them, and re-layouts: 15.2 us -> none  [shards(): w_half = widen(w_qkv.reshape(width, 3, 2, half), 3).transpose(2, 0, 1, 3)]
    reshape x2 -> x1, local copies, waits for them, and re-layouts: 13.3 us -> 1.35 us  [shards(): b_ada.astype(f32).reshape(6, 1, width)]
  transfers between devices with their start and end apart: 63 -> 44, of which waited for: 17 -> 14; matrix products, arithmetic and copies ran while one was open for 28% -> 21% of each run, Pallas kernels for 29% -> 10%
where the time goes in v3:
time: 683 us; the launch traced here: 673 us
  Pallas kernels  279 us (41%)
  starting transfers between devices  80.7 us (12%)
  local copies, waits for them, and re-layouts  79.5 us (12%)
  waiting for transfers between devices  71.3 us (10%)
  blocking collectives  67.9 us (10%)
  other arithmetic  47.1 us (7%)
  matrix products  44.6 us (7%)
    pallas_call x1, Pallas kernels, middle(): pl.pallas_call(functools.partial(middle_kernel, blk, chunks), grid=(chunk...  121 us
    pallas_call x1, Pallas kernels, forward(): pl.pallas_call(functools.partial(forward_kernel, heads, hd), in_specs=[an...  90 us
    psum x1, blocking collectives, shards(): small = lax.psum(small, ('row', 'col', 'img'))  67.9 us
    ppermute x12, waiting for transfers between devices, over_col(): return lax.ppermute(v, 'col', [(i, i ^ far) for i in range(4)])  47.9 us
    dot_general x8, matrix products, dot(): return lax.dot_general(left, right, dims, preferred_element_type=f32)  44.6 us
    pallas_call x2, Pallas kernels, attend_back(): pl.pallas_call(functools.partial(attend_back_kernel, heads, hd, count, fa...  43.7 us
    unnamed x116, local copies, waits for them, and re-layouts  38.2 us
    ppermute x12, starting transfers between devices, over_col(): return lax.ppermute(v, 'col', [(i, i ^ far) for i in range(4)])  28.9 us
  transfers between devices with their start and end apart: 44, of which 14 were waited for; matrix products, arithmetic and copies ran while one was open for 21% of the time, Pallas kernels for 10%

profile of v3, /device:TPU:0, one launch (start us, length us, event | category | flops | bytes accessed | tf_op | source)
XLA Modules:
  0.0 672.7 jit_solution(11471048154232443180)
XLA Ops:
  19.5 90.0 %forward.1 = (bf16[12,64,1152]{2,1,0:T(8,128)(2,1)}, bf16[12,64,1152]{2,1,0:T(8,128)(2,1)}, bf16[768,1920]{1,0:T(8,128)(2,1)}, bf16[768,1920]{1,0:T(8,128)(2,1)}...) custom-call(bf16[12,64,1152]{2,1,0:T(8,128)(2,1)} %bitcast.197, ...), custom_call_target="tpu_custom_call" | custom-call | flops 32564576256 | bytes 73400320 | tf_op jit(solution)/shard_map/forward/pallas_call | solution.py:392
  109.6 121.5 %middle.1 = (bf16[768,1152]{1,0:T(8,128)(2,1)}, bf16[768,1152]{1,0:T(8,128)(2,1)}, bf16[768,640]{1,0:T(8,128)(2,1)}, bf16[768,640]{1,0:T(8,128)(2,1)}, bf16[4,72...) custom-call(bf16[768,1152]{1,0:T(8,128)(2,1)} %bitcast.186, ...), custom_call_target="tpu_custom_call" | custom-call | flops 55717134336 | bytes 62914560 | tf_op jit(solution)/shard_map/middle/pallas_call | solution.py:744
  234.3 5.8 collective-permute-start
  279.3 9.2 %collective-permute-start.24 = (bf16[12,4608]{1,0:T(8,128)(2,1)S(1)}, bf16[12,4608]{1,0:T(8,128)(2,1)S(1)}, u32[]{:S(2)}, u32[]{:S(2)}) collective-permute-start(bf16[12,4608]{1,0:T(8,128)(2,1)S(1)} %add_convert_fusion.2), channel_id=1, source_target_pairs={{0,1},{1,0},{2,3},{3,2},{4,5},{5,4},{6,7},{7,6},{8,9},{9,8},{10,11... | collective-permute-start | bytes 331784 | tf_op jit(solution)/shard_map/ppermute | solution.py:874
  295.4 8.1 %place.2 = bf16[12,64,1152]{2,1,0:T(8,128)(2,1)} custom-call(s32[12]{0:T(128)} %compare_select_fusion.1.order_ref, bf16[12,64,1152]{2,1,0:T(8,128)(2,1)} %slice_dynamic-update-slice_fusion.6.in_ref), custom_call_target="tpu_custom_call" | custom-call | bytes 5308416 | tf_op jit(solution)/shard_map/place/pallas_call | solution.py:845
  308.1 6.5 fusion
  314.7 13.4 %attend_far_back.1 = (bf16[256,1920]{1,0:T(8,128)(2,1)}, bf16[256,1920]{1,0:T(8,128)(2,1)}, bf16[512,1280]{1,0:T(8,128)(2,1)}) custom-call(s32[1]{0:T(128)} %bitcast.32.flag_ref, bf16[768,1920]{1,0:T(8,128)(2,1)} %get-tuple-element.50.mine_ref, bf16[768,1920]{1,0:T(8,128)(2,1)} %get-tuple-element.51.sib_ref, bf16[768,640]{1,0:T(8,128)(2,1)} %get-tuple-element.52.rest_0_, ...), custom_call_target="tpu_custom_call" | custom-call | flops 5368709120 | bytes 12582912 | tf_op jit(solution)/shard_map/attend_far_back/pallas_call | solution.py:505
  330.0 30.3 %attend_near_back.1 = (bf16[512,1920]{1,0:T(8,128)(2,1)}, bf16[512,1920]{1,0:T(8,128)(2,1)}) custom-call(s32[1]{0:T(128)} %bitcast.31.flag_ref, bf16[768,1920]{1,0:T(8,128)(2,1)} %get-tuple-element.50.mine_ref, bf16[768,1920]{1,0:T(8,128)(2,1)} %get-tuple-element.51.sib_ref, bf16[768,640]{1,0:T(8,128)(2,1)} %get-tuple-element.52.rest_0_, ...), custom_call_target="tpu_custom_call" | custom-call | flops 10737418240 | bytes 12582912 | tf_op jit(solution)/shard_map/attend_near_back/pallas_call | solution.py:505
  372.1 5.1 collective-permute-done.33
  378.2 8.1 %collective-permute-start.34 = (bf16[2,72,1152]{2,1,0:T(8,128)(2,1)}, bf16[2,72,1152]{2,1,0:T(8,128)(2,1)}, u32[]{:S(2)}, u32[]{:S(2)}) collective-permute-start(bf16[2,72,1152]{2,1,0:T(8,128)(2,1)} %dynamic-slice_bitcast_fusion.6), channel_id=1, source_target_pairs={{0,1},{1,0},{2,3},{3,2},{4,5},{5,4},{6,7},{7,6},{8,9},{9,8},{10,11... | collective-permute-start | bytes 995336 | tf_op jit(solution)/shard_map/ppermute | solution.py:874
  386.4 10.9 %collective-permute-done.38 = bf16[72,4608]{1,0:T(8,128)(2,1)S(1)} collective-permute-done((bf16[72,4608]{1,0:T(8,128)(2,1)S(1)}, bf16[72,4608]{1,0:T(8,128)(2,1)S(1)}, u32[]{:S(2)}, u32[]{:S(2)}) %collective-permute-start.38) | collective-permute-done | bytes 663584 | tf_op jit(solution)/shard_map/ppermute | solution.py:874
  399.7 10.9 %fusion.12.ga_ref = bf16[768,1152]{1,0:T(8,128)(2,1)} fusion(bf16[2,1152,1920]{2,1,0:T(8,128)(2,1)} %get-tuple-element.60, s32[]{:T(128)S(6)} %select_n.232, bf16[256,1280]{1,0:T(8,128)(2,1)S(1)} %get-tuple-element.145, bf16[256,640]{1,0:T(8,128)(2,1)S(1)} %slice.261, bf16[512,1920]{1,0:T(8,128)(2,1)S(1)} %copy-done.2), kind=kOutput, calls=%fused_computation.19 | convolution fusion | flops 3407118336 | bytes 9142276 | tf_op jit(solution)/shard_map/dot_general | solution.py:29
  410.6 8.5 %fusion.15 = bf16[768,1152]{1,0:T(8,128)(2,1)} fusion(bf16[2,1152,1920]{2,1,0:T(8,128)(2,1)S(1)} %bitcast.201, s32[]{:T(128)S(6)} %select_n.232, bf16[256,1280]{1,0:T(8,128)(2,1)S(1)} %get-tuple-element.144, bf16[256,640]{1,0:T(8,128)(2,1)S(1)} %slice.264, bf16[512,1920]{1,0:T(8,128)(2,1)S(1)} %copy-done.3), kind=kOutput, calls=%fused_computation.20 | convolution fusion | flops 3407118336 | bytes 9142276 | tf_op jit(solution)/shard_map/dot_general | solution.py:29
  419.1 5.8 convert_reduce_fusion
  428.9 7.8 %fusion.2 = bf16[1152,1920]{1,0:T(8,128)(2,1)S(1)} fusion(f32[1152,1920]{1,0:T(8,128)S(1)} %fusion.53, bf16[1152,768]{1,0:T(8,128)(2,1)S(1)} %copy-done.38, bf16[256,1280]{1,0:T(8,128)(2,1)S(1)} %get-tuple-element.145, bf16[256,640]{1,0:T(8,128)(2,1)S(1)} %slice.261, bf16[512,1920]{1,0:T(8,128)(2,1)S(1)} %copy-done.2), kind=kOutput, calls=%fused_computation.4 | convolution fusion | flops 3410657280 | bytes 17989632 | tf_op jit(solution)/shard_map/dot_general | solution.py:29
  456.6 4.8 all-to-all-start
  464.6 67.9 %psum.7 = f32[9216]{0:T(1024)S(1)} all-reduce(f32[9216]{0:T(1024)S(1)} %constant_dynamic-update-slice_fusion.1), channel_id=1, replica_groups=mesh['img'=2,'row'=4,'col'=4] {'row','col','img'}, use_global_device_ids=true, to_apply=%region_4.5 | all-reduce | flops 9216 | bytes 73728 | tf_op jit(solution)/shard_map/psum | solution.py:1119
  540.7 6.8 %first_back.1 = (bf16[768,1152]{1,0:T(8,128)(2,1)}, f32[6,2,1152]{2,1,0:T(2,128)}) custom-call(bf16[768,1152]{1,0:T(8,128)(2,1)} %bitcast.187, bf16[768,1152]{1,0:T(8,128)(2,1)} %fusion.12.ga_ref, bf16[768,1152]{1,0:T(8,128)(2,1)} %collective-permute-done.9.gb_ref, bf16[768,1152]{1,0:T(8,128)(2,1)} %get-tuple-element.63.gmid_ref, ...), custom_call_target="tpu_custom_call" | custom-call | flops 17694720 | bytes 8847360 | tf_op jit(solution)/shard_map/first_back/pallas_call | solution.py:824
  581.0 6.3 collective-permute-start.42
  592.1 5.3 collective-permute-start.15
  609.7 20.4 %collective-permute-done.28 = bf16[2,2,72,1920]{3,2,1,0:T(8,128)(2,1)S(1)} collective-permute-done((bf16[2,2,72,1920]{3,2,1,0:T(8,128)(2,1)S(1)}, bf16[2,2,72,1920]{3,2,1,0:T(8,128)(2,1)S(1)}, u32[]{:S(2)}, u32[]{:S(2)}) %collective-permute-start.28) | collective-permute-done | bytes 1105952 | tf_op jit(solution)/shard_map/ppermute | solution.py:874
  634.7 8.4 %place.3 = f32[12,64,1152]{2,1,0:T(8,128)} custom-call(s32[12]{0:T(128)} %compare_select_fusion.1.order_ref, bf16[12,64,1152]{2,1,0:T(8,128)(2,1)} %slice_dynamic-update-slice_fusion.in_ref), custom_call_target="tpu_custom_call" | custom-call | bytes 5308416 | tf_op jit(solution)/shard_map/place/pallas_call | solution.py:845
  643.2 11.0 %collective-permute-done.29 = bf16[2,72,1920]{2,1,0:T(8,128)(2,1)S(1)} collective-permute-done((bf16[2,72,1920]{2,1,0:T(8,128)(2,1)S(1)}, bf16[2,72,1920]{2,1,0:T(8,128)(2,1)S(1)}, u32[]{:S(2)}, u32[]{:S(2)}) %collective-permute-start.29) | collective-permute-done | bytes 552992 | tf_op jit(solution)/shard_map/ppermute | solution.py:874
  656.3 10.7 %collective-permute-done.30 = bf16[2,72,1920]{2,1,0:T(8,128)(2,1)S(1)} collective-permute-done((bf16[2,72,1920]{2,1,0:T(8,128)(2,1)S(1)}, bf16[2,72,1920]{2,1,0:T(8,128)(2,1)S(1)}, u32[]{:S(2)}, u32[]{:S(2)}) %collective-permute-start.30) | collective-permute-done | bytes 552992 | tf_op jit(solution)/shard_map/ppermute | solution.py:884
  (311 shorter events, 186.2 us)
Async XLA Ops:
  234.3 29.8 %collective-permute-start = (bf16[2,64,1152]{2,1,0:T(8,128)(2,1)}, bf16[2,64,1152]{2,1,0:T(8,128)(2,1)}, u32[]{:S(2)}, u32[]{:S(2)}) collective-permute-start(bf16[2,64,1152]{2,1,0:T(8,128)(2,1)} %pad_maximum_fusion.4), channel_id=1, source_target_pairs={{0,1},{1,0},{2,3},{3,2},{4,5},{5,4},{6,7},{7,6},{8,9},{9,8},{10,11... | collective-permute-start | bytes 884744 | tf_op jit(solution)/shard_map/ppermute | solution.py:879
  240.8 27.3 %collective-permute-start.1 = (bf16[2,64,1152]{2,1,0:T(8,128)(2,1)}, bf16[2,64,1152]{2,1,0:T(8,128)(2,1)}, u32[]{:S(2)}, u32[]{:S(2)}) collective-permute-start(bf16[2,64,1152]{2,1,0:T(8,128)(2,1)} %pad_maximum_fusion.5), channel_id=1, source_target_pairs={{0,2},{1,3},{2,0},{3,1},{4,6},{5,7},{6,4},{7,5},{8,10},{9,11},{10,... | collective-permute-start | bytes 884744 | tf_op jit(solution)/shard_map/ppermute | solution.py:879
  242.8 29.1 %collective-permute-start.2 = (bf16[2,64,1152]{2,1,0:T(8,128)(2,1)}, bf16[2,64,1152]{2,1,0:T(8,128)(2,1)}, u32[]{:S(2)}, u32[]{:S(2)}) collective-permute-start(bf16[2,64,1152]{2,1,0:T(8,128)(2,1)} %pad_maximum_fusion.6), channel_id=1, source_target_pairs={{0,3},{1,2},{2,1},{3,0},{4,7},{5,6},{6,5},{7,4},{8,11},{9,10},{10,... | collective-permute-start | bytes 884744 | tf_op jit(solution)/shard_map/ppermute | solution.py:879
  244.2 29.2 %collective-permute-start.3 = (bf16[64,1152]{1,0:T(8,128)(2,1)}, bf16[64,1152]{1,0:T(8,128)(2,1)}, u32[]{:S(2)}, u32[]{:S(2)}) collective-permute-start(bf16[64,1152]{1,0:T(8,128)(2,1)} %get-tuple-element.135), channel_id=1, source_target_pairs={{0,8},{1,9},{2,10},{3,11},{4,12},{5,13},{6,14},{7,15},{8,0},{9,1},... | collective-permute-start | bytes 442376 | tf_op jit(solution)/shard_map/ppermute | solution.py:879
  271.9 42.8 %collective-permute-start.7 = (bf16[768,640]{1,0:T(8,128)(2,1)}, bf16[768,640]{1,0:T(8,128)(2,1)}, u32[]{:S(2)}, u32[]{:S(2)}) collective-permute-start(bf16[768,640]{1,0:T(8,128)(2,1)} %get-tuple-element.53), channel_id=1, source_target_pairs={{0,4},{4,0},{8,12},{12,8},{1,5},{5,1},{9,13},{13,9},{2,6},{6,2},{1... | collective-permute-start | bytes 2949128 | tf_op jit(solution)/shard_map/ppermute | solution.py:866
  273.4 91.2 %collective-permute-start.32 = (bf16[2,288,1152]{2,1,0:T(8,128)(2,1)}, bf16[2,288,1152]{2,1,0:T(8,128)(2,1)}, u32[]{:S(2)}, u32[]{:S(2)}) collective-permute-start(bf16[2,288,1152]{2,1,0:T(8,128)(2,1)} %dynamic-slice_bitcast_fusion.1), channel_id=1, source_target_pairs={{0,4},{4,0},{8,12},{12,8},{1,5},{5,1},{9,13},{13,9},{2,6},{6,2},{1... | collective-permute-start | bytes 3981320 | tf_op jit(solution)/shard_map/ppermute | solution.py:866
  275.5 28.0 %collective-permute-start.26 = (bf16[12,4608]{1,0:T(8,128)(2,1)S(1)}, bf16[12,4608]{1,0:T(8,128)(2,1)S(1)}, u32[]{:S(2)}, u32[]{:S(2)}) collective-permute-start(bf16[12,4608]{1,0:T(8,128)(2,1)S(1)} %add_convert_fusion.2), channel_id=1, source_target_pairs={{0,3},{1,2},{2,1},{3,0},{4,7},{5,6},{6,5},{7,4},{8,11},{9,10},{10,... | collective-permute-start | bytes 331784 | tf_op jit(solution)/shard_map/ppermute | solution.py:874
  278.6 25.0 %collective-permute-start.25 = (bf16[12,4608]{1,0:T(8,128)(2,1)S(1)}, bf16[12,4608]{1,0:T(8,128)(2,1)S(1)}, u32[]{:S(2)}, u32[]{:S(2)}) collective-permute-start(bf16[12,4608]{1,0:T(8,128)(2,1)S(1)} %add_convert_fusion.2), channel_id=1, source_target_pairs={{0,2},{1,3},{2,0},{3,1},{4,6},{5,7},{6,4},{7,5},{8,10},{9,11},{10,... | collective-permute-start | bytes 331784 | tf_op jit(solution)/shard_map/ppermute | solution.py:874
  279.3 24.3 %collective-permute-start.24 = (bf16[12,4608]{1,0:T(8,128)(2,1)S(1)}, bf16[12,4608]{1,0:T(8,128)(2,1)S(1)}, u32[]{:S(2)}, u32[]{:S(2)}) collective-permute-start(bf16[12,4608]{1,0:T(8,128)(2,1)S(1)} %add_convert_fusion.2), channel_id=1, source_target_pairs={{0,1},{1,0},{2,3},{3,2},{4,5},{5,4},{6,7},{7,6},{8,9},{9,8},{10,11... | collective-permute-start | bytes 331784 | tf_op jit(solution)/shard_map/ppermute | solution.py:874
  303.5 63.1 %collective-permute-start.37 = (bf16[2,72,4608]{2,1,0:T(8,128)(2,1)}, bf16[2,72,4608]{2,1,0:T(8,128)(2,1)}, u32[]{:S(2)}, u32[]{:S(2)}) collective-permute-start(bf16[2,72,4608]{2,1,0:T(8,128)(2,1)} %dynamic-slice_bitcast_fusion), channel_id=1, source_target_pairs={{0,1},{1,0},{2,3},{3,2},{4,5},{5,4},{6,7},{7,6},{8,9},{9,8},{10,11... | collective-permute-start | bytes 3981320 | tf_op jit(solution)/shard_map/ppermute | solution.py:874
  305.9 56.4 %collective-permute-start.41 = (bf16[72,4608]{1,0:T(8,128)(2,1)S(1)}, bf16[72,4608]{1,0:T(8,128)(2,1)}, u32[]{:S(2)}, u32[]{:S(2)}) collective-permute-start(bf16[72,4608]{1,0:T(8,128)(2,1)S(1)} %convolution_convert_fusion), channel_id=1, source_target_pairs={{0,16},{16,0},{1,17},{17,1},{2,18},{18,2},{3,19},{19,3},{4,20},{20... | collective-permute-start | bytes 1990664 | tf_op jit(solution)/shard_map/ppermute | solution.py:884
  328.1 69.7 %collective-permute-start.8 = (bf16[512,1280]{1,0:T(8,128)(2,1)}, bf16[512,1280]{1,0:T(8,128)(2,1)}, u32[]{:S(2)}, u32[]{:S(2)}) collective-permute-start(bf16[512,1280]{1,0:T(8,128)(2,1)} %get-tuple-element.59), channel_id=1, source_target_pairs={{0,8},{4,12},{8,0},{12,4},{1,9},{5,13},{9,1},{13,5},{2,10},{6,14},... | collective-permute-start | bytes 3932168 | tf_op jit(solution)/shard_map/ppermute | solution.py:870
  368.5 28.7 %collective-permute-start.38 = (bf16[72,4608]{1,0:T(8,128)(2,1)S(1)}, bf16[72,4608]{1,0:T(8,128)(2,1)S(1)}, u32[]{:S(2)}, u32[]{:S(2)}) collective-permute-start(bf16[72,4608]{1,0:T(8,128)(2,1)S(1)} %dynamic-slice_bitcast_fusion.3), channel_id=1, source_target_pairs={{0,2},{1,3},{2,0},{3,1},{4,6},{5,7},{6,4},{7,5},{8,10},{9,11},{10,... | collective-permute-start | bytes 1990664 | tf_op jit(solution)/shard_map/ppermute | solution.py:874
  378.2 69.9 %collective-permute-start.34 = (bf16[2,72,1152]{2,1,0:T(8,128)(2,1)}, bf16[2,72,1152]{2,1,0:T(8,128)(2,1)}, u32[]{:S(2)}, u32[]{:S(2)}) collective-permute-start(bf16[2,72,1152]{2,1,0:T(8,128)(2,1)} %dynamic-slice_bitcast_fusion.6), channel_id=1, source_target_pairs={{0,1},{1,0},{2,3},{3,2},{4,5},{5,4},{6,7},{7,6},{8,9},{9,8},{10,11... | collective-permute-start | bytes 995336 | tf_op jit(solution)/shard_map/ppermute | solution.py:874
  397.5 53.1 %collective-permute-start.39 = (bf16[72,4608]{1,0:T(8,128)(2,1)S(1)}, bf16[72,4608]{1,0:T(8,128)(2,1)}, u32[]{:S(2)}, u32[]{:S(2)}) collective-permute-start(bf16[72,4608]{1,0:T(8,128)(2,1)S(1)} %fusion.28), channel_id=1, source_target_pairs={{0,16},{16,0},{1,17},{17,1},{2,18},{18,2},{3,19},{19,3},{4,20},{20... | collective-permute-start | bytes 1990664 | tf_op jit(solution)/shard_map/ppermute | solution.py:1039
  424.9 115.7 %collective-permute-start.9 = (bf16[768,1152]{1,0:T(8,128)(2,1)}, bf16[768,1152]{1,0:T(8,128)(2,1)}, u32[]{:S(2)}, u32[]{:S(2)}) collective-permute-start(bf16[768,1152]{1,0:T(8,128)(2,1)} %fusion.15), channel_id=1, source_target_pairs={{0,4},{4,0},{8,12},{12,8},{1,5},{5,1},{9,13},{13,9},{2,6},{6,2},{1... | collective-permute-start | bytes 5308424 | tf_op jit(solution)/shard_map/ppermute | solution.py:866
  438.5 165.6 %collective-permute-start.27 = (bf16[4,2,72,1920]{3,2,1,0:T(8,128)(2,1)}, bf16[4,2,72,1920]{3,2,1,0:T(8,128)(2,1)}, u32[]{:S(2)}, u32[]{:S(2)}) collective-permute-start(bf16[4,2,72,1920]{3,2,1,0:T(8,128)(2,1)} %bitcast.170), channel_id=1, source_target_pairs={{0,8},{4,12},{8,0},{12,4},{1,9},{5,13},{9,1},{13,5},{2,10},{6,14},... | collective-permute-start | bytes 6635528 | tf_op jit(solution)/shard_map/ppermute | solution.py:870
  456.6 79.5 %all-to-all-start = ((bf16[16,72,288]{2,1,0:T(8,128)(2,1)}), bf16[16,72,288]{2,1,0:T(8,128)(2,1)S(1)}, u32[]{:S(2)}, u32[]{:S(2)}) async-start(bf16[16,72,288]{2,1,0:T(8,128)(2,1)} %bitcast.171), calls=%async_computation | async-start | bytes 1769472 | tf_op jit(solution)/shard_map/all_to_all | solution.py:1042
  463.3 71.1 %collective-permute-start.36 = (bf16[72,1152]{1,0:T(8,128)(2,1)}, bf16[72,1152]{1,0:T(8,128)(2,1)S(1)}, u32[]{:S(2)}, u32[]{:S(2)}) collective-permute-start(bf16[72,1152]{1,0:T(8,128)(2,1)} %fusion.34), channel_id=1, source_target_pairs={{0,16},{16,0},{1,17},{17,1},{2,18},{18,2},{3,19},{19,3},{4,20},{20... | collective-permute-start | bytes 497672 | tf_op jit(solution)/shard_map/ppermute | solution.py:884
  552.6 38.8 %collective-permute-start.10 = (bf16[2,64,1152]{2,1,0:T(8,128)(2,1)}, bf16[2,64,1152]{2,1,0:T(8,128)(2,1)S(1)}, u32[]{:S(2)}, u32[]{:S(2)}) collective-permute-start(bf16[2,64,1152]{2,1,0:T(8,128)(2,1)} %pad_maximum_fusion.7), channel_id=1, source_target_pairs={{0,1},{1,0},{2,3},{3,2},{4,5},{5,4},{6,7},{7,6},{8,9},{9,8},{10,11... | collective-permute-start | bytes 884744 | tf_op jit(solution)/shard_map/ppermute | solution.py:879
  565.0 27.0 %collective-permute-start.11 = (bf16[2,64,1152]{2,1,0:T(8,128)(2,1)}, bf16[2,64,1152]{2,1,0:T(8,128)(2,1)}, u32[]{:S(2)}, u32[]{:S(2)}) collective-permute-start(bf16[2,64,1152]{2,1,0:T(8,128)(2,1)} %pad_maximum_fusion.8), channel_id=1, source_target_pairs={{0,2},{1,3},{2,0},{3,1},{4,6},{5,7},{6,4},{7,5},{8,10},{9,11},{10,... | collective-permute-start | bytes 884744 | tf_op jit(solution)/shard_map/ppermute | solution.py:879
  571.7 27.3 %collective-permute-start.12 = (bf16[2,64,1152]{2,1,0:T(8,128)(2,1)}, bf16[2,64,1152]{2,1,0:T(8,128)(2,1)}, u32[]{:S(2)}, u32[]{:S(2)}) collective-permute-start(bf16[2,64,1152]{2,1,0:T(8,128)(2,1)} %pad_maximum_fusion.9), channel_id=1, source_target_pairs={{0,3},{1,2},{2,1},{3,0},{4,7},{5,6},{6,5},{7,4},{8,11},{9,10},{10,... | collective-permute-start | bytes 884744 | tf_op jit(solution)/shard_map/ppermute | solution.py:879
  600.6 55.7 %collective-permute-start.40 = (bf16[72,2304]{1,0:T(8,128)(2,1)S(1)}, bf16[72,2304]{1,0:T(8,128)(2,1)S(1)}, u32[]{:S(2)}, u32[]{:S(2)}) collective-permute-start(bf16[72,2304]{1,0:T(8,128)(2,1)S(1)} %convolution_convert_fusion.1), channel_id=1, source_target_pairs={{0,16},{16,0},{1,17},{17,1},{2,18},{18,2},{3,19},{19,3},{4,20},{20... | collective-permute-start | bytes 995336 | tf_op jit(solution)/shard_map/ppermute | solution.py:884
  606.4 23.7 %collective-permute-start.28 = (bf16[2,2,72,1920]{3,2,1,0:T(8,128)(2,1)S(1)}, bf16[2,2,72,1920]{3,2,1,0:T(8,128)(2,1)S(1)}, u32[]{:S(2)}, u32[]{:S(2)}) collective-permute-start(bf16[2,2,72,1920]{3,2,1,0:T(8,128)(2,1)S(1)} %dynamic-slice_bitcast_fusion.2), channel_id=1, source_target_pairs={{0,1},{1,0},{2,3},{3,2},{4,5},{5,4},{6,7},{7,6},{8,9},{9,8},{10,11... | collective-permute-start | bytes 3317768 | tf_op jit(solution)/shard_map/ppermute | solution.py:874
  (63 other events, 1176.6 us)
